TPU v7x, 256 devices: a whole 4x4x8 slice. The times are simulated.
256 devices in a mesh: ki: 8 (over x_hi, y), kj: 32 (over x_lo, z, core).
Axes of the slice: x: 4 (x_hi: 2, x_lo: 2; x = x_hi * 2 + x_lo), y: 4, z: 8, core: 2. Of those that a mesh axis runs over, the one named last changes fastest.
Arguments:
- amps: bfloat16 [8, 32, 8, 4, 400, 400], P('ki', 'kj'), may hold values from -24 to 24
- conserve: int32 [8, 32, 8], P('ki', 'kj'), may hold values from 0 to 7, as said below
Outputs:
- density: float32 [8, 400, 400], P('ki')
Inputs may be any that keep to these rules, and one draw needn't show every extreme that they name: For every pair slot (r, s) there is an offset m with conserve[r, s, a] = (m - a) mod 8, so the 8 entries name every block index once and conserve[r, s, conserve[r, s, a]] = a.
All inputs are finite; a program needn't handle non-finite values.
Results may differ from a plain program's by a relative error of at most 0.0003.
Values sent between devices are 32-bit elements; how exact they have to be, the bound alone decides.
No kernel may reach another device: no remote copies, remote signals or barrier semaphores. Data moves between devices by JAX's collectives and lax.ppermute only.
A program may use at most 128 MiB of HBM per device.

v0:
```python
import jax
import jax.numpy as jnp
from jax import lax
from jax.sharding import PartitionSpec as P


def on_device(amps, conserve):
    own = amps[0, 0]
    table = conserve[0, 0]
    blocks = own.shape[0]
    other = jnp.take(own, table, axis=0)
    exchange = jnp.swapaxes(other, -1, -2)
    conj_mix = (2.0 * own.astype(jnp.float32) - exchange.astype(jnp.float32)).astype(jnp.bfloat16)
    scale = 1.0 / (lax.axis_size("ki") * lax.axis_size("kj") * own.shape[1] * own.shape[2])
    owned = blocks // lax.axis_size("ki")
    whole = lax.psum(
        jnp.einsum("koxc,koyc->kxy", own, conj_mix, preferred_element_type=jnp.float32),
        ("ki", "kj"),
    )
    total = lax.dynamic_slice_in_dim(whole, lax.axis_index("ki") * owned, owned, 0)
    return total * scale


def solution(mesh):
    placed = (P("ki", "kj", None, None, None, None), P("ki", "kj", None))
    return jax.shard_map(
        on_device, mesh=mesh, in_specs=placed, out_specs=P("ki", None, None), check_vma=False
    )
```

profile of v0, /device:TPU:1, one launch (start us, length us, event | category | flops | bytes accessed | tf_op | source)
XLA Modules:
  0.0 345.9 jit_solution(12850720100067507294)
XLA Ops:
  6.5 0.0 all-reduce.2.cloned.1.call-start
  6.5 0.7 fusion.10
  7.2 0.7 compare_and_fusion
  7.9 21.1 %copy.3 = bf16[8,4,400,400]{2,3,1,0:T(8,128)(2,1)} copy(bf16[8,4,400,400]{3,2,1,0:T(8,128)(2,1)} %bitcast.21) | data formatting | bytes 20480000 | tf_op jit(solution)/shard_map/squeeze | solution.py:8
  28.9 11.4 %gather_fusion = bf16[8,4,400,400]{3,2,1,0:T(8,128)(2,1)} fusion(bf16[8,4,400,400]{3,2,1,0:T(8,128)(2,1)} %bitcast.22, s32[1024]{0:T(1024)S(1)} %pad_clamp_fusion), kind=kCustom, calls=%fused_computation | custom fusion | bytes 20480032 | tf_op jit(solution)/shard_map/jit(_take)/gather | solution.py:11
  40.3 19.0 %fusion.7 = f32[8,400,400]{1,2,0:T(8,128)} fusion(bf16[8,4,400,400]{2,3,1,0:T(8,128)(2,1)} %copy.3, bf16[8,4,400,400]{3,2,1,0:T(8,128)(2,1)} %gather_fusion, pred[8]{0:T(512)(128)(4,1)S(1)} %compare_and_fusion, bf16[1,1,8,4,400,400]{5,4,3,2,1,0:T(8,128)(2,1)} %param.2), kind=kOutput, calls=%fused_computation.8 | convolution fusion | flops 4126720000 | bytes 35840008 | tf_op jit(solution)/shard_map/koxc,koyc->kxy/dot_general | solution.py:17
  59.3 0.0 all-reduce.2.cloned.1.call-update
  59.3 277.3 %all-reduce.2.cloned.1.call-done = f32[8,400,400]{1,2,0:T(8,128)} async-done(((f32[8,400,400]{1,2,0:T(8,128)}), f32[8,400,400]{1,2,0:T(8,128)}) %all-reduce.2.cloned.1.call-update) | async-done | bytes 5120016 | tf_op jit(solution)/shard_map/psum | solution.py:16
  336.7 1.2 dynamic-slice_multiply_fusion
  337.9 1.2 copy.5
  (1 shorter events, 0.0 us)
Async XLA Ops:
  6.5 330.1 %all-reduce.2.cloned.1.call-start = ((), (), s32[]{:S(2)}) async-start(), calls=%async_computation | async-start | bytes 13107200 | tf_op jit(solution)/shard_map/psum | solution.py:16
Sparse Core Ops, SparseCore 0:
  59.4 277.1 all-reduce.1
where the time goes:
time: 347 us; the launch traced here: 346 us
  waiting for transfers between devices  277 us (80%)
  local copies, waits for them, and re-layouts  33.6 us (10%)
  matrix products  19 us (5%)
  between operations  13.4 us (4%)
    psum x1, waiting for transfers between devices, on_device(): lax.psum(jnp.einsum('koxc,koyc->kxy', own, conj_mix, preferred_element_ty...  277 us
    squeeze x1, local copies, waits for them, and re-layouts, on_device(): own = amps[0, 0]  21.1 us
    dot_general x1, matrix products, on_device(): jnp.einsum('koxc,koyc->kxy', own, conj_mix, preferred_element_type=jnp.fl...  19 us
    gather x1, local copies, waits for them, and re-layouts, on_device(): other = jnp.take(own, table, axis=0)  11.4 us
  transfers between devices with their start and end apart: 1, of which 1 were waited for; matrix products, arithmetic and copies ran while one was open for 0% of the time, Pallas kernels for 0%

commit v1 on v0

v1 whole, which is shorter than its diff:
```python
import functools
import jax
import jax.numpy as jnp
from jax import lax
from jax.experimental import pallas as pl
from jax.experimental.pallas import tpu as pltpu
from jax.sharding import Mesh, PartitionSpec as P

FINE = ("x_hi", "y", "x_lo", "z", "core")
SIZES = (2, 4, 2, 8, 2)
GROUPS, WIDE, TILES, UNIT = 50, 3, 160, 40


def position(x, y, z, core):
    x, y, z, core = x % 4, y % 4, z % 8, core % 2
    return (((x // 2 * 4 + y) * 2 + x % 2) * 8 + z) * 2 + core


def pairs(move):
    found = []
    for x in range(4):
        for y in range(4):
            for z in range(8):
                for core in range(2):
                    dx, dy, dz, dc = move(x, y, z, core)
                    found.append((position(x, y, z, core), position(x + dx, y + dy, z + dz, core + dc)))
    return found


def send(value, move):
    return lax.ppermute(value, FINE, pairs(move))


def density_kernel(table, amps, keep, give, blocks, acc, tiles, in_sems, out_sems):
    count, orbitals, size = amps.shape[0], amps.shape[1], amps.shape[2]
    x = lax.axis_index("x_hi") * 2 + lax.axis_index("x_lo")
    y = lax.axis_index("y")
    core = lax.axis_index("core")

    def fetch(b):
        return pltpu.make_async_copy(amps.at[b], blocks.at[b], in_sems.at[b])

    for i in range(count):
        partner = table[i]

        @pl.when(partner >= i)
        def _():
            fetch(i).start()

        @pl.when(partner > i)
        def _():
            fetch(partner).start()

    lane = lax.broadcasted_iota(jnp.int32, (8, 128), 1)

    def step(i, carry):
        partner = table[i]

        @pl.when(partner >= i)
        def _():
            fetch(i).wait()

        @pl.when(partner > i)
        def _():
            fetch(partner).wait()

        total = None
        for o in range(orbitals):
            own = blocks[i, o]
            mix = (2.0 * own.T.astype(jnp.float32) - blocks[partner, o].astype(jnp.float32)).astype(jnp.bfloat16)
            part = jnp.dot(own, mix, preferred_element_type=jnp.float32)
            total = part if total is None else total + part
        acc[:, :size] = total

        slot = lax.rem(i, 2)

        def leave(half, low, target, k, j):
            return pltpu.make_async_copy(
                tiles.at[slot, half * 2 + low], target.at[k, j], out_sems.at[slot, half * 2 + low]
            )

        @pl.when(i >= 2)
        def _():
            for half in range(2):
                for low in range(2):
                    leave(half, low, keep, 0, 0).wait()

        for t in range(GROUPS * WIDE):
            g, l = divmod(t, WIDE)
            tiles[slot, t // UNIT, t % UNIT] = acc[8 * g : 8 * g + 8, 128 * l : 128 * l + 128]
        for n in range(7):
            t = GROUPS * WIDE + n
            tile = jnp.zeros((8, 128), jnp.float32)
            for k in range(min(8, GROUPS - 8 * n)):
                g = 8 * n + k
                piece = acc[8 * g : 8 * g + 8, 128 * WIDE : 128 * WIDE + 128]
                if k:
                    piece = pltpu.roll(piece, 16 * k, 1)
                tile = jnp.where((lane >= 16 * k) & (lane < 16 * k + 16), piece, tile)
            tiles[slot, t // UNIT, t % UNIT] = tile
        for t in range(GROUPS * WIDE + 7, TILES):
            tiles[slot, t // UNIT, t % UNIT] = jnp.zeros((8, 128), jnp.float32)

        high, dy = i // 4, lax.rem(i % 4 - y + 4, 4)
        for half in range(2):
            for low in range(2):
                dx = lax.rem(high * 2 + low - x + 4, 4)
                k, j = (dy, dx) if half == 0 else (dx, dy)

                @pl.when(core == half)
                def _():
                    leave(half, low, keep, k, j).start()

                @pl.when(core != half)
                def _():
                    leave(half, low, give, k, j).start()

        return carry

    lax.fori_loop(0, count, step, 0)
    for slot in range(2):
        for u in range(4):
            pltpu.make_async_copy(tiles.at[slot, u], keep.at[0, 0], out_sems.at[slot, u]).wait()


def densities(table, amps):
    count, orbitals, size, _ = amps.shape
    out = jax.ShapeDtypeStruct((4, 4, UNIT, 8, 128), jnp.float32)
    return pl.pallas_call(
        density_kernel,
        out_shape=(out, out),
        in_specs=[pl.BlockSpec(memory_space=pltpu.SMEM), pl.BlockSpec(memory_space=pl.ANY)],
        out_specs=(pl.BlockSpec(memory_space=pl.ANY), pl.BlockSpec(memory_space=pl.ANY)),
        scratch_shapes=[
            pltpu.VMEM(amps.shape, jnp.bfloat16),
            pltpu.VMEM((size, 512), jnp.float32),
            pltpu.VMEM((2, 4, UNIT, 8, 128), jnp.float32),
            pltpu.SemaphoreType.DMA((count,)),
            pltpu.SemaphoreType.DMA((2, 4)),
        ],
        compiler_params=pltpu.CompilerParams(vmem_limit_bytes=40 << 20),
        cost_estimate=pl.CostEstimate(flops=8 << 30, bytes_accessed=20 << 20, transcendentals=0),
        name="densities",
    )(table, amps)


def layout_kernel(scale, mine, beside, other, other_beside, out, whole, sems):
    low, core = lax.axis_index("x_lo"), lax.axis_index("core")
    copies = [
        pltpu.make_async_copy(ref, whole.at[pl.ds(u * UNIT, UNIT)], sems.at[n])
        for n, (ref, u) in enumerate(
            (
                (mine, core * 2 + low),
                (beside, core * 2 + 1 - low),
                (other, (1 - core) * 2 + low),
                (other_beside, (1 - core) * 2 + 1 - low),
            )
        )
    ]
    for copy in copies:
        copy.start()
    for copy in copies:
        copy.wait()
    for t in range(GROUPS * WIDE):
        g, l = divmod(t, WIDE)
        out[0, 8 * g : 8 * g + 8, 128 * l : 128 * l + 128] = whole[t] * scale
    for g in range(GROUPS):
        n, k = divmod(g, 8)
        tile = whole[GROUPS * WIDE + n] * scale
        if k:
            tile = pltpu.roll(tile, 128 - 16 * k, 1)
        out[0, 8 * g : 8 * g + 8, 128 * WIDE : 128 * WIDE + 16] = tile[:, :16]


def lay_out(scale, size, *units):
    return pl.pallas_call(
        functools.partial(layout_kernel, scale),
        out_shape=jax.ShapeDtypeStruct((1, size, size), jnp.float32),
        in_specs=[pl.BlockSpec(memory_space=pl.ANY)] * 4,
        out_specs=pl.BlockSpec(memory_space=pltpu.VMEM),
        scratch_shapes=[pltpu.VMEM((TILES, 8, 128), jnp.float32), pltpu.SemaphoreType.DMA((4,))],
        compiler_params=pltpu.CompilerParams(vmem_limit_bytes=8 << 20),
        name="lay_out",
    )(*units)


def on_device(amps, conserve):
    scale = 1.0 / (8 * 32 * amps.shape[3] * amps.shape[4])
    keep, give = densities(conserve[0, 0], amps[0, 0])

    got = send(give, lambda x, y, z, core: (0, 0, 0, 1))
    first = [keep[k] + got[k] for k in range(4)]
    came = [
        send(first[k], lambda x, y, z, core, k=k: (0, k, 0, 0) if core == 0 else (k, 0, 0, 0)) for k in (1, 2, 3)
    ]
    second = [first[0][j] + came[0][j] + came[1][j] + came[2][j] for j in range(4)]
    came = [
        send(second[j], lambda x, y, z, core, j=j: (j, 0, 0, 0) if core == 0 else (0, j, 0, 0)) for j in (1, 2, 3)
    ]
    third = second[0] + came[0] + came[1] + came[2]
    parts = lax.all_to_all(third.reshape(8, UNIT // 8, 8, 128), "z", 0, 0, tiled=True)
    eighth = jnp.sum(parts, axis=0, keepdims=True)
    mine = lax.all_to_all(jnp.broadcast_to(eighth, parts.shape), "z", 0, 0, tiled=True).reshape(UNIT, 8, 128)
    beside = send(mine, lambda x, y, z, core: (1 - 2 * (x % 2), 0, 0, 0))
    other = send(mine, lambda x, y, z, core: (0, 0, 0, 1))
    other_beside = send(beside, lambda x, y, z, core: (0, 0, 0, 1))
    return lay_out(scale, amps.shape[4], mine, beside, other, other_beside)


def solution(mesh):
    fine = Mesh(mesh.devices.reshape(SIZES), FINE)
    ki, kj = ("x_hi", "y"), ("x_lo", "z", "core")
    return jax.shard_map(
        on_device,
        mesh=fine,
        in_specs=(P(ki, kj, None, None, None, None), P(ki, kj, None)),
        out_specs=P(ki, None, None),
        check_vma=False,
    )
```

time: 347 us -> 97.6 us (0.28)
  waiting for transfers between devices: 277 us -> 27 us
  local copies, waits for them, and re-layouts: 33.6 us -> 0.67 us
  blocking collectives: 0 us -> 27 us
  starting transfers between devices: 0.01 us -> 21.2 us
  Pallas kernels: 0 us -> 21 us
  matrix products: 19 us -> 0 us
  between operations: 13.4 us -> 0.04 us
    psum x1 -> x0, waiting for transfers between devices: 277 us -> none  [on_device(): lax.psum(jnp.einsum('koxc,koyc->kxy', own, conj_mix, preferred_element_ty...]
    all_to_all x0 -> x2, blocking collectives: none -> 27 us  [the longest x1 16.4 us: on_device(): lax.all_to_all(third.reshape(8, UNIT // 8, 8, 128), 'z', 0, 0, tiled=True)]
    ppermute x0 -> x10, waiting for transfers between devices: none -> 27 us  [send(): return lax.ppermute(value, FINE, pairs(move))]
    ppermute x0 -> x10, starting transfers between devices: none -> 21.2 us  [send(): return lax.ppermute(value, FINE, pairs(move))]
    squeeze x1 -> x0, local copies, waits for them, and re-layouts: 21.1 us -> none  [on_device(): own = amps[0, 0]]
    pallas_call x0 -> x2, Pallas kernels: none -> 21 us  [the longest x1 19.2 us: densities(): pl.pallas_call(density_kernel, out_shape=(out, out), in_specs=[pl.BlockSp...]
    dot_general x1 -> x0, matrix products: 19 us -> none  [on_device(): jnp.einsum('koxc,koyc->kxy', own, conj_mix, preferred_element_type=jnp.fl...]
    gather x1 -> x0, local copies, waits for them, and re-layouts: 11.4 us -> none  [on_device(): other = jnp.take(own, table, axis=0)]
  transfers between devices with their start and end apart: 1 -> 10, of which waited for: 1 -> 7; matrix products, arithmetic and copies ran while one was open for 0% -> 0% of each run, Pallas kernels for 0% -> 0%
where the time goes in v1:
time: 97.6 us; the launch traced here: 97.5 us
  waiting for transfers between devices  27 us (28%)
  blocking collectives  27 us (28%)
  starting transfers between devices  21.2 us (22%)
  Pallas kernels  21 us (22%)
    ppermute x10, waiting for transfers between devices, send(): return lax.ppermute(value, FINE, pairs(move))  27 us
    ppermute x10, starting transfers between devices, send(): return lax.ppermute(value, FINE, pairs(move))  21.2 us
    pallas_call x1, Pallas kernels, densities(): pl.pallas_call(density_kernel, out_shape=(out, out), in_specs=[pl.BlockSp...  19.2 us
    all_to_all x1, blocking collectives, on_device(): lax.all_to_all(third.reshape(8, UNIT // 8, 8, 128), 'z', 0, 0, tiled=True)  16.4 us
    all_to_all x1, blocking collectives, on_device(): lax.all_to_all(jnp.broadcast_to(eighth, parts.shape), 'z', 0, 0, tiled=True)  10.7 us
  transfers between devices with their start and end apart: 10, of which 7 were waited for; matrix products, arithmetic and copies ran while one was open for 0% of the time, Pallas kernels for 0%

profile of v1, /device:TPU:1, one launch (start us, length us, event | category | flops | bytes accessed | tf_op | source)
XLA Modules:
  0.0 97.5 jit_solution(4957753951482018316)
XLA Ops:
  0.0 0.0 copy-start
  0.0 0.7 copy-done
  0.7 19.2 %densities.1 = (f32[4,4,40,8,128]{4,3,2,1,0:T(8,128)S(1)}, f32[4,4,40,8,128]{4,3,2,1,0:T(8,128)S(1)}) custom-call(s32[8]{0:T(128)S(1)} %bitcast.43, bf16[8,4,400,400]{3,2,1,0:T(8,128)(2,1)} %bitcast.45), custom_call_target="tpu_custom_call" | custom-call | flops 8589934592 | bytes 20971520 | tf_op jit(solution)/shard_map/densities/pallas_call | solution.py:129
  19.8 3.4 %collective-permute-start = (f32[4,4,40,8,128]{4,3,2,1,0:T(8,128)S(1)}, f32[4,4,40,8,128]{4,3,2,1,0:T(8,128)S(1)}, u32[]{:S(2)}, u32[]{:S(2)}) collective-permute-start(f32[4,4,40,8,128]{4,3,2,1,0:T(8,128)S(1)} %get-tuple-element.8), channel_id=1, source_target_pairs={{0,1},{1,0},{2,3},{3,2},{4,5},{5,4},{6,7},{7,6},{8,9},{9,8},{10,11... | collective-permute-start | bytes 7864328 | tf_op jit(solution)/shard_map/ppermute | solution.py:31
  23.2 4.5 %collective-permute-done = f32[4,4,40,8,128]{4,3,2,1,0:T(8,128)S(1)} collective-permute-done((f32[4,4,40,8,128]{4,3,2,1,0:T(8,128)S(1)}, f32[4,4,40,8,128]{4,3,2,1,0:T(8,128)S(1)}, u32[]{:S(2)}, u32[]{:S(2)}) %collective-permute-start) | collective-permute-done | bytes 2621472 | tf_op jit(solution)/shard_map/ppermute | solution.py:31
  27.7 0.3 slice_add_fusion.3
  28.0 1.3 %collective-permute-start.3 = (f32[4,40,8,128]{3,2,1,0:T(8,128)S(1)}, f32[4,40,8,128]{3,2,1,0:T(8,128)S(1)}, u32[]{:S(2)}, u32[]{:S(2)}) collective-permute-start(f32[4,40,8,128]{3,2,1,0:T(8,128)S(1)} %get-tuple-element.10), channel_id=1, source_target_pairs={{0,96},{1,145},{2,98},{3,147},{4,100},{5,149},{6,102},{7,151},{8,1... | collective-permute-start | bytes 1966088 | tf_op jit(solution)/shard_map/ppermute | solution.py:31
  29.4 0.5 collective-permute-start.2
  29.9 0.6 collective-permute-start.1
  30.5 7.4 %collective-permute-done.3 = f32[4,40,8,128]{3,2,1,0:T(8,128)S(1)} collective-permute-done((f32[4,40,8,128]{3,2,1,0:T(8,128)S(1)}, f32[4,40,8,128]{3,2,1,0:T(8,128)S(1)}, u32[]{:S(2)}, u32[]{:S(2)}) %collective-permute-start.3) | collective-permute-done | bytes 655392 | tf_op jit(solution)/shard_map/ppermute | solution.py:31
  37.9 2.8 %collective-permute-done.2 = f32[4,40,8,128]{3,2,1,0:T(8,128)S(1)} collective-permute-done((f32[4,40,8,128]{3,2,1,0:T(8,128)S(1)}, f32[4,40,8,128]{3,2,1,0:T(8,128)S(1)}, u32[]{:S(2)}, u32[]{:S(2)}) %collective-permute-start.2) | collective-permute-done | bytes 655392 | tf_op jit(solution)/shard_map/ppermute | solution.py:31
  40.6 7.0 %collective-permute-done.1 = f32[4,40,8,128]{3,2,1,0:T(8,128)S(1)} collective-permute-done((f32[4,40,8,128]{3,2,1,0:T(8,128)S(1)}, f32[4,40,8,128]{3,2,1,0:T(8,128)S(1)}, u32[]{:S(2)}, u32[]{:S(2)}) %collective-permute-start.1) | collective-permute-done | bytes 655392 | tf_op jit(solution)/shard_map/ppermute | solution.py:31
  47.6 0.1 fusion.5
  47.7 1.1 %collective-permute-start.4 = (f32[40,8,128]{2,1,0:T(8,128)S(1)}, f32[40,8,128]{2,1,0:T(8,128)S(1)}, u32[]{:S(2)}, u32[]{:S(2)}) collective-permute-start(f32[40,8,128]{2,1,0:T(8,128)S(1)} %get-tuple-element.13), channel_id=1, source_target_pairs={{0,16},{1,33},{2,18},{3,35},{4,20},{5,37},{6,22},{7,39},{8,24},{9,... | collective-permute-start | bytes 491528 | tf_op jit(solution)/shard_map/ppermute | solution.py:31
  48.8 1.7 %collective-permute-start.6 = (f32[40,8,128]{2,1,0:T(8,128)S(1)}, f32[40,8,128]{2,1,0:T(8,128)S(1)}, u32[]{:S(2)}, u32[]{:S(2)}) collective-permute-start(f32[40,8,128]{2,1,0:T(8,128)S(1)} %get-tuple-element.14), channel_id=1, source_target_pairs={{0,144},{1,97},{2,146},{3,99},{4,148},{5,101},{6,150},{7,103},{8,1... | collective-permute-start | bytes 491528 | tf_op jit(solution)/shard_map/ppermute | solution.py:31
  50.5 1.4 %collective-permute-start.5 = (f32[40,8,128]{2,1,0:T(8,128)S(1)}, f32[40,8,128]{2,1,0:T(8,128)S(1)}, u32[]{:S(2)}, u32[]{:S(2)}) collective-permute-start(f32[40,8,128]{2,1,0:T(8,128)S(1)} %get-tuple-element.15), channel_id=1, source_target_pairs={{0,128},{1,65},{2,130},{3,67},{4,132},{5,69},{6,134},{7,71},{8,136... | collective-permute-start | bytes 491528 | tf_op jit(solution)/shard_map/ppermute | solution.py:31
  51.9 1.3 %collective-permute-done.4 = f32[40,8,128]{2,1,0:T(8,128)S(1)} collective-permute-done((f32[40,8,128]{2,1,0:T(8,128)S(1)}, f32[40,8,128]{2,1,0:T(8,128)S(1)}, u32[]{:S(2)}, u32[]{:S(2)}) %collective-permute-start.4) | collective-permute-done | bytes 163872 | tf_op jit(solution)/shard_map/ppermute | solution.py:31
  53.2 0.0 collective-permute-done.6
  53.2 3.0 %collective-permute-done.5 = f32[40,8,128]{2,1,0:T(8,128)S(1)} collective-permute-done((f32[40,8,128]{2,1,0:T(8,128)S(1)}, f32[40,8,128]{2,1,0:T(8,128)S(1)}, u32[]{:S(2)}, u32[]{:S(2)}) %collective-permute-start.5) | collective-permute-done | bytes 163872 | tf_op jit(solution)/shard_map/ppermute | solution.py:31
  56.2 0.1 fusion.9
  56.2 16.4 %all_to_all.10 = f32[8,5,8,128]{3,2,1,0:T(8,128)S(1)} all-to-all(f32[8,5,8,128]{3,2,1,0:T(8,128)S(1)} %bitcast.44), channel_id=1, replica_groups=mesh['x_hi'=2,'y'=4,'x_lo'=2,'z'=8,'core'=2] {'z'}, dimensions={0} | all-to-all | bytes 327680 | tf_op jit(solution)/shard_map/all_to_all | solution.py:201
  72.6 10.7 %all_to_all.11 = f32[8,5,8,128]{3,2,1,0:T(8,128)S(1)} all-to-all(f32[8,5,8,128]{3,2,1,0:T(8,128)S(1)} %broadcast_in_dim.2), channel_id=1, replica_groups=mesh['x_hi'=2,'y'=4,'x_lo'=2,'z'=8,'core'=2] {'z'}, dimensions={0} | all-to-all | bytes 327680 | tf_op jit(solution)/shard_map/all_to_all | solution.py:203
  83.3 0.0 collective-permute-start.7
  83.3 6.6 %collective-permute-start.8 = (f32[40,8,128]{2,1,0:T(8,128)S(1)}, f32[40,8,128]{2,1,0:T(8,128)S(1)}, u32[]{:S(2)}, u32[]{:S(2)}) collective-permute-start(f32[40,8,128]{2,1,0:T(8,128)S(1)} %bitcast.41), channel_id=1, source_target_pairs={{0,1},{1,0},{2,3},{3,2},{4,5},{5,4},{6,7},{7,6},{8,9},{9,8},{10,11... | collective-permute-start | bytes 491528 | tf_op jit(solution)/shard_map/ppermute | solution.py:31
  89.9 0.0 collective-permute-done.7.beside
  89.9 4.7 %collective-permute-start.9 = (f32[40,8,128]{2,1,0:T(8,128)S(1)}, f32[40,8,128]{2,1,0:T(8,128)S(1)}, u32[]{:S(2)}, u32[]{:S(2)}) collective-permute-start(f32[40,8,128]{2,1,0:T(8,128)S(1)} %collective-permute-done.7.beside), channel_id=1, source_target_pairs={{0,1},{1,0},{2,3},{3,2},{4,5},{5,4},{6,7},{7,6},{8,9},{9,8},{10,11... | collective-permute-start | bytes 491528 | tf_op jit(solution)/shard_map/ppermute | solution.py:31
  94.6 0.0 collective-permute-done.8.other
  94.6 1.0 %collective-permute-done.9.other_beside = f32[40,8,128]{2,1,0:T(8,128)S(1)} collective-permute-done((f32[40,8,128]{2,1,0:T(8,128)S(1)}, f32[40,8,128]{2,1,0:T(8,128)S(1)}, u32[]{:S(2)}, u32[]{:S(2)}) %collective-permute-start.9) | collective-permute-done | bytes 163872 | tf_op jit(solution)/shard_map/ppermute | solution.py:31
  95.6 1.9 %lay_out.1 = f32[1,400,400]{2,1,0:T(8,128)} custom-call(f32[40,8,128]{2,1,0:T(8,128)S(1)} %bitcast.42, f32[40,8,128]{2,1,0:T(8,128)S(1)} %collective-permute-done.7.beside, f32[40,8,128]{2,1,0:T(8,128)S(1)} %collective-permute-done.8.other, f32[40,8,128]{2,1,0:T(8,128)S(1)} %collective-permute-done.9.other_beside), custom_call_target="tpu_custom_call" | custom-call | tf_op jit(solution)/shard_map/lay_out/pallas_call | solution.py:176
  (2 shorter events, 0.0 us)
Async XLA Ops:
  0.0 0.7 copy-start
  19.8 7.9 %collective-permute-start = (f32[4,4,40,8,128]{4,3,2,1,0:T(8,128)S(1)}, f32[4,4,40,8,128]{4,3,2,1,0:T(8,128)S(1)}, u32[]{:S(2)}, u32[]{:S(2)}) collective-permute-start(f32[4,4,40,8,128]{4,3,2,1,0:T(8,128)S(1)} %get-tuple-element.8), channel_id=1, source_target_pairs={{0,1},{1,0},{2,3},{3,2},{4,5},{5,4},{6,7},{7,6},{8,9},{9,8},{10,11... | collective-permute-start | bytes 7864328 | tf_op jit(solution)/shard_map/ppermute | solution.py:31
  28.0 9.8 %collective-permute-start.3 = (f32[4,40,8,128]{3,2,1,0:T(8,128)S(1)}, f32[4,40,8,128]{3,2,1,0:T(8,128)S(1)}, u32[]{:S(2)}, u32[]{:S(2)}) collective-permute-start(f32[4,40,8,128]{3,2,1,0:T(8,128)S(1)} %get-tuple-element.10), channel_id=1, source_target_pairs={{0,96},{1,145},{2,98},{3,147},{4,100},{5,149},{6,102},{7,151},{8,1... | collective-permute-start | bytes 1966088 | tf_op jit(solution)/shard_map/ppermute | solution.py:31
  29.4 11.3 %collective-permute-start.2 = (f32[4,40,8,128]{3,2,1,0:T(8,128)S(1)}, f32[4,40,8,128]{3,2,1,0:T(8,128)S(1)}, u32[]{:S(2)}, u32[]{:S(2)}) collective-permute-start(f32[4,40,8,128]{3,2,1,0:T(8,128)S(1)} %get-tuple-element.11), channel_id=1, source_target_pairs={{0,64},{1,129},{2,66},{3,131},{4,68},{5,133},{6,70},{7,135},{8,72}... | collective-permute-start | bytes 1966088 | tf_op jit(solution)/shard_map/ppermute | solution.py:31
  29.9 17.7 %collective-permute-start.1 = (f32[4,40,8,128]{3,2,1,0:T(8,128)S(1)}, f32[4,40,8,128]{3,2,1,0:T(8,128)S(1)}, u32[]{:S(2)}, u32[]{:S(2)}) collective-permute-start(f32[4,40,8,128]{3,2,1,0:T(8,128)S(1)} %get-tuple-element.12), channel_id=1, source_target_pairs={{0,32},{1,17},{2,34},{3,19},{4,36},{5,21},{6,38},{7,23},{8,40},{9,... | collective-permute-start | bytes 1966088 | tf_op jit(solution)/shard_map/ppermute | solution.py:31
  47.7 5.5 %collective-permute-start.4 = (f32[40,8,128]{2,1,0:T(8,128)S(1)}, f32[40,8,128]{2,1,0:T(8,128)S(1)}, u32[]{:S(2)}, u32[]{:S(2)}) collective-permute-start(f32[40,8,128]{2,1,0:T(8,128)S(1)} %get-tuple-element.13), channel_id=1, source_target_pairs={{0,16},{1,33},{2,18},{3,35},{4,20},{5,37},{6,22},{7,39},{8,24},{9,... | collective-permute-start | bytes 491528 | tf_op jit(solution)/shard_map/ppermute | solution.py:31
  48.8 4.4 %collective-permute-start.6 = (f32[40,8,128]{2,1,0:T(8,128)S(1)}, f32[40,8,128]{2,1,0:T(8,128)S(1)}, u32[]{:S(2)}, u32[]{:S(2)}) collective-permute-start(f32[40,8,128]{2,1,0:T(8,128)S(1)} %get-tuple-element.14), channel_id=1, source_target_pairs={{0,144},{1,97},{2,146},{3,99},{4,148},{5,101},{6,150},{7,103},{8,1... | collective-permute-start | bytes 491528 | tf_op jit(solution)/shard_map/ppermute | solution.py:31
  50.5 5.7 %collective-permute-start.5 = (f32[40,8,128]{2,1,0:T(8,128)S(1)}, f32[40,8,128]{2,1,0:T(8,128)S(1)}, u32[]{:S(2)}, u32[]{:S(2)}) collective-permute-start(f32[40,8,128]{2,1,0:T(8,128)S(1)} %get-tuple-element.15), channel_id=1, source_target_pairs={{0,128},{1,65},{2,130},{3,67},{4,132},{5,69},{6,134},{7,71},{8,136... | collective-permute-start | bytes 491528 | tf_op jit(solution)/shard_map/ppermute | solution.py:31
  83.3 6.6 %collective-permute-start.7 = (f32[40,8,128]{2,1,0:T(8,128)S(1)}, f32[40,8,128]{2,1,0:T(8,128)S(1)}, u32[]{:S(2)}, u32[]{:S(2)}) collective-permute-start(f32[40,8,128]{2,1,0:T(8,128)S(1)} %bitcast.40), channel_id=1, source_target_pairs={{0,16},{1,17},{2,18},{3,19},{4,20},{5,21},{6,22},{7,23},{8,24},{9,... | collective-permute-start | bytes 491528 | tf_op jit(solution)/shard_map/ppermute | solution.py:31
  83.3 11.3 %collective-permute-start.8 = (f32[40,8,128]{2,1,0:T(8,128)S(1)}, f32[40,8,128]{2,1,0:T(8,128)S(1)}, u32[]{:S(2)}, u32[]{:S(2)}) collective-permute-start(f32[40,8,128]{2,1,0:T(8,128)S(1)} %bitcast.41), channel_id=1, source_target_pairs={{0,1},{1,0},{2,3},{3,2},{4,5},{5,4},{6,7},{7,6},{8,9},{9,8},{10,11... | collective-permute-start | bytes 491528 | tf_op jit(solution)/shard_map/ppermute | solution.py:31
  89.9 5.7 %collective-permute-start.9 = (f32[40,8,128]{2,1,0:T(8,128)S(1)}, f32[40,8,128]{2,1,0:T(8,128)S(1)}, u32[]{:S(2)}, u32[]{:S(2)}) collective-permute-start(f32[40,8,128]{2,1,0:T(8,128)S(1)} %collective-permute-done.7.beside), channel_id=1, source_target_pairs={{0,1},{1,0},{2,3},{3,2},{4,5},{5,4},{6,7},{7,6},{8,9},{9,8},{10,11... | collective-permute-start | bytes 491528 | tf_op jit(solution)/shard_map/ppermute | solution.py:31

commit v2 on v0

v2 whole, which is shorter than its diff:
```python
import functools
import jax
import jax.numpy as jnp
from jax import lax
from jax.experimental import pallas as pl
from jax.experimental.pallas import tpu as pltpu
from jax.sharding import Mesh, PartitionSpec as P

FINE = ("x_hi", "y", "x_lo", "z", "core")
SIZES = (2, 4, 2, 8, 2)
GROUPS, WIDE, TILES, UNIT = 50, 3, 160, 40


def position(x, y, z, core):
    x, y, z, core = x % 4, y % 4, z % 8, core % 2
    return (((x // 2 * 4 + y) * 2 + x % 2) * 8 + z) * 2 + core


def pairs(move):
    found = []
    for x in range(4):
        for y in range(4):
            for z in range(8):
                for core in range(2):
                    dx, dy, dz, dc = move(x, y, z, core)
                    found.append((position(x, y, z, core), position(x + dx, y + dy, z + dz, core + dc)))
    return found


def send(value, move):
    return lax.ppermute(value, FINE, pairs(move))


def across(x, y, z, core):
    return 0, 0, 0, 1


def around(step, turn, x, y, z, core):
    return (0, (y ^ step) - y, 0, 0) if core == turn else ((x ^ step) - x, 0, 0, 0)


def block_of(place):
    run, y = place // 4, place % 4
    return (y // 2 ^ run) * 4 + y


def place_of(block):
    y = block % 4
    return (block // 4 ^ y // 2) * 4 + y


def density_kernel(run, table, amps, blocks, keep, give, acc, in_sems):
    count, orbitals, size = blocks.shape[0], blocks.shape[1], blocks.shape[2]
    x_low = lax.axis_index("x_lo")
    x = lax.axis_index("x_hi") * 2 + x_low
    y = lax.axis_index("y")
    core = lax.axis_index("core")

    def arrivals(place, o, act):
        block = block_of(place)
        partner = table[block]
        other_place = place_of(partner)

        @pl.when(other_place >= place)
        def _():
            act(pltpu.make_async_copy(amps.at[block], blocks.at[block], in_sems.at[block]))

        @pl.when(other_place > place)
        def _():
            act(pltpu.make_async_copy(amps.at[partner], blocks.at[partner], in_sems.at[partner]))

    if run == 0:
        for place in range(count):
            arrivals(place, slice(None), lambda copy: copy.start())

    lane = lax.broadcasted_iota(jnp.int32, (8, 128), 1)

    def tile_of(t):
        if t < GROUPS * WIDE:
            g, l = divmod(t, WIDE)
            return acc[8 * g : 8 * g + 8, 128 * l : 128 * l + 128]
        tile = jnp.zeros((8, 128), jnp.float32)
        first = 8 * (t - GROUPS * WIDE)
        for k in range(max(0, min(8, GROUPS - first))):
            g = first + k
            piece = acc[8 * g : 8 * g + 8, 128 * WIDE : 128 * WIDE + 128]
            if k:
                piece = pltpu.roll(piece, 16 * k, 1)
            tile = jnp.where((lane >= 16 * k) & (lane < 16 * k + 16), piece, tile)
        return tile

    def step(i, carry):
        place = run * 4 + i
        block = block_of(place)
        partner = table[block]
        total = None
        for o in range(orbitals):
            if run == 0 and o == 0:
                arrivals(place, slice(None), lambda copy: copy.wait())
            own = blocks[block, o]
            turned = own.T
            mix = turned + turned - blocks[partner, o]
            part = jnp.dot(own, mix, preferred_element_type=jnp.float32)
            total = part if total is None else total + part
        acc[:, :size] = total

        high, dy = block // 4, i ^ y
        for half in range(2):
            for target, here in ((keep, core == half), (give, core != half)):

                @pl.when(here)
                def _():
                    for low in range(2):
                        u, dx = half * 2 + low, (high * 2 + low) ^ x
                        k, j = (dy, low ^ x_low) if half == 0 else (dx, dy & 1)
                        for n in range(UNIT):
                            target[k, j, n] = tile_of(u * UNIT + n)

        return carry

    lax.fori_loop(0, 4, step, 0)
    if run == 0:
        for place in range(4, count):
            arrivals(place, slice(None), lambda copy: copy.wait())


def densities(run, table, amps, blocks=None):
    shape = amps.shape
    half = pltpu.VMEM((4, 2, UNIT, 8, 128), jnp.float32)
    in_vmem = pl.BlockSpec(memory_space=pltpu.VMEM)
    params = dict(
        compiler_params=pltpu.CompilerParams(vmem_limit_bytes=12 << 20),
        cost_estimate=pl.CostEstimate(flops=4 << 30, bytes_accessed=13 << 20, transcendentals=0),
        name="densities",
    )
    acc = pltpu.VMEM((shape[2], 512), jnp.float32)
    if run == 0:
        return pl.pallas_call(
            functools.partial(density_kernel, 0),
            out_shape=(pltpu.VMEM(shape, jnp.bfloat16), half, half),
            in_specs=[pl.BlockSpec(memory_space=pltpu.SMEM), pl.BlockSpec(memory_space=pltpu.HBM)],
            out_specs=(in_vmem,) * 3,
            scratch_shapes=[acc, pltpu.SemaphoreType.DMA(shape[:1])],
            **params,
        )(table, pltpu.with_memory_space_constraint(amps, pltpu.HBM))

    def later(table, blocks, keep, give, acc):
        density_kernel(run, table, None, blocks, keep, give, acc, None)

    return pl.pallas_call(
        later,
        out_shape=(half, half),
        in_specs=[pl.BlockSpec(memory_space=pltpu.SMEM), in_vmem],
        out_specs=(in_vmem,) * 2,
        scratch_shapes=[acc],
        **params,
    )(table, pltpu.with_memory_space_constraint(blocks, pltpu.VMEM))


def layout_kernel(scale, mine, beside, other, other_beside, out, whole):
    low, core = lax.axis_index("x_lo"), lax.axis_index("core")
    for ref, u in (
        (mine, core * 2 + low),
        (beside, core * 2 + 1 - low),
        (other, (1 - core) * 2 + low),
        (other_beside, (1 - core) * 2 + 1 - low),
    ):
        whole[pl.ds(u * UNIT, UNIT)] = ref[...] * scale
    for t in range(GROUPS * WIDE):
        g, l = divmod(t, WIDE)
        out[0, 8 * g : 8 * g + 8, 128 * l : 128 * l + 128] = whole[t]
    for g in range(GROUPS):
        n, k = divmod(g, 8)
        tile = whole[GROUPS * WIDE + n]
        if k:
            tile = pltpu.roll(tile, 128 - 16 * k, 1)
        out[0, 8 * g : 8 * g + 8, 128 * WIDE : 128 * WIDE + 16] = tile[:, :16]


def lay_out(scale, size, *units):
    return pl.pallas_call(
        functools.partial(layout_kernel, scale),
        out_shape=jax.ShapeDtypeStruct((1, size, size), jnp.float32),
        in_specs=[pl.BlockSpec(memory_space=pltpu.VMEM)] * 4,
        out_specs=pl.BlockSpec(memory_space=pltpu.VMEM),
        scratch_shapes=[pltpu.VMEM((TILES, 8, 128), jnp.float32)],
        compiler_params=pltpu.CompilerParams(vmem_limit_bytes=8 << 20),
        name="lay_out",
    )(*(pltpu.with_memory_space_constraint(unit, pltpu.VMEM) for unit in units))


def on_device(amps, conserve):
    scale = 1.0 / (8 * 32 * amps.shape[3] * amps.shape[4])
    table, own = conserve[0, 0], amps[0, 0]
    blocks, keep, give = densities(0, table, own)
    runs = [(keep, send(give, across)), None]
    keep, give = densities(1, table, own, blocks)
    runs[1] = (keep, send(give, across))

    sums = []
    for keep, got in runs:
        first = [keep[k] + got[k] for k in range(4)]
        came = [send(first[k], functools.partial(around, k, 0)) for k in (1, 2, 3)]
        sums.append(first[0] + came[0] + came[1] + came[2])
    swapped = (lax.axis_index("y") >> 1) != lax.axis_index("x_hi")
    second = [jnp.where(swapped, sums[1 - j // 2][j % 2], sums[j // 2][j % 2]) for j in range(4)]
    came = [send(second[j], functools.partial(around, j, 1)) for j in (1, 2, 3)]
    third = second[0] + came[0] + came[1] + came[2]
    parts = lax.all_to_all(third.reshape(8, UNIT // 8, 8, 128), "z", 0, 0, tiled=True)
    eighth = jnp.sum(parts, axis=0, keepdims=True)
    mine = lax.all_to_all(jnp.broadcast_to(eighth, parts.shape), "z", 0, 0, tiled=True).reshape(UNIT, 8, 128)
    beside = send(mine, lambda x, y, z, core: (1 - 2 * (x % 2), 0, 0, 0))
    other = send(mine, across)
    other_beside = send(beside, across)
    return lay_out(scale, amps.shape[4], mine, beside, other, other_beside)


def solution(mesh):
    fine = Mesh(mesh.devices.reshape(SIZES), FINE)
    ki, kj = ("x_hi", "y"), ("x_lo", "z", "core")
    return jax.shard_map(
        on_device,
        mesh=fine,
        in_specs=(P(ki, kj, None, None, None, None), P(ki, kj, None)),
        out_specs=P(ki, None, None),
        check_vma=False,
    )
```

time: 347 us -> 85.7 us (0.25)
  waiting for transfers between devices: 277 us -> 17.1 us
  local copies, waits for them, and re-layouts: 33.6 us -> 1.26 us
  blocking collectives: 0 us -> 25.5 us
  starting transfers between devices: 0.01 us -> 22.5 us
  matrix products: 19 us -> 0 us
  Pallas kernels: 0 us -> 14.4 us
  between operations: 13.4 us -> 0.08 us
    psum x1 -> x0, waiting for transfers between devices: 277 us -> none  [on_device(): lax.psum(jnp.einsum('koxc,koyc->kxy', own, conj_mix, preferred_element_ty...]
    all_to_all x0 -> x2, blocking collectives: none -> 25.5 us  [the longest x1 14.8 us: on_device(): lax.all_to_all(third.reshape(8, UNIT // 8, 8, 128), 'z', 0, 0, tiled=True)]
    ppermute x0 -> x14, starting transfers between devices: none -> 22.5 us  [send(): return lax.ppermute(value, FINE, pairs(move))]
    squeeze x1 -> x0, local copies, waits for them, and re-layouts: 21.1 us -> none  [on_device(): own = amps[0, 0]]
    dot_general x1 -> x0, matrix products: 19 us -> none  [on_device(): jnp.einsum('koxc,koyc->kxy', own, conj_mix, preferred_element_type=jnp.fl...]
    ppermute x0 -> x14, waiting for transfers between devices: none -> 17.1 us  [send(): return lax.ppermute(value, FINE, pairs(move))]
    pallas_call x0 -> x3, Pallas kernels: none -> 14.4 us  [the longest x1 7.75 us: densities(): pl.pallas_call(functools.partial(density_kernel, 0), out_shape=(pltpu.VME...]
    gather x1 -> x0, local copies, waits for them, and re-layouts: 11.4 us -> none  [on_device(): other = jnp.take(own, table, axis=0)]
  transfers between devices with their start and end apart: 1 -> 14, of which waited for: 1 -> 7; matrix products, arithmetic and copies ran while one was open for 0% -> 4% of each run, Pallas kernels for 0% -> 7%
where the time goes in v2:
time: 85.7 us; the launch traced here: 85.5 us
  blocking collectives  25.5 us (30%)
  starting transfers between devices  22.5 us (26%)
  waiting for transfers between devices  17.1 us (20%)
  Pallas kernels  14.4 us (17%)
  other arithmetic  4.68 us (5%)
  local copies, waits for them, and re-layouts  1.26 us (1%)
    ppermute x14, starting transfers between devices, send(): return lax.ppermute(value, FINE, pairs(move))  22.5 us
    ppermute x14, waiting for transfers between devices, send(): return lax.ppermute(value, FINE, pairs(move))  17.1 us
    all_to_all x1, blocking collectives, on_device(): lax.all_to_all(third.reshape(8, UNIT // 8, 8, 128), 'z', 0, 0, tiled=True)  14.8 us
    all_to_all x1, blocking collectives, on_device(): lax.all_to_all(jnp.broadcast_to(eighth, parts.shape), 'z', 0, 0, tiled=True)  10.7 us
    pallas_call x1, Pallas kernels, densities(): pl.pallas_call(functools.partial(density_kernel, 0), out_shape=(pltpu.VME...  7.75 us
    pallas_call x1, Pallas kernels, densities(): pl.pallas_call(later, out_shape=(half, half), in_specs=[pl.BlockSpec(memo...  5.65 us
    add x2, other arithmetic, on_device(): sums.append(first[0] + came[0] + came[1] + came[2])  2.59 us
    add x2, other arithmetic, on_device(): first = [keep[k] + got[k] for k in range(4)]  1.96 us
  transfers between devices with their start and end apart: 14, of which 7 were waited for; matrix products, arithmetic and copies ran while one was open for 4% of the time, Pallas kernels for 7%

profile of v2, /device:TPU:1, one launch (start us, length us, event | category | flops | bytes accessed | tf_op | source)
XLA Modules:
  0.0 85.5 jit_solution(560595040740237510)
XLA Ops:
  0.0 0.7 copy-done
  0.7 7.8 %densities.2 = (bf16[8,4,400,400]{3,2,1,0:T(8,128)(2,1)S(1)}, f32[4,2,40,8,128]{4,3,2,1,0:T(8,128)S(1)}, f32[4,2,40,8,128]{4,3,2,1,0:T(8,128)S(1)}) custom-call(s32[8]{0:T(128)S(1)} %bitcast.47, bf16[8,4,400,400]{3,2,1,0:T(8,128)(2,1)} %bitcast.50), custom_call_target="tpu_custom_call" | custom-call | flops 4294967296 | bytes 13631488 | tf_op jit(solution)/shard_map/densities/pallas_call | solution.py:138
  8.4 3.3 %collective-permute-start.4 = (f32[4,2,40,8,128]{4,3,2,1,0:T(8,128)S(1)}, f32[4,2,40,8,128]{4,3,2,1,0:T(8,128)S(1)}, u32[]{:S(2)}, u32[]{:S(2)}) collective-permute-start(f32[4,2,40,8,128]{4,3,2,1,0:T(8,128)S(1)} %get-tuple-element.14), channel_id=1, source_target_pairs={{0,1},{1,0},{2,3},{3,2},{4,5},{5,4},{6,7},{7,6},{8,9},{9,8},{10,11... | collective-permute-start | bytes 3932168 | tf_op jit(solution)/shard_map/ppermute | solution.py:31
  11.7 5.6 %densities.3 = (f32[4,2,40,8,128]{4,3,2,1,0:T(8,128)S(1)}, f32[4,2,40,8,128]{4,3,2,1,0:T(8,128)S(1)}) custom-call(s32[8]{0:T(128)S(1)} %bitcast.48, bf16[8,4,400,400]{3,2,1,0:T(8,128)(2,1)S(1)} %get-tuple-element.10.blocks), custom_call_target="tpu_custom_call" | custom-call | flops 4294967296 | bytes 13631488 | tf_op jit(solution)/shard_map/densities/pallas_call | solution.py:150
  17.3 0.1 collective-permute-start
  17.5 0.9 %fusion.2 = (f32[2,40,8,128]{3,2,1,0:T(8,128)S(1)}, f32[2,40,8,128]{3,2,1,0:T(8,128)S(1)}, f32[2,40,8,128]{3,2,1,0:T(8,128)}) fusion(f32[4,2,40,8,128]{4,3,2,1,0:T(8,128)S(1)} %collective-permute-done.4, f32[4,2,40,8,128]{4,3,2,1,0:T(8,128)S(1)} %get-tuple-element.13), kind=kLoop, calls=%fused_computation.5 | loop fusion | flops 245760 | bytes 2949120 | tf_op jit(solution)/shard_map/add | solution.py:202
  18.4 0.2 copy-done.2
  18.6 0.6 collective-permute-start.7
  19.2 0.7 collective-permute-start.6
  19.9 2.0 %collective-permute-start.5 = (f32[2,40,8,128]{3,2,1,0:T(8,128)S(1)}, f32[2,40,8,128]{3,2,1,0:T(8,128)}, u32[]{:S(2)}, u32[]{:S(2)}) collective-permute-start(f32[2,40,8,128]{3,2,1,0:T(8,128)S(1)} %get-tuple-element.18), channel_id=1, source_target_pairs={{0,32},{1,17},{2,34},{3,19},{4,36},{5,21},{6,38},{7,23},{8,40},{9,... | collective-permute-start | bytes 983048 | tf_op jit(solution)/shard_map/ppermute | solution.py:31
  21.9 1.0 %fusion.9 = (f32[2,40,8,128]{3,2,1,0:T(8,128)}, f32[2,40,8,128]{3,2,1,0:T(8,128)}, f32[2,40,8,128]{3,2,1,0:T(8,128)}) fusion(f32[4,2,40,8,128]{4,3,2,1,0:T(8,128)S(1)} %collective-permute-done, f32[4,2,40,8,128]{4,3,2,1,0:T(8,128)S(1)} %get-tuple-element.11), kind=kLoop, calls=%fused_computation.16 | loop fusion | flops 245760 | bytes 2949120 | tf_op jit(solution)/shard_map/add | solution.py:202
  22.9 0.3 copy-done.1
  23.3 0.6 collective-permute-start.3
  23.8 1.2 %collective-permute-start.2 = (f32[2,40,8,128]{3,2,1,0:T(8,128)}, f32[2,40,8,128]{3,2,1,0:T(8,128)}, u32[]{:S(2)}, u32[]{:S(2)}) collective-permute-start(f32[2,40,8,128]{3,2,1,0:T(8,128)} %get-tuple-element.17), channel_id=1, source_target_pairs={{0,64},{1,129},{2,66},{3,131},{4,68},{5,133},{6,70},{7,135},{8,72}... | collective-permute-start | bytes 983048 | tf_op jit(solution)/shard_map/ppermute | solution.py:31
  25.1 4.5 %collective-permute-done.7 = f32[2,40,8,128]{3,2,1,0:T(8,128)S(1)} collective-permute-done((f32[2,40,8,128]{3,2,1,0:T(8,128)S(1)}, f32[2,40,8,128]{3,2,1,0:T(8,128)S(1)}, u32[]{:S(2)}, u32[]{:S(2)}) %collective-permute-start.7) | collective-permute-done | bytes 327712 | tf_op jit(solution)/shard_map/ppermute | solution.py:31
  29.6 0.9 %collective-permute-done.5 = f32[2,40,8,128]{3,2,1,0:T(8,128)} collective-permute-done((f32[2,40,8,128]{3,2,1,0:T(8,128)S(1)}, f32[2,40,8,128]{3,2,1,0:T(8,128)}, u32[]{:S(2)}, u32[]{:S(2)}) %collective-permute-start.5) | collective-permute-done | bytes 327712 | tf_op jit(solution)/shard_map/ppermute | solution.py:31
  30.5 1.2 %fusion.6 = f32[2,40,8,128]{3,2,1,0:T(8,128)S(1)} fusion(f32[2,40,8,128]{3,2,1,0:T(8,128)S(1)} %collective-permute-done.7, f32[2,40,8,128]{3,2,1,0:T(8,128)} %collective-permute-done.6, f32[2,40,8,128]{3,2,1,0:T(8,128)} %collective-permute-done.5, f32[4,2,40,8,128]{4,3,2,1,0:T(8,128)} %copy-done.2, f32[4,2,40,8,128]{4,3,2,1,0:T(8,128)S(1)} %get-tuple-element.13), kind=kLoop, calls=%fused_computation.10 | loop fusion | flops 327680 | bytes 1966080 | tf_op jit(solution)/shard_map/add | solution.py:204
  31.8 4.9 %collective-permute-done.3 = f32[2,40,8,128]{3,2,1,0:T(8,128)} collective-permute-done((f32[2,40,8,128]{3,2,1,0:T(8,128)}, f32[2,40,8,128]{3,2,1,0:T(8,128)}, u32[]{:S(2)}, u32[]{:S(2)}) %collective-permute-start.3) | collective-permute-done | bytes 327712 | tf_op jit(solution)/shard_map/ppermute | solution.py:31
  36.7 0.9 %collective-permute-done.1 = f32[2,40,8,128]{3,2,1,0:T(8,128)} collective-permute-done((f32[2,40,8,128]{3,2,1,0:T(8,128)}, f32[2,40,8,128]{3,2,1,0:T(8,128)}, u32[]{:S(2)}, u32[]{:S(2)}) %collective-permute-start.1) | collective-permute-done | bytes 327712 | tf_op jit(solution)/shard_map/ppermute | solution.py:31
  37.6 1.3 %fusion.13 = f32[2,40,8,128]{3,2,1,0:T(8,128)S(1)} fusion(f32[2,40,8,128]{3,2,1,0:T(8,128)} %collective-permute-done.3, f32[2,40,8,128]{3,2,1,0:T(8,128)} %collective-permute-done.2, f32[2,40,8,128]{3,2,1,0:T(8,128)} %collective-permute-done.1, f32[4,2,40,8,128]{4,3,2,1,0:T(8,128)} %copy-done.1, f32[4,2,40,8,128]{4,3,2,1,0:T(8,128)S(1)} %get-tuple-element.11), kind=kLoop, calls=%fused_computation.21 | loop fusion | flops 327680 | bytes 1966080 | tf_op jit(solution)/shard_map/add | solution.py:204
  39.0 1.1 %collective-permute-start.10 = (f32[40,8,128]{2,1,0:T(8,128)S(1)}, f32[40,8,128]{2,1,0:T(8,128)S(1)}, u32[]{:S(2)}, u32[]{:S(2)}) collective-permute-start(f32[40,8,128]{2,1,0:T(8,128)S(1)} %get-tuple-element.23), channel_id=1, source_target_pairs={{0,144},{1,97},{2,146},{3,99},{4,148},{5,101},{6,150},{7,103},{8,1... | collective-permute-start | bytes 491528 | tf_op jit(solution)/shard_map/ppermute | solution.py:31
  40.1 0.3 collective-permute-start.9
  40.4 1.9 %collective-permute-start.8 = (f32[40,8,128]{2,1,0:T(8,128)S(1)}, f32[40,8,128]{2,1,0:T(8,128)S(1)}, u32[]{:S(2)}, u32[]{:S(2)}) collective-permute-start(f32[40,8,128]{2,1,0:T(8,128)S(1)} %get-tuple-element.21), channel_id=1, source_target_pairs={{0,16},{1,33},{2,18},{3,35},{4,20},{5,37},{6,22},{7,39},{8,24},{9,... | collective-permute-start | bytes 491528 | tf_op jit(solution)/shard_map/ppermute | solution.py:31
  42.3 4.2 %collective-permute-done.10 = f32[40,8,128]{2,1,0:T(8,128)S(1)} collective-permute-done((f32[40,8,128]{2,1,0:T(8,128)S(1)}, f32[40,8,128]{2,1,0:T(8,128)S(1)}, u32[]{:S(2)}, u32[]{:S(2)}) %collective-permute-start.10) | collective-permute-done | bytes 163872 | tf_op jit(solution)/shard_map/ppermute | solution.py:31
  46.5 0.6 collective-permute-done.8
  47.1 14.8 %all_to_all.10 = f32[8,5,8,128]{3,2,1,0:T(8,128)S(1)} all-to-all(f32[8,5,8,128]{3,2,1,0:T(8,128)S(1)} %bitcast.49), channel_id=1, replica_groups=mesh['x_hi'=2,'y'=4,'x_lo'=2,'z'=8,'core'=2] {'z'}, dimensions={0} | all-to-all | bytes 327680 | tf_op jit(solution)/shard_map/all_to_all | solution.py:209
  62.0 10.7 %all_to_all.11 = f32[8,5,8,128]{3,2,1,0:T(8,128)S(1)} all-to-all(f32[8,5,8,128]{3,2,1,0:T(8,128)S(1)} %broadcast_in_dim.2), channel_id=1, replica_groups=mesh['x_hi'=2,'y'=4,'x_lo'=2,'z'=8,'core'=2] {'z'}, dimensions={0} | all-to-all | bytes 327680 | tf_op jit(solution)/shard_map/all_to_all | solution.py:211
  72.7 1.5 %collective-permute-start.11 = (f32[40,8,128]{2,1,0:T(8,128)S(1)}, f32[40,8,128]{2,1,0:T(8,128)S(1)}, u32[]{:S(2)}, u32[]{:S(2)}) collective-permute-start(f32[40,8,128]{2,1,0:T(8,128)S(1)} %bitcast.44), channel_id=1, source_target_pairs={{0,16},{1,17},{2,18},{3,19},{4,20},{5,21},{6,22},{7,23},{8,24},{9,... | collective-permute-start | bytes 491528 | tf_op jit(solution)/shard_map/ppermute | solution.py:31
  74.2 5.0 %collective-permute-start.12 = (f32[40,8,128]{2,1,0:T(8,128)S(1)}, f32[40,8,128]{2,1,0:T(8,128)S(1)}, u32[]{:S(2)}, u32[]{:S(2)}) collective-permute-start(f32[40,8,128]{2,1,0:T(8,128)S(1)} %bitcast.45), channel_id=1, source_target_pairs={{0,1},{1,0},{2,3},{3,2},{4,5},{5,4},{6,7},{7,6},{8,9},{9,8},{10,11... | collective-permute-start | bytes 491528 | tf_op jit(solution)/shard_map/ppermute | solution.py:31
  79.2 4.3 %collective-permute-start.13 = (f32[40,8,128]{2,1,0:T(8,128)S(1)}, f32[40,8,128]{2,1,0:T(8,128)S(1)}, u32[]{:S(2)}, u32[]{:S(2)}) collective-permute-start(f32[40,8,128]{2,1,0:T(8,128)S(1)} %collective-permute-done.11.beside), channel_id=1, source_target_pairs={{0,1},{1,0},{2,3},{3,2},{4,5},{5,4},{6,7},{7,6},{8,9},{9,8},{10,11... | collective-permute-start | bytes 491528 | tf_op jit(solution)/shard_map/ppermute | solution.py:31
  83.5 1.0 %collective-permute-done.13.other_beside = f32[40,8,128]{2,1,0:T(8,128)S(1)} collective-permute-done((f32[40,8,128]{2,1,0:T(8,128)S(1)}, f32[40,8,128]{2,1,0:T(8,128)S(1)}, u32[]{:S(2)}, u32[]{:S(2)}) %collective-permute-start.13) | collective-permute-done | bytes 163872 | tf_op jit(solution)/shard_map/ppermute | solution.py:31
  84.5 1.0 %lay_out.1 = f32[1,400,400]{2,1,0:T(8,128)} custom-call(f32[40,8,128]{2,1,0:T(8,128)S(1)} %bitcast.46, f32[40,8,128]{2,1,0:T(8,128)S(1)} %collective-permute-done.11.beside, f32[40,8,128]{2,1,0:T(8,128)S(1)} %collective-permute-done.12.other, f32[40,8,128]{2,1,0:T(8,128)S(1)} %collective-permute-done.13.other_beside), custom_call_target="tpu_custom_call" | custom-call | tf_op jit(solution)/shard_map/lay_out/pallas_call | solution.py:181
  (15 shorter events, 0.2 us)
Async XLA Ops:
  0.0 0.7 copy-start
  8.4 9.0 %collective-permute-start.4 = (f32[4,2,40,8,128]{4,3,2,1,0:T(8,128)S(1)}, f32[4,2,40,8,128]{4,3,2,1,0:T(8,128)S(1)}, u32[]{:S(2)}, u32[]{:S(2)}) collective-permute-start(f32[4,2,40,8,128]{4,3,2,1,0:T(8,128)S(1)} %get-tuple-element.14), channel_id=1, source_target_pairs={{0,1},{1,0},{2,3},{3,2},{4,5},{5,4},{6,7},{7,6},{8,9},{9,8},{10,11... | collective-permute-start | bytes 3932168 | tf_op jit(solution)/shard_map/ppermute | solution.py:31
  17.3 4.6 %collective-permute-start = (f32[4,2,40,8,128]{4,3,2,1,0:T(8,128)S(1)}, f32[4,2,40,8,128]{4,3,2,1,0:T(8,128)S(1)}, u32[]{:S(2)}, u32[]{:S(2)}) collective-permute-start(f32[4,2,40,8,128]{4,3,2,1,0:T(8,128)S(1)} %get-tuple-element.12), channel_id=1, source_target_pairs={{0,1},{1,0},{2,3},{3,2},{4,5},{5,4},{6,7},{7,6},{8,9},{9,8},{10,11... | collective-permute-start | bytes 3932168 | tf_op jit(solution)/shard_map/ppermute | solution.py:31
  17.4 1.2 %copy-start.2 = (f32[4,2,40,8,128]{4,3,2,1,0:T(8,128)}, f32[4,2,40,8,128]{4,3,2,1,0:T(8,128)S(1)}, u32[]{:S(2)}) copy-start(f32[4,2,40,8,128]{4,3,2,1,0:T(8,128)S(1)} %collective-permute-done.4) | copy-start | bytes 3932164
  18.6 10.9 %collective-permute-start.7 = (f32[2,40,8,128]{3,2,1,0:T(8,128)S(1)}, f32[2,40,8,128]{3,2,1,0:T(8,128)S(1)}, u32[]{:S(2)}, u32[]{:S(2)}) collective-permute-start(f32[2,40,8,128]{3,2,1,0:T(8,128)S(1)} %get-tuple-element.19), channel_id=1, source_target_pairs={{0,96},{1,145},{2,98},{3,147},{4,100},{5,149},{6,102},{7,151},{8,1... | collective-permute-start | bytes 983048 | tf_op jit(solution)/shard_map/ppermute | solution.py:31
  19.2 10.4 %collective-permute-start.6 = (f32[2,40,8,128]{3,2,1,0:T(8,128)}, f32[2,40,8,128]{3,2,1,0:T(8,128)}, u32[]{:S(2)}, u32[]{:S(2)}) collective-permute-start(f32[2,40,8,128]{3,2,1,0:T(8,128)} %get-tuple-element.20), channel_id=1, source_target_pairs={{0,64},{1,129},{2,66},{3,131},{4,68},{5,133},{6,70},{7,135},{8,72}... | collective-permute-start | bytes 983048 | tf_op jit(solution)/shard_map/ppermute | solution.py:31
  19.9 10.6 %collective-permute-start.5 = (f32[2,40,8,128]{3,2,1,0:T(8,128)S(1)}, f32[2,40,8,128]{3,2,1,0:T(8,128)}, u32[]{:S(2)}, u32[]{:S(2)}) collective-permute-start(f32[2,40,8,128]{3,2,1,0:T(8,128)S(1)} %get-tuple-element.18), channel_id=1, source_target_pairs={{0,32},{1,17},{2,34},{3,19},{4,36},{5,21},{6,38},{7,23},{8,40},{9,... | collective-permute-start | bytes 983048 | tf_op jit(solution)/shard_map/ppermute | solution.py:31
  21.9 1.4 %copy-start.1 = (f32[4,2,40,8,128]{4,3,2,1,0:T(8,128)}, f32[4,2,40,8,128]{4,3,2,1,0:T(8,128)S(1)}, u32[]{:S(2)}) copy-start(f32[4,2,40,8,128]{4,3,2,1,0:T(8,128)S(1)} %collective-permute-done) | copy-start | bytes 3932164
  23.3 13.4 %collective-permute-start.3 = (f32[2,40,8,128]{3,2,1,0:T(8,128)}, f32[2,40,8,128]{3,2,1,0:T(8,128)}, u32[]{:S(2)}, u32[]{:S(2)}) collective-permute-start(f32[2,40,8,128]{3,2,1,0:T(8,128)} %get-tuple-element.16), channel_id=1, source_target_pairs={{0,96},{1,145},{2,98},{3,147},{4,100},{5,149},{6,102},{7,151},{8,1... | collective-permute-start | bytes 983048 | tf_op jit(solution)/shard_map/ppermute | solution.py:31
  23.8 12.9 %collective-permute-start.2 = (f32[2,40,8,128]{3,2,1,0:T(8,128)}, f32[2,40,8,128]{3,2,1,0:T(8,128)}, u32[]{:S(2)}, u32[]{:S(2)}) collective-permute-start(f32[2,40,8,128]{3,2,1,0:T(8,128)} %get-tuple-element.17), channel_id=1, source_target_pairs={{0,64},{1,129},{2,66},{3,131},{4,68},{5,133},{6,70},{7,135},{8,72}... | collective-permute-start | bytes 983048 | tf_op jit(solution)/shard_map/ppermute | solution.py:31
  29.6 8.0 %collective-permute-start.1 = (f32[2,40,8,128]{3,2,1,0:T(8,128)}, f32[2,40,8,128]{3,2,1,0:T(8,128)}, u32[]{:S(2)}, u32[]{:S(2)}) collective-permute-start(f32[2,40,8,128]{3,2,1,0:T(8,128)} %get-tuple-element.15), channel_id=1, source_target_pairs={{0,32},{1,17},{2,34},{3,19},{4,36},{5,21},{6,38},{7,23},{8,40},{9,... | collective-permute-start | bytes 983048 | tf_op jit(solution)/shard_map/ppermute | solution.py:31
  39.0 7.5 %collective-permute-start.10 = (f32[40,8,128]{2,1,0:T(8,128)S(1)}, f32[40,8,128]{2,1,0:T(8,128)S(1)}, u32[]{:S(2)}, u32[]{:S(2)}) collective-permute-start(f32[40,8,128]{2,1,0:T(8,128)S(1)} %get-tuple-element.23), channel_id=1, source_target_pairs={{0,144},{1,97},{2,146},{3,99},{4,148},{5,101},{6,150},{7,103},{8,1... | collective-permute-start | bytes 491528 | tf_op jit(solution)/shard_map/ppermute | solution.py:31
  40.1 6.4 %collective-permute-start.9 = (f32[40,8,128]{2,1,0:T(8,128)S(1)}, f32[40,8,128]{2,1,0:T(8,128)S(1)}, u32[]{:S(2)}, u32[]{:S(2)}) collective-permute-start(f32[40,8,128]{2,1,0:T(8,128)S(1)} %get-tuple-element.22), channel_id=1, source_target_pairs={{0,128},{1,65},{2,130},{3,67},{4,132},{5,69},{6,134},{7,71},{8,136... | collective-permute-start | bytes 491528 | tf_op jit(solution)/shard_map/ppermute | solution.py:31
  40.4 6.7 %collective-permute-start.8 = (f32[40,8,128]{2,1,0:T(8,128)S(1)}, f32[40,8,128]{2,1,0:T(8,128)S(1)}, u32[]{:S(2)}, u32[]{:S(2)}) collective-permute-start(f32[40,8,128]{2,1,0:T(8,128)S(1)} %get-tuple-element.21), channel_id=1, source_target_pairs={{0,16},{1,33},{2,18},{3,35},{4,20},{5,37},{6,22},{7,39},{8,24},{9,... | collective-permute-start | bytes 491528 | tf_op jit(solution)/shard_map/ppermute | solution.py:31
  72.7 6.5 %collective-permute-start.11 = (f32[40,8,128]{2,1,0:T(8,128)S(1)}, f32[40,8,128]{2,1,0:T(8,128)S(1)}, u32[]{:S(2)}, u32[]{:S(2)}) collective-permute-start(f32[40,8,128]{2,1,0:T(8,128)S(1)} %bitcast.44), channel_id=1, source_target_pairs={{0,16},{1,17},{2,18},{3,19},{4,20},{5,21},{6,22},{7,23},{8,24},{9,... | collective-permute-start | bytes 491528 | tf_op jit(solution)/shard_map/ppermute | solution.py:31
  74.2 9.3 %collective-permute-start.12 = (f32[40,8,128]{2,1,0:T(8,128)S(1)}, f32[40,8,128]{2,1,0:T(8,128)S(1)}, u32[]{:S(2)}, u32[]{:S(2)}) collective-permute-start(f32[40,8,128]{2,1,0:T(8,128)S(1)} %bitcast.45), channel_id=1, source_target_pairs={{0,1},{1,0},{2,3},{3,2},{4,5},{5,4},{6,7},{7,6},{8,9},{9,8},{10,11... | collective-permute-start | bytes 491528 | tf_op jit(solution)/shard_map/ppermute | solution.py:31
  79.2 5.3 %collective-permute-start.13 = (f32[40,8,128]{2,1,0:T(8,128)S(1)}, f32[40,8,128]{2,1,0:T(8,128)S(1)}, u32[]{:S(2)}, u32[]{:S(2)}) collective-permute-start(f32[40,8,128]{2,1,0:T(8,128)S(1)} %collective-permute-done.11.beside), channel_id=1, source_target_pairs={{0,1},{1,0},{2,3},{3,2},{4,5},{5,4},{6,7},{7,6},{8,9},{9,8},{10,11... | collective-permute-start | bytes 491528 | tf_op jit(solution)/shard_map/ppermute | solution.py:31

commit v3 on v2

--- a/solution.py
+++ b/solution.py
@@ -8,7 +8,8 @@
 
 FINE = ("x_hi", "y", "x_lo", "z", "core")
 SIZES = (2, 4, 2, 8, 2)
-GROUPS, WIDE, TILES, UNIT = 50, 3, 160, 40
+HALF_GROUPS, WIDE, UNIT, PIECE = 25, 3, 40, 10
+FULL = HALF_GROUPS * WIDE
 
 
 def position(x, y, z, core):
@@ -39,6 +40,10 @@
     return (0, (y ^ step) - y, 0, 0) if core == turn else ((x ^ step) - x, 0, 0, 0)
 
 
+def along(step, x, y, z, core):
+    return 0, 0, (z ^ step) - z, 0
+
+
 def block_of(place):
     run, y = place // 4, place % 4
     return (y // 2 ^ run) * 4 + y
@@ -55,6 +60,7 @@
     x = lax.axis_index("x_hi") * 2 + x_low
     y = lax.axis_index("y")
     core = lax.axis_index("core")
+    starts = [(lax.axis_index("z") // 2 ^ q) * PIECE for q in range(4)]
 
     def arrivals(place, o, act):
         block = block_of(place)
@@ -75,18 +81,20 @@
 
     lane = lax.broadcasted_iota(jnp.int32, (8, 128), 1)
 
-    def tile_of(t):
-        if t < GROUPS * WIDE:
-            g, l = divmod(t, WIDE)
-            return acc[8 * g : 8 * g + 8, 128 * l : 128 * l + 128]
-        tile = jnp.zeros((8, 128), jnp.float32)
-        first = 8 * (t - GROUPS * WIDE)
-        for k in range(max(0, min(8, GROUPS - first))):
-            g = first + k
-            piece = acc[8 * g : 8 * g + 8, 128 * WIDE : 128 * WIDE + 128]
-            if k:
-                piece = pltpu.roll(piece, 16 * k, 1)
-            tile = jnp.where((lane >= 16 * k) & (lane < 16 * k + 16), piece, tile)
+    def tile_of(acc, half, m):
+        if m == UNIT * 2 - 1:
+            return jnp.zeros((8, 128), jnp.float32)
+
+        def read(g, l):
+            row = pl.multiple_of(half * (8 * HALF_GROUPS) + 8 * g, 8)
+            return acc[pl.ds(row, 8), 128 * l : 128 * l + 128]
+
+        if m < FULL:
+            return read(*divmod(m, WIDE))
+        first = 8 * (m - FULL)
+        tile = read(first, WIDE)
+        for k in range(1, min(8, HALF_GROUPS - first)):
+            tile = jnp.where(lane < 16 * k, tile, pltpu.roll(read(first + k, WIDE), 16 * k, 1))
         return tile
 
     def step(i, carry):
@@ -105,16 +113,13 @@
         acc[:, :size] = total
 
         high, dy = block // 4, i ^ y
-        for half in range(2):
-            for target, here in ((keep, core == half), (give, core != half)):
-
-                @pl.when(here)
-                def _():
-                    for low in range(2):
-                        u, dx = half * 2 + low, (high * 2 + low) ^ x
-                        k, j = (dy, low ^ x_low) if half == 0 else (dx, dy & 1)
-                        for n in range(UNIT):
-                            target[k, j, n] = tile_of(u * UNIT + n)
+        for target, half in ((keep, core), (give, 1 - core)):
+            for low in range(2):
+                dx = (high * 2 + low) ^ x
+                k = jnp.where(half == 0, dy, dx)
+                j = jnp.where(half == 0, low ^ x_low, dy & 1)
+                for n in range(UNIT):
+                    target[k, j, starts[n // PIECE] + n % PIECE] = tile_of(acc, half, low * UNIT + n)
 
         return carry
 
@@ -157,24 +162,66 @@
     )(table, pltpu.with_memory_space_constraint(blocks, pltpu.VMEM))
 
 
+def combine(body, outs, *arrays):
+    in_vmem = pl.BlockSpec(memory_space=pltpu.VMEM)
+    return pl.pallas_call(
+        body,
+        out_shape=tuple(pltpu.VMEM(shape, jnp.float32) for shape in outs),
+        in_specs=[in_vmem] * len(arrays),
+        out_specs=(in_vmem,) * len(outs),
+        compiler_params=pltpu.CompilerParams(vmem_limit_bytes=4 << 20),
+        name=body.__name__,
+    )(*(pltpu.with_memory_space_constraint(array, pltpu.VMEM) for array in arrays))
+
+
+def add_halves(keep, got, *sums):
+    for k, out in enumerate(sums):
+        out[...] = keep[k] + got[k]
+
+
+def add_ring(*refs):
+    arrived, sums = refs[:8], refs[8:]
+    swapped = (lax.axis_index("y") >> 1) ^ lax.axis_index("x_hi")
+    for turn in range(2):
+
+        @pl.when(swapped == turn)
+        def _():
+            for run in range(2):
+                a, b, c, d = arrived[4 * run : 4 * run + 4]
+                for low in range(2):
+                    sums[2 * (run ^ turn) + low][...] = (a[low] + b[low]) + (c[low] + d[low])
+
+
+def add_last(*refs):
+    a, b, c, d = refs[:4]
+    for r, out in enumerate(refs[4:]):
+        part = slice(r * PIECE, (r + 1) * PIECE)
+        out[...] = (a[part] + b[part]) + (c[part] + d[part])
+
+
 def layout_kernel(scale, mine, beside, other, other_beside, out, whole):
     low, core = lax.axis_index("x_lo"), lax.axis_index("core")
+    away = lax.axis_index("z") // 2
     for ref, u in (
         (mine, core * 2 + low),
         (beside, core * 2 + 1 - low),
         (other, (1 - core) * 2 + low),
         (other_beside, (1 - core) * 2 + 1 - low),
     ):
-        whole[pl.ds(u * UNIT, UNIT)] = ref[...] * scale
-    for t in range(GROUPS * WIDE):
-        g, l = divmod(t, WIDE)
-        out[0, 8 * g : 8 * g + 8, 128 * l : 128 * l + 128] = whole[t]
-    for g in range(GROUPS):
-        n, k = divmod(g, 8)
-        tile = whole[GROUPS * WIDE + n]
-        if k:
-            tile = pltpu.roll(tile, 128 - 16 * k, 1)
-        out[0, 8 * g : 8 * g + 8, 128 * WIDE : 128 * WIDE + 16] = tile[:, :16]
+        for r in range(4):
+            whole[pl.ds(u * UNIT + (away ^ r) * PIECE, PIECE)] = ref[r * PIECE : (r + 1) * PIECE] * scale
+    for half in range(2):
+        for m in range(FULL):
+            g, l = divmod(m, WIDE)
+            row = 8 * (half * HALF_GROUPS + g)
+            out[0, row : row + 8, 128 * l : 128 * l + 128] = whole[half * 2 * UNIT + m]
+        for g in range(HALF_GROUPS):
+            n, k = divmod(g, 8)
+            tile = whole[half * 2 * UNIT + FULL + n]
+            if k:
+                tile = pltpu.roll(tile, 128 - 16 * k, 1)
+            row = 8 * (half * HALF_GROUPS + g)
+            out[0, row : row + 8, 128 * WIDE : 128 * WIDE + 16] = tile[:, :16]
 
 
 def lay_out(scale, size, *units):
@@ -183,7 +230,7 @@
         out_shape=jax.ShapeDtypeStruct((1, size, size), jnp.float32),
         in_specs=[pl.BlockSpec(memory_space=pltpu.VMEM)] * 4,
         out_specs=pl.BlockSpec(memory_space=pltpu.VMEM),
-        scratch_shapes=[pltpu.VMEM((TILES, 8, 128), jnp.float32)],
+        scratch_shapes=[pltpu.VMEM((4 * UNIT, 8, 128), jnp.float32)],
         compiler_params=pltpu.CompilerParams(vmem_limit_bytes=8 << 20),
         name="lay_out",
     )(*(pltpu.with_memory_space_constraint(unit, pltpu.VMEM) for unit in units))
@@ -197,18 +244,18 @@
     keep, give = densities(1, table, own, blocks)
     runs[1] = (keep, send(give, across))
 
-    sums = []
+    unit, piece = (UNIT, 8, 128), (PIECE, 8, 128)
+    arrived = []
     for keep, got in runs:
-        first = [keep[k] + got[k] for k in range(4)]
-        came = [send(first[k], functools.partial(around, k, 0)) for k in (1, 2, 3)]
-        sums.append(first[0] + came[0] + came[1] + came[2])
-    swapped = (lax.axis_index("y") >> 1) != lax.axis_index("x_hi")
-    second = [jnp.where(swapped, sums[1 - j // 2][j % 2], sums[j // 2][j % 2]) for j in range(4)]
+        first = combine(add_halves, [(2, *unit)] * 4, keep, got)
+        arrived += [first[0]] + [send(first[k], functools.partial(around, k, 0)) for k in (1, 2, 3)]
+    second = combine(add_ring, [unit] * 4, *arrived)
     came = [send(second[j], functools.partial(around, j, 1)) for j in (1, 2, 3)]
-    third = second[0] + came[0] + came[1] + came[2]
-    parts = lax.all_to_all(third.reshape(8, UNIT // 8, 8, 128), "z", 0, 0, tiled=True)
-    eighth = jnp.sum(parts, axis=0, keepdims=True)
-    mine = lax.all_to_all(jnp.broadcast_to(eighth, parts.shape), "z", 0, 0, tiled=True).reshape(UNIT, 8, 128)
+    third = combine(add_last, [piece] * 4, second[0], *came)
+    came = [send(third[r], functools.partial(along, 2 * r)) for r in (1, 2, 3)]
+    fourth = (third[0] + came[0]) + (came[1] + came[2])
+    fifth = fourth + send(fourth, functools.partial(along, 1))
+    mine = jnp.concatenate([fifth] + [send(fifth, functools.partial(along, 2 * r)) for r in (1, 2, 3)])
     beside = send(mine, lambda x, y, z, core: (1 - 2 * (x % 2), 0, 0, 0))
     other = send(mine, across)
     other_beside = send(beside, across)

time: 85.7 us -> 88.1 us (1.028)
  blocking collectives: 25.5 us -> 0 us
  starting transfers between devices: 22.5 us -> 42.2 us
  waiting for transfers between devices: 17.1 us -> 30.4 us
  other arithmetic: 4.68 us -> 0.03 us
    all_to_all x2 -> x0, blocking collectives: 25.5 us -> none  [the longest x1 14.8 us: on_device(): lax.all_to_all(third.reshape(8, UNIT // 8, 8, 128), 'z', 0, 0, tiled=True)]
    ppermute x14 -> x21, starting transfers between devices: 22.5 us -> 42.2 us  [send(): return lax.ppermute(value, FINE, pairs(move))]
    ppermute x14 -> x21, waiting for transfers between devices: 17.1 us -> 30.4 us  [send(): return lax.ppermute(value, FINE, pairs(move))]
    add x5 -> x2, other arithmetic: 4.62 us -> 0.02 us  [the longest x1 0.01 us: on_device(): fourth = third[0] + came[0] + (came[1] + came[2])]
  transfers between devices with their start and end apart: 14 -> 21, of which waited for: 7 -> 15; matrix products, arithmetic and copies ran while one was open for 4% -> 0% of each run, Pallas kernels for 7% -> 7%
where the time goes in v3:
time: 88.1 us
  starting transfers between devices  42.2 us (48%)
  waiting for transfers between devices  30.4 us (35%)
  Pallas kernels  14.7 us (17%)
    ppermute x21, starting transfers between devices, send(): return lax.ppermute(value, FINE, pairs(move))  42.2 us
    ppermute x21, waiting for transfers between devices, send(): return lax.ppermute(value, FINE, pairs(move))  30.4 us
    pallas_call x1, Pallas kernels, densities(): pl.pallas_call(functools.partial(density_kernel, 0), out_shape=(pltpu.VME...  7.65 us
    pallas_call x1, Pallas kernels, densities(): pl.pallas_call(later, out_shape=(half, half), in_specs=[pl.BlockSpec(memo...  5.55 us
  transfers between devices with their start and end apart: 21, of which 15 were waited for; matrix products, arithmetic and copies ran while one was open for 0% of the time, Pallas kernels for 7%

profile of v3, /device:TPU:1, one launch (start us, length us, event | category | flops | bytes accessed | tf_op | source)
XLA Modules:
  0.0 88.1 jit_solution(4179571842423246794)
XLA Ops:
  0.0 0.7 copy-done
  0.7 7.6 %densities.2 = (bf16[8,4,400,400]{3,2,1,0:T(8,128)(2,1)S(1)}, f32[4,2,40,8,128]{4,3,2,1,0:T(8,128)S(1)}, f32[4,2,40,8,128]{4,3,2,1,0:T(8,128)S(1)}) custom-call(s32[8]{0:T(128)S(1)} %bitcast.2, bf16[8,4,400,400]{3,2,1,0:T(8,128)(2,1)} %bitcast.4), custom_call_target="tpu_custom_call" | custom-call | flops 4294967296 | bytes 13631488 | tf_op jit(solution)/shard_map/densities/pallas_call | solution.py:143
  8.3 3.3 %collective-permute-start = (f32[4,2,40,8,128]{4,3,2,1,0:T(8,128)S(1)}, f32[4,2,40,8,128]{4,3,2,1,0:T(8,128)S(1)}, u32[]{:S(2)}, u32[]{:S(2)}) collective-permute-start(f32[4,2,40,8,128]{4,3,2,1,0:T(8,128)S(1)} %get-tuple-element.27), channel_id=1, source_target_pairs={{0,1},{1,0},{2,3},{3,2},{4,5},{5,4},{6,7},{7,6},{8,9},{9,8},{10,11... | collective-permute-start | bytes 3932168 | tf_op jit(solution)/shard_map/ppermute | solution.py:32
  11.6 5.5 %densities.3 = (f32[4,2,40,8,128]{4,3,2,1,0:T(8,128)S(1)}, f32[4,2,40,8,128]{4,3,2,1,0:T(8,128)S(1)}) custom-call(s32[8]{0:T(128)S(1)} %bitcast.3, bf16[8,4,400,400]{3,2,1,0:T(8,128)(2,1)S(1)} %get-tuple-element.32.blocks), custom_call_target="tpu_custom_call" | custom-call | flops 4294967296 | bytes 13631488 | tf_op jit(solution)/shard_map/densities/pallas_call | solution.py:155
  17.5 1.9 %collective-permute-start.2 = (f32[2,40,8,128]{3,2,1,0:T(8,128)S(1)}, f32[2,40,8,128]{3,2,1,0:T(8,128)S(1)}, u32[]{:S(2)}, u32[]{:S(2)}) collective-permute-start(f32[2,40,8,128]{3,2,1,0:T(8,128)S(1)} %get-tuple-element.30), channel_id=1, source_target_pairs={{0,64},{1,129},{2,66},{3,131},{4,68},{5,133},{6,70},{7,135},{8,72}... | collective-permute-start | bytes 983048 | tf_op jit(solution)/shard_map/ppermute | solution.py:32
  19.4 1.9 %collective-permute-start.3 = (f32[2,40,8,128]{3,2,1,0:T(8,128)S(1)}, f32[2,40,8,128]{3,2,1,0:T(8,128)S(1)}, u32[]{:S(2)}, u32[]{:S(2)}) collective-permute-start(f32[2,40,8,128]{3,2,1,0:T(8,128)S(1)} %get-tuple-element.31), channel_id=1, source_target_pairs={{0,96},{1,145},{2,98},{3,147},{4,100},{5,149},{6,102},{7,151},{8,1... | collective-permute-start | bytes 983048 | tf_op jit(solution)/shard_map/ppermute | solution.py:32
  21.6 1.9 %collective-permute-start.6 = (f32[2,40,8,128]{3,2,1,0:T(8,128)S(1)}, f32[2,40,8,128]{3,2,1,0:T(8,128)S(1)}, u32[]{:S(2)}, u32[]{:S(2)}) collective-permute-start(f32[2,40,8,128]{3,2,1,0:T(8,128)S(1)} %get-tuple-element.37), channel_id=1, source_target_pairs={{0,64},{1,129},{2,66},{3,131},{4,68},{5,133},{6,70},{7,135},{8,72}... | collective-permute-start | bytes 983048 | tf_op jit(solution)/shard_map/ppermute | solution.py:32
  23.7 1.7 %collective-permute-start.7 = (f32[2,40,8,128]{3,2,1,0:T(8,128)S(1)}, f32[2,40,8,128]{3,2,1,0:T(8,128)S(1)}, u32[]{:S(2)}, u32[]{:S(2)}) collective-permute-start(f32[2,40,8,128]{3,2,1,0:T(8,128)S(1)} %get-tuple-element.38), channel_id=1, source_target_pairs={{0,96},{1,145},{2,98},{3,147},{4,100},{5,149},{6,102},{7,151},{8,1... | collective-permute-start | bytes 983048 | tf_op jit(solution)/shard_map/ppermute | solution.py:32
  25.5 2.3 %collective-permute-done.2.refs_2_ = f32[2,40,8,128]{3,2,1,0:T(8,128)S(1)} collective-permute-done((f32[2,40,8,128]{3,2,1,0:T(8,128)S(1)}, f32[2,40,8,128]{3,2,1,0:T(8,128)S(1)}, u32[]{:S(2)}, u32[]{:S(2)}) %collective-permute-start.2) | collective-permute-done | bytes 327712 | tf_op jit(solution)/shard_map/ppermute | solution.py:32
  27.8 2.6 %collective-permute-done.3.refs_3_ = f32[2,40,8,128]{3,2,1,0:T(8,128)S(1)} collective-permute-done((f32[2,40,8,128]{3,2,1,0:T(8,128)S(1)}, f32[2,40,8,128]{3,2,1,0:T(8,128)S(1)}, u32[]{:S(2)}, u32[]{:S(2)}) %collective-permute-start.3) | collective-permute-done | bytes 327712 | tf_op jit(solution)/shard_map/ppermute | solution.py:32
  30.4 0.4 collective-permute-done.5.refs_5_
  30.8 4.0 %collective-permute-done.6.refs_6_ = f32[2,40,8,128]{3,2,1,0:T(8,128)S(1)} collective-permute-done((f32[2,40,8,128]{3,2,1,0:T(8,128)S(1)}, f32[2,40,8,128]{3,2,1,0:T(8,128)S(1)}, u32[]{:S(2)}, u32[]{:S(2)}) %collective-permute-start.6) | collective-permute-done | bytes 327712 | tf_op jit(solution)/shard_map/ppermute | solution.py:32
  34.8 2.6 %collective-permute-done.7.refs_7_ = f32[2,40,8,128]{3,2,1,0:T(8,128)S(1)} collective-permute-done((f32[2,40,8,128]{3,2,1,0:T(8,128)S(1)}, f32[2,40,8,128]{3,2,1,0:T(8,128)S(1)}, u32[]{:S(2)}, u32[]{:S(2)}) %collective-permute-start.7) | collective-permute-done | bytes 327712 | tf_op jit(solution)/shard_map/ppermute | solution.py:32
  37.5 1.1 %collective-permute-start.8 = (f32[40,8,128]{2,1,0:T(8,128)S(1)}, f32[40,8,128]{2,1,0:T(8,128)S(1)}, u32[]{:S(2)}, u32[]{:S(2)}) collective-permute-start(f32[40,8,128]{2,1,0:T(8,128)S(1)} %get-tuple-element.40), channel_id=1, source_target_pairs={{0,16},{1,33},{2,18},{3,35},{4,20},{5,37},{6,22},{7,39},{8,24},{9,... | collective-permute-start | bytes 491528 | tf_op jit(solution)/shard_map/ppermute | solution.py:32
  38.6 2.9 %collective-permute-start.9 = (f32[40,8,128]{2,1,0:T(8,128)S(1)}, f32[40,8,128]{2,1,0:T(8,128)S(1)}, u32[]{:S(2)}, u32[]{:S(2)}) collective-permute-start(f32[40,8,128]{2,1,0:T(8,128)S(1)} %get-tuple-element.41), channel_id=1, source_target_pairs={{0,128},{1,65},{2,130},{3,67},{4,132},{5,69},{6,134},{7,71},{8,136... | collective-permute-start | bytes 491528 | tf_op jit(solution)/shard_map/ppermute | solution.py:32
  41.6 0.3 collective-permute-done.8.refs_1_
  41.8 4.3 %collective-permute-done.9.refs_2_ = f32[40,8,128]{2,1,0:T(8,128)S(1)} collective-permute-done((f32[40,8,128]{2,1,0:T(8,128)S(1)}, f32[40,8,128]{2,1,0:T(8,128)S(1)}, u32[]{:S(2)}, u32[]{:S(2)}) %collective-permute-start.9) | collective-permute-done | bytes 163872 | tf_op jit(solution)/shard_map/ppermute | solution.py:32
  46.1 2.0 %collective-permute-done.10.refs_3_ = f32[40,8,128]{2,1,0:T(8,128)S(1)} collective-permute-done((f32[40,8,128]{2,1,0:T(8,128)S(1)}, f32[40,8,128]{2,1,0:T(8,128)S(1)}, u32[]{:S(2)}, u32[]{:S(2)}) %collective-permute-start.10) | collective-permute-done | bytes 163872 | tf_op jit(solution)/shard_map/ppermute | solution.py:32
  48.1 2.3 %collective-permute-start.11 = (f32[10,8,128]{2,1,0:T(8,128)S(1)}, f32[10,8,128]{2,1,0:T(8,128)S(1)}, u32[]{:S(2)}, u32[]{:S(2)}) collective-permute-start(f32[10,8,128]{2,1,0:T(8,128)S(1)} %get-tuple-element.44), channel_id=1, source_target_pairs={{0,4},{1,5},{2,6},{3,7},{4,0},{5,1},{6,2},{7,3},{8,12},{9,13},{10,... | collective-permute-start | bytes 122888 | tf_op jit(solution)/shard_map/ppermute | solution.py:32
  50.4 5.6 %collective-permute-start.12 = (f32[10,8,128]{2,1,0:T(8,128)S(1)}, f32[10,8,128]{2,1,0:T(8,128)S(1)}, u32[]{:S(2)}, u32[]{:S(2)}) collective-permute-start(f32[10,8,128]{2,1,0:T(8,128)S(1)} %get-tuple-element.45), channel_id=1, source_target_pairs={{0,8},{1,9},{2,10},{3,11},{4,12},{5,13},{6,14},{7,15},{8,0},{9,1},... | collective-permute-start | bytes 122888 | tf_op jit(solution)/shard_map/ppermute | solution.py:32
  56.0 1.8 %collective-permute-done.12 = f32[10,8,128]{2,1,0:T(8,128)S(1)} collective-permute-done((f32[10,8,128]{2,1,0:T(8,128)S(1)}, f32[10,8,128]{2,1,0:T(8,128)S(1)}, u32[]{:S(2)}, u32[]{:S(2)}) %collective-permute-start.12) | collective-permute-done | bytes 40992 | tf_op jit(solution)/shard_map/ppermute | solution.py:32
  57.8 3.4 %collective-permute-done.13 = f32[10,8,128]{2,1,0:T(8,128)S(1)} collective-permute-done((f32[10,8,128]{2,1,0:T(8,128)S(1)}, f32[10,8,128]{2,1,0:T(8,128)S(1)}, u32[]{:S(2)}, u32[]{:S(2)}) %collective-permute-start.13) | collective-permute-done | bytes 40992 | tf_op jit(solution)/shard_map/ppermute | solution.py:32
  61.3 0.5 collective-permute-start.14
  61.8 2.7 %collective-permute-done.14 = f32[10,8,128]{2,1,0:T(8,128)S(1)} collective-permute-done((f32[10,8,128]{2,1,0:T(8,128)S(1)}, f32[10,8,128]{2,1,0:T(8,128)S(1)}, u32[]{:S(2)}, u32[]{:S(2)}) %collective-permute-start.14) | collective-permute-done | bytes 40992 | tf_op jit(solution)/shard_map/ppermute | solution.py:32
  64.5 1.4 %collective-permute-start.17 = (f32[10,8,128]{2,1,0:T(8,128)S(1)}, f32[10,8,128]{2,1,0:T(8,128)S(1)}, u32[]{:S(2)}, u32[]{:S(2)}) collective-permute-start(f32[10,8,128]{2,1,0:T(8,128)S(1)} %add.15), channel_id=1, source_target_pairs={{0,12},{1,13},{2,14},{3,15},{4,8},{5,9},{6,10},{7,11},{8,4},{9,5},... | collective-permute-start | bytes 122888 | tf_op jit(solution)/shard_map/ppermute | solution.py:32
  65.9 3.2 %collective-permute-start.16 = (f32[10,8,128]{2,1,0:T(8,128)S(1)}, f32[10,8,128]{2,1,0:T(8,128)S(1)}, u32[]{:S(2)}, u32[]{:S(2)}) collective-permute-start(f32[10,8,128]{2,1,0:T(8,128)S(1)} %add.15), channel_id=1, source_target_pairs={{0,8},{1,9},{2,10},{3,11},{4,12},{5,13},{6,14},{7,15},{8,0},{9,1},... | collective-permute-start | bytes 122888 | tf_op jit(solution)/shard_map/ppermute | solution.py:32
  69.1 1.0 %collective-permute-start.15 = (f32[10,8,128]{2,1,0:T(8,128)S(1)}, f32[10,8,128]{2,1,0:T(8,128)S(1)}, u32[]{:S(2)}, u32[]{:S(2)}) collective-permute-start(f32[10,8,128]{2,1,0:T(8,128)S(1)} %add.15), channel_id=1, source_target_pairs={{0,4},{1,5},{2,6},{3,7},{4,0},{5,1},{6,2},{7,3},{8,12},{9,13},{10,... | collective-permute-start | bytes 122888 | tf_op jit(solution)/shard_map/ppermute | solution.py:32
  70.2 2.5 %collective-permute-done.16 = f32[10,8,128]{2,1,0:T(8,128)S(1)} collective-permute-done((f32[10,8,128]{2,1,0:T(8,128)S(1)}, f32[10,8,128]{2,1,0:T(8,128)S(1)}, u32[]{:S(2)}, u32[]{:S(2)}) %collective-permute-start.16) | collective-permute-done | bytes 40992 | tf_op jit(solution)/shard_map/ppermute | solution.py:32
  73.0 7.8 %collective-permute-start.19 = (f32[40,8,128]{2,1,0:T(8,128)S(1)}, f32[40,8,128]{2,1,0:T(8,128)S(1)}, u32[]{:S(2)}, u32[]{:S(2)}) collective-permute-start(f32[40,8,128]{2,1,0:T(8,128)S(1)} %pad_maximum_fusion.mine), channel_id=1, source_target_pairs={{0,1},{1,0},{2,3},{3,2},{4,5},{5,4},{6,7},{7,6},{8,9},{9,8},{10,11... | collective-permute-start | bytes 491528 | tf_op jit(solution)/shard_map/ppermute | solution.py:32
  80.8 5.2 %collective-permute-start.20 = (f32[40,8,128]{2,1,0:T(8,128)S(1)}, f32[40,8,128]{2,1,0:T(8,128)S(1)}, u32[]{:S(2)}, u32[]{:S(2)}) collective-permute-start(f32[40,8,128]{2,1,0:T(8,128)S(1)} %collective-permute-done.18.beside), channel_id=1, source_target_pairs={{0,1},{1,0},{2,3},{3,2},{4,5},{5,4},{6,7},{7,6},{8,9},{9,8},{10,11... | collective-permute-start | bytes 491528 | tf_op jit(solution)/shard_map/ppermute | solution.py:32
  86.0 1.0 %collective-permute-done.20.other_beside = f32[40,8,128]{2,1,0:T(8,128)S(1)} collective-permute-done((f32[40,8,128]{2,1,0:T(8,128)S(1)}, f32[40,8,128]{2,1,0:T(8,128)S(1)}, u32[]{:S(2)}, u32[]{:S(2)}) %collective-permute-start.20) | collective-permute-done | bytes 163872 | tf_op jit(solution)/shard_map/ppermute | solution.py:32
  87.1 1.1 %lay_out.1 = f32[1,400,400]{2,1,0:T(8,128)} custom-call(f32[40,8,128]{2,1,0:T(8,128)S(1)} %pad_maximum_fusion.mine, f32[40,8,128]{2,1,0:T(8,128)S(1)} %collective-permute-done.18.beside, f32[40,8,128]{2,1,0:T(8,128)S(1)} %collective-permute-done.19.other, f32[40,8,128]{2,1,0:T(8,128)S(1)} %collective-permute-done.20.other_beside), custom_call_target="tpu_custom_call" | custom-call | tf_op jit(solution)/shard_map/lay_out/pallas_call | solution.py:228
  (22 shorter events, 1.3 us)
Async XLA Ops:
  0.0 0.7 copy-start
  8.3 9.0 %collective-permute-start = (f32[4,2,40,8,128]{4,3,2,1,0:T(8,128)S(1)}, f32[4,2,40,8,128]{4,3,2,1,0:T(8,128)S(1)}, u32[]{:S(2)}, u32[]{:S(2)}) collective-permute-start(f32[4,2,40,8,128]{4,3,2,1,0:T(8,128)S(1)} %get-tuple-element.27), channel_id=1, source_target_pairs={{0,1},{1,0},{2,3},{3,2},{4,5},{5,4},{6,7},{7,6},{8,9},{9,8},{10,11... | collective-permute-start | bytes 3932168 | tf_op jit(solution)/shard_map/ppermute | solution.py:32
  17.2 4.2 %collective-permute-start.4 = (f32[4,2,40,8,128]{4,3,2,1,0:T(8,128)S(1)}, f32[4,2,40,8,128]{4,3,2,1,0:T(8,128)S(1)}, u32[]{:S(2)}, u32[]{:S(2)}) collective-permute-start(f32[4,2,40,8,128]{4,3,2,1,0:T(8,128)S(1)} %get-tuple-element.34), channel_id=1, source_target_pairs={{0,1},{1,0},{2,3},{3,2},{4,5},{5,4},{6,7},{7,6},{8,9},{9,8},{10,11... | collective-permute-start | bytes 3932168 | tf_op jit(solution)/shard_map/ppermute | solution.py:32
  17.4 6.3 %collective-permute-start.1 = (f32[2,40,8,128]{3,2,1,0:T(8,128)S(1)}, f32[2,40,8,128]{3,2,1,0:T(8,128)S(1)}, u32[]{:S(2)}, u32[]{:S(2)}) collective-permute-start(f32[2,40,8,128]{3,2,1,0:T(8,128)S(1)} %get-tuple-element.29), channel_id=1, source_target_pairs={{0,32},{1,17},{2,34},{3,19},{4,36},{5,21},{6,38},{7,23},{8,40},{9,... | collective-permute-start | bytes 983048 | tf_op jit(solution)/shard_map/ppermute | solution.py:32
  17.5 10.2 %collective-permute-start.2 = (f32[2,40,8,128]{3,2,1,0:T(8,128)S(1)}, f32[2,40,8,128]{3,2,1,0:T(8,128)S(1)}, u32[]{:S(2)}, u32[]{:S(2)}) collective-permute-start(f32[2,40,8,128]{3,2,1,0:T(8,128)S(1)} %get-tuple-element.30), channel_id=1, source_target_pairs={{0,64},{1,129},{2,66},{3,131},{4,68},{5,133},{6,70},{7,135},{8,72}... | collective-permute-start | bytes 983048 | tf_op jit(solution)/shard_map/ppermute | solution.py:32
  19.4 10.9 %collective-permute-start.3 = (f32[2,40,8,128]{3,2,1,0:T(8,128)S(1)}, f32[2,40,8,128]{3,2,1,0:T(8,128)S(1)}, u32[]{:S(2)}, u32[]{:S(2)}) collective-permute-start(f32[2,40,8,128]{3,2,1,0:T(8,128)S(1)} %get-tuple-element.31), channel_id=1, source_target_pairs={{0,96},{1,145},{2,98},{3,147},{4,100},{5,149},{6,102},{7,151},{8,1... | collective-permute-start | bytes 983048 | tf_op jit(solution)/shard_map/ppermute | solution.py:32
  21.5 9.3 %collective-permute-start.5 = (f32[2,40,8,128]{3,2,1,0:T(8,128)S(1)}, f32[2,40,8,128]{3,2,1,0:T(8,128)S(1)}, u32[]{:S(2)}, u32[]{:S(2)}) collective-permute-start(f32[2,40,8,128]{3,2,1,0:T(8,128)S(1)} %get-tuple-element.36), channel_id=1, source_target_pairs={{0,32},{1,17},{2,34},{3,19},{4,36},{5,21},{6,38},{7,23},{8,40},{9,... | collective-permute-start | bytes 983048 | tf_op jit(solution)/shard_map/ppermute | solution.py:32
  21.6 13.2 %collective-permute-start.6 = (f32[2,40,8,128]{3,2,1,0:T(8,128)S(1)}, f32[2,40,8,128]{3,2,1,0:T(8,128)S(1)}, u32[]{:S(2)}, u32[]{:S(2)}) collective-permute-start(f32[2,40,8,128]{3,2,1,0:T(8,128)S(1)} %get-tuple-element.37), channel_id=1, source_target_pairs={{0,64},{1,129},{2,66},{3,131},{4,68},{5,133},{6,70},{7,135},{8,72}... | collective-permute-start | bytes 983048 | tf_op jit(solution)/shard_map/ppermute | solution.py:32
  23.7 13.7 %collective-permute-start.7 = (f32[2,40,8,128]{3,2,1,0:T(8,128)S(1)}, f32[2,40,8,128]{3,2,1,0:T(8,128)S(1)}, u32[]{:S(2)}, u32[]{:S(2)}) collective-permute-start(f32[2,40,8,128]{3,2,1,0:T(8,128)S(1)} %get-tuple-element.38), channel_id=1, source_target_pairs={{0,96},{1,145},{2,98},{3,147},{4,100},{5,149},{6,102},{7,151},{8,1... | collective-permute-start | bytes 983048 | tf_op jit(solution)/shard_map/ppermute | solution.py:32
  37.5 4.3 %collective-permute-start.8 = (f32[40,8,128]{2,1,0:T(8,128)S(1)}, f32[40,8,128]{2,1,0:T(8,128)S(1)}, u32[]{:S(2)}, u32[]{:S(2)}) collective-permute-start(f32[40,8,128]{2,1,0:T(8,128)S(1)} %get-tuple-element.40), channel_id=1, source_target_pairs={{0,16},{1,33},{2,18},{3,35},{4,20},{5,37},{6,22},{7,39},{8,24},{9,... | collective-permute-start | bytes 491528 | tf_op jit(solution)/shard_map/ppermute | solution.py:32
  38.6 7.5 %collective-permute-start.9 = (f32[40,8,128]{2,1,0:T(8,128)S(1)}, f32[40,8,128]{2,1,0:T(8,128)S(1)}, u32[]{:S(2)}, u32[]{:S(2)}) collective-permute-start(f32[40,8,128]{2,1,0:T(8,128)S(1)} %get-tuple-element.41), channel_id=1, source_target_pairs={{0,128},{1,65},{2,130},{3,67},{4,132},{5,69},{6,134},{7,71},{8,136... | collective-permute-start | bytes 491528 | tf_op jit(solution)/shard_map/ppermute | solution.py:32
  41.5 6.5 %collective-permute-start.10 = (f32[40,8,128]{2,1,0:T(8,128)S(1)}, f32[40,8,128]{2,1,0:T(8,128)S(1)}, u32[]{:S(2)}, u32[]{:S(2)}) collective-permute-start(f32[40,8,128]{2,1,0:T(8,128)S(1)} %get-tuple-element.42), channel_id=1, source_target_pairs={{0,144},{1,97},{2,146},{3,99},{4,148},{5,101},{6,150},{7,103},{8,1... | collective-permute-start | bytes 491528 | tf_op jit(solution)/shard_map/ppermute | solution.py:32
  48.1 7.9 %collective-permute-start.11 = (f32[10,8,128]{2,1,0:T(8,128)S(1)}, f32[10,8,128]{2,1,0:T(8,128)S(1)}, u32[]{:S(2)}, u32[]{:S(2)}) collective-permute-start(f32[10,8,128]{2,1,0:T(8,128)S(1)} %get-tuple-element.44), channel_id=1, source_target_pairs={{0,4},{1,5},{2,6},{3,7},{4,0},{5,1},{6,2},{7,3},{8,12},{9,13},{10,... | collective-permute-start | bytes 122888 | tf_op jit(solution)/shard_map/ppermute | solution.py:32
  50.4 7.4 %collective-permute-start.12 = (f32[10,8,128]{2,1,0:T(8,128)S(1)}, f32[10,8,128]{2,1,0:T(8,128)S(1)}, u32[]{:S(2)}, u32[]{:S(2)}) collective-permute-start(f32[10,8,128]{2,1,0:T(8,128)S(1)} %get-tuple-element.45), channel_id=1, source_target_pairs={{0,8},{1,9},{2,10},{3,11},{4,12},{5,13},{6,14},{7,15},{8,0},{9,1},... | collective-permute-start | bytes 122888 | tf_op jit(solution)/shard_map/ppermute | solution.py:32
  56.0 5.3 %collective-permute-start.13 = (f32[10,8,128]{2,1,0:T(8,128)S(1)}, f32[10,8,128]{2,1,0:T(8,128)S(1)}, u32[]{:S(2)}, u32[]{:S(2)}) collective-permute-start(f32[10,8,128]{2,1,0:T(8,128)S(1)} %get-tuple-element.46), channel_id=1, source_target_pairs={{0,12},{1,13},{2,14},{3,15},{4,8},{5,9},{6,10},{7,11},{8,4},{9,5},... | collective-permute-start | bytes 122888 | tf_op jit(solution)/shard_map/ppermute | solution.py:32
  61.3 3.2 %collective-permute-start.14 = (f32[10,8,128]{2,1,0:T(8,128)S(1)}, f32[10,8,128]{2,1,0:T(8,128)S(1)}, u32[]{:S(2)}, u32[]{:S(2)}) collective-permute-start(f32[10,8,128]{2,1,0:T(8,128)S(1)} %add_add_fusion), channel_id=1, source_target_pairs={{0,2},{1,3},{2,0},{3,1},{4,6},{5,7},{6,4},{7,5},{8,10},{9,11},{10,... | collective-permute-start | bytes 122888 | tf_op jit(solution)/shard_map/ppermute | solution.py:32
  64.5 5.7 %collective-permute-start.17 = (f32[10,8,128]{2,1,0:T(8,128)S(1)}, f32[10,8,128]{2,1,0:T(8,128)S(1)}, u32[]{:S(2)}, u32[]{:S(2)}) collective-permute-start(f32[10,8,128]{2,1,0:T(8,128)S(1)} %add.15), channel_id=1, source_target_pairs={{0,12},{1,13},{2,14},{3,15},{4,8},{5,9},{6,10},{7,11},{8,4},{9,5},... | collective-permute-start | bytes 122888 | tf_op jit(solution)/shard_map/ppermute | solution.py:32
  65.9 6.8 %collective-permute-start.16 = (f32[10,8,128]{2,1,0:T(8,128)S(1)}, f32[10,8,128]{2,1,0:T(8,128)S(1)}, u32[]{:S(2)}, u32[]{:S(2)}) collective-permute-start(f32[10,8,128]{2,1,0:T(8,128)S(1)} %add.15), channel_id=1, source_target_pairs={{0,8},{1,9},{2,10},{3,11},{4,12},{5,13},{6,14},{7,15},{8,0},{9,1},... | collective-permute-start | bytes 122888 | tf_op jit(solution)/shard_map/ppermute | solution.py:32
  69.1 3.8 %collective-permute-start.15 = (f32[10,8,128]{2,1,0:T(8,128)S(1)}, f32[10,8,128]{2,1,0:T(8,128)S(1)}, u32[]{:S(2)}, u32[]{:S(2)}) collective-permute-start(f32[10,8,128]{2,1,0:T(8,128)S(1)} %add.15), channel_id=1, source_target_pairs={{0,4},{1,5},{2,6},{3,7},{4,0},{5,1},{6,2},{7,3},{8,12},{9,13},{10,... | collective-permute-start | bytes 122888 | tf_op jit(solution)/shard_map/ppermute | solution.py:32
  72.9 7.9 %collective-permute-start.18 = (f32[40,8,128]{2,1,0:T(8,128)S(1)}, f32[40,8,128]{2,1,0:T(8,128)S(1)}, u32[]{:S(2)}, u32[]{:S(2)}) collective-permute-start(f32[40,8,128]{2,1,0:T(8,128)S(1)} %pad_maximum_fusion.mine), channel_id=1, source_target_pairs={{0,16},{1,17},{2,18},{3,19},{4,20},{5,21},{6,22},{7,23},{8,24},{9,... | collective-permute-start | bytes 491528 | tf_op jit(solution)/shard_map/ppermute | solution.py:32
  73.0 13.0 %collective-permute-start.19 = (f32[40,8,128]{2,1,0:T(8,128)S(1)}, f32[40,8,128]{2,1,0:T(8,128)S(1)}, u32[]{:S(2)}, u32[]{:S(2)}) collective-permute-start(f32[40,8,128]{2,1,0:T(8,128)S(1)} %pad_maximum_fusion.mine), channel_id=1, source_target_pairs={{0,1},{1,0},{2,3},{3,2},{4,5},{5,4},{6,7},{7,6},{8,9},{9,8},{10,11... | collective-permute-start | bytes 491528 | tf_op jit(solution)/shard_map/ppermute | solution.py:32
  80.8 6.2 %collective-permute-start.20 = (f32[40,8,128]{2,1,0:T(8,128)S(1)}, f32[40,8,128]{2,1,0:T(8,128)S(1)}, u32[]{:S(2)}, u32[]{:S(2)}) collective-permute-start(f32[40,8,128]{2,1,0:T(8,128)S(1)} %collective-permute-done.18.beside), channel_id=1, source_target_pairs={{0,1},{1,0},{2,3},{3,2},{4,5},{5,4},{6,7},{7,6},{8,9},{9,8},{10,11... | collective-permute-start | bytes 491528 | tf_op jit(solution)/shard_map/ppermute | solution.py:32

commit v4 on v3

--- a/solution.py
+++ b/solution.py
@@ -8,7 +8,7 @@
 
 FINE = ("x_hi", "y", "x_lo", "z", "core")
 SIZES = (2, 4, 2, 8, 2)
-HALF_GROUPS, WIDE, UNIT, PIECE = 25, 3, 40, 10
+HALF_GROUPS, WIDE, UNIT = 25, 3, 40
 FULL = HALF_GROUPS * WIDE
 
 
@@ -40,10 +40,6 @@
     return (0, (y ^ step) - y, 0, 0) if core == turn else ((x ^ step) - x, 0, 0, 0)
 
 
-def along(step, x, y, z, core):
-    return 0, 0, (z ^ step) - z, 0
-
-
 def block_of(place):
     run, y = place // 4, place % 4
     return (y // 2 ^ run) * 4 + y
@@ -60,7 +56,6 @@
     x = lax.axis_index("x_hi") * 2 + x_low
     y = lax.axis_index("y")
     core = lax.axis_index("core")
-    starts = [(lax.axis_index("z") // 2 ^ q) * PIECE for q in range(4)]
 
     def arrivals(place, o, act):
         block = block_of(place)
@@ -119,7 +114,7 @@
                 k = jnp.where(half == 0, dy, dx)
                 j = jnp.where(half == 0, low ^ x_low, dy & 1)
                 for n in range(UNIT):
-                    target[k, j, starts[n // PIECE] + n % PIECE] = tile_of(acc, half, low * UNIT + n)
+                    target[k, j, n] = tile_of(acc, half, low * UNIT + n)
 
         return carry
 
@@ -174,9 +169,17 @@
     )(*(pltpu.with_memory_space_constraint(array, pltpu.VMEM) for array in arrays))
 
 
-def add_halves(keep, got, *sums):
-    for k, out in enumerate(sums):
-        out[...] = keep[k] + got[k]
+def add_halves(keep, got, send_a, keep_a, send_b, keep_b):
+    for low, out, distances in ((0, send_a, (1, 2)), (0, keep_a, (0, 3)), (1, send_b, (3, 2)), (1, keep_b, (0, 1))):
+        for n, k in enumerate(distances):
+            out[n] = keep[k, low] + got[k, low]
+
+
+def add_first(keep_a, got_a, keep_b, got_b, own_a, send_a, own_b, send_b):
+    own_a[...] = keep_a[0] + got_a[0]
+    send_a[...] = keep_a[1] + got_a[1]
+    own_b[...] = keep_b[0] + got_b[0]
+    send_b[...] = keep_b[1] + got_b[1]
 
 
 def add_ring(*refs):
@@ -187,29 +190,15 @@
         @pl.when(swapped == turn)
         def _():
             for run in range(2):
-                a, b, c, d = arrived[4 * run : 4 * run + 4]
                 for low in range(2):
-                    sums[2 * (run ^ turn) + low][...] = (a[low] + b[low]) + (c[low] + d[low])
-
-
-def add_last(*refs):
-    a, b, c, d = refs[:4]
-    for r, out in enumerate(refs[4:]):
-        part = slice(r * PIECE, (r + 1) * PIECE)
-        out[...] = (a[part] + b[part]) + (c[part] + d[part])
-
-
-def layout_kernel(scale, mine, beside, other, other_beside, out, whole):
-    low, core = lax.axis_index("x_lo"), lax.axis_index("core")
-    away = lax.axis_index("z") // 2
-    for ref, u in (
-        (mine, core * 2 + low),
-        (beside, core * 2 + 1 - low),
-        (other, (1 - core) * 2 + low),
-        (other_beside, (1 - core) * 2 + 1 - low),
-    ):
-        for r in range(4):
-            whole[pl.ds(u * UNIT + (away ^ r) * PIECE, PIECE)] = ref[r * PIECE : (r + 1) * PIECE] * scale
+                    own, got = arrived[4 * run + 2 * low : 4 * run + 2 * low + 2]
+                    sums[2 * (run ^ turn) + low][...] = own[...] + got[...]
+
+
+def layout_kernel(scale, mine, other, out, whole):
+    core = lax.axis_index("core")
+    whole[pl.ds(core * 2 * UNIT, 2 * UNIT)] = mine[...] * scale
+    whole[pl.ds((1 - core) * 2 * UNIT, 2 * UNIT)] = other[...] * scale
     for half in range(2):
         for m in range(FULL):
             g, l = divmod(m, WIDE)
@@ -228,7 +217,7 @@
     return pl.pallas_call(
         functools.partial(layout_kernel, scale),
         out_shape=jax.ShapeDtypeStruct((1, size, size), jnp.float32),
-        in_specs=[pl.BlockSpec(memory_space=pltpu.VMEM)] * 4,
+        in_specs=[pl.BlockSpec(memory_space=pltpu.VMEM)] * 2,
         out_specs=pl.BlockSpec(memory_space=pltpu.VMEM),
         scratch_shapes=[pltpu.VMEM((4 * UNIT, 8, 128), jnp.float32)],
         compiler_params=pltpu.CompilerParams(vmem_limit_bytes=8 << 20),
@@ -244,22 +233,23 @@
     keep, give = densities(1, table, own, blocks)
     runs[1] = (keep, send(give, across))
 
-    unit, piece = (UNIT, 8, 128), (PIECE, 8, 128)
+    unit = (UNIT, 8, 128)
+    begun = []
+    for keep, got in runs:
+        send_a, keep_a, send_b, keep_b = combine(add_halves, [(2, *unit)] * 4, keep, got)
+        begun.append((keep_a, send(send_a, functools.partial(around, 1, 0)), keep_b, send(send_b, functools.partial(around, 3, 0))))
     arrived = []
-    for keep, got in runs:
-        first = combine(add_halves, [(2, *unit)] * 4, keep, got)
-        arrived += [first[0]] + [send(first[k], functools.partial(around, k, 0)) for k in (1, 2, 3)]
+    for halves in begun:
+        own_a, send_a, own_b, send_b = combine(add_first, [unit] * 4, *halves)
+        arrived += [own_a, send(send_a, functools.partial(around, 3, 0)), own_b, send(send_b, functools.partial(around, 1, 0))]
     second = combine(add_ring, [unit] * 4, *arrived)
     came = [send(second[j], functools.partial(around, j, 1)) for j in (1, 2, 3)]
-    third = combine(add_last, [piece] * 4, second[0], *came)
-    came = [send(third[r], functools.partial(along, 2 * r)) for r in (1, 2, 3)]
-    fourth = (third[0] + came[0]) + (came[1] + came[2])
-    fifth = fourth + send(fourth, functools.partial(along, 1))
-    mine = jnp.concatenate([fifth] + [send(fifth, functools.partial(along, 2 * r)) for r in (1, 2, 3)])
-    beside = send(mine, lambda x, y, z, core: (1 - 2 * (x % 2), 0, 0, 0))
-    other = send(mine, across)
-    other_beside = send(beside, across)
-    return lay_out(scale, amps.shape[4], mine, beside, other, other_beside)
+    third = (second[0] + came[0]) + (came[1] + came[2])
+    parts = lax.all_to_all(third.reshape(8, UNIT // 8, 8, 128), "z", 0, 0, tiled=True)
+    eighth = jnp.sum(parts, axis=0, keepdims=True)
+    mine = lax.all_to_all(jnp.broadcast_to(eighth, (16, *parts.shape[1:])), ("x_lo", "z"), 0, 0, tiled=True)
+    mine = mine.reshape(2 * UNIT, 8, 128)
+    return lay_out(scale, amps.shape[4], mine, send(mine, across))
 
 
 def solution(mesh):

time: 88.1 us -> 81.5 us (0.925)
  blocking collectives: 0 us -> 27.5 us
  starting transfers between devices: 42.2 us -> 20.3 us
  waiting for transfers between devices: 30.4 us -> 18.4 us
    all_to_all x0 -> x2, blocking collectives: none -> 27.5 us  [the longest x1 16.7 us: on_device(): lax.all_to_all(third.reshape(8, UNIT // 8, 8, 128), 'z', 0, 0, tiled=True)]
    ppermute x21 -> x14, starting transfers between devices: 42.2 us -> 20.3 us  [send(): return lax.ppermute(value, FINE, pairs(move))]
    ppermute x21 -> x14, waiting for transfers between devices: 30.4 us -> 18.4 us  [send(): return lax.ppermute(value, FINE, pairs(move))]
  transfers between devices with their start and end apart: 21 -> 14, of which waited for: 15 -> 11; matrix products, arithmetic and copies ran while one was open for 0% -> 0% of each run, Pallas kernels for 7% -> 7%
where the time goes in v4:
time: 81.5 us; the launch traced here: 81.8 us
  blocking collectives  27.5 us (34%)
  starting transfers between devices  20.3 us (25%)
  waiting for transfers between devices  18.4 us (23%)
  Pallas kernels  14.7 us (18%)
    ppermute x14, starting transfers between devices, send(): return lax.ppermute(value, FINE, pairs(move))  20.3 us
    ppermute x14, waiting for transfers between devices, send(): return lax.ppermute(value, FINE, pairs(move))  18.4 us
    all_to_all x1, blocking collectives, on_device(): lax.all_to_all(third.reshape(8, UNIT // 8, 8, 128), 'z', 0, 0, tiled=True)  16.7 us
    all_to_all x1, blocking collectives, on_device(): lax.all_to_all(jnp.broadcast_to(eighth, (16, *parts.shape[1:])), ('x_lo',...  10.8 us
    pallas_call x1, Pallas kernels, densities(): pl.pallas_call(functools.partial(density_kernel, 0), out_shape=(pltpu.VME...  7.62 us
    pallas_call x1, Pallas kernels, densities(): pl.pallas_call(later, out_shape=(half, half), in_specs=[pl.BlockSpec(memo...  5.57 us
  transfers between devices with their start and end apart: 14, of which 11 were waited for; matrix products, arithmetic and copies ran while one was open for 0% of the time, Pallas kernels for 7%

profile of v4, /device:TPU:1, one launch (start us, length us, event | category | flops | bytes accessed | tf_op | source)
XLA Modules:
  0.0 81.8 jit_solution(15962881857940460060)
XLA Ops:
  0.0 0.7 copy-done
  0.7 7.6 %densities.2 = (bf16[8,4,400,400]{3,2,1,0:T(8,128)(2,1)S(1)}, f32[4,2,40,8,128]{4,3,2,1,0:T(8,128)S(1)}, f32[4,2,40,8,128]{4,3,2,1,0:T(8,128)S(1)}) custom-call(s32[8]{0:T(128)S(1)} %bitcast.6, bf16[8,4,400,400]{3,2,1,0:T(8,128)(2,1)} %bitcast.9), custom_call_target="tpu_custom_call" | custom-call | flops 4294967296 | bytes 13631488 | tf_op jit(solution)/shard_map/densities/pallas_call | solution.py:138
  8.3 3.3 %collective-permute-start = (f32[4,2,40,8,128]{4,3,2,1,0:T(8,128)S(1)}, f32[4,2,40,8,128]{4,3,2,1,0:T(8,128)S(1)}, u32[]{:S(2)}, u32[]{:S(2)}) collective-permute-start(f32[4,2,40,8,128]{4,3,2,1,0:T(8,128)S(1)} %get-tuple-element.31), channel_id=1, source_target_pairs={{0,1},{1,0},{2,3},{3,2},{4,5},{5,4},{6,7},{7,6},{8,9},{9,8},{10,11... | collective-permute-start | bytes 3932168 | tf_op jit(solution)/shard_map/ppermute | solution.py:32
  11.6 5.6 %densities.3 = (f32[4,2,40,8,128]{4,3,2,1,0:T(8,128)S(1)}, f32[4,2,40,8,128]{4,3,2,1,0:T(8,128)S(1)}) custom-call(s32[8]{0:T(128)S(1)} %bitcast.7, bf16[8,4,400,400]{3,2,1,0:T(8,128)(2,1)S(1)} %get-tuple-element.40.blocks), custom_call_target="tpu_custom_call" | custom-call | flops 4294967296 | bytes 13631488 | tf_op jit(solution)/shard_map/densities/pallas_call | solution.py:150
  17.2 0.1 collective-permute-start.5
  17.3 0.1 add_halves.2
  17.4 0.1 collective-permute-start.1
  17.5 1.3 %collective-permute-start.2 = (f32[2,40,8,128]{3,2,1,0:T(8,128)S(1)}, f32[2,40,8,128]{3,2,1,0:T(8,128)S(1)}, u32[]{:S(2)}, u32[]{:S(2)}) collective-permute-start(f32[2,40,8,128]{3,2,1,0:T(8,128)S(1)} %get-tuple-element.35), channel_id=1, source_target_pairs={{0,96},{1,145},{2,98},{3,147},{4,100},{5,149},{6,102},{7,151},{8,1... | collective-permute-start | bytes 983048 | tf_op jit(solution)/shard_map/ppermute | solution.py:32
  18.8 1.5 %collective-permute-done.5.got = f32[4,2,40,8,128]{4,3,2,1,0:T(8,128)S(1)} collective-permute-done((f32[4,2,40,8,128]{4,3,2,1,0:T(8,128)S(1)}, f32[4,2,40,8,128]{4,3,2,1,0:T(8,128)S(1)}, u32[]{:S(2)}, u32[]{:S(2)}) %collective-permute-start.5) | collective-permute-done | bytes 1310752 | tf_op jit(solution)/shard_map/ppermute | solution.py:32
  20.3 0.1 add_halves.3
  20.4 0.1 collective-permute-start.6
  20.5 1.3 %collective-permute-start.7 = (f32[2,40,8,128]{3,2,1,0:T(8,128)S(1)}, f32[2,40,8,128]{3,2,1,0:T(8,128)S(1)}, u32[]{:S(2)}, u32[]{:S(2)}) collective-permute-start(f32[2,40,8,128]{3,2,1,0:T(8,128)S(1)} %get-tuple-element.46), channel_id=1, source_target_pairs={{0,96},{1,145},{2,98},{3,147},{4,100},{5,149},{6,102},{7,151},{8,1... | collective-permute-start | bytes 983048 | tf_op jit(solution)/shard_map/ppermute | solution.py:32
  21.8 1.9 %collective-permute-done.1.got_a = f32[2,40,8,128]{3,2,1,0:T(8,128)S(1)} collective-permute-done((f32[2,40,8,128]{3,2,1,0:T(8,128)S(1)}, f32[2,40,8,128]{3,2,1,0:T(8,128)S(1)}, u32[]{:S(2)}, u32[]{:S(2)}) %collective-permute-start.1) | collective-permute-done | bytes 327712 | tf_op jit(solution)/shard_map/ppermute | solution.py:32
  23.7 1.3 %collective-permute-done.2.got_b = f32[2,40,8,128]{3,2,1,0:T(8,128)S(1)} collective-permute-done((f32[2,40,8,128]{3,2,1,0:T(8,128)S(1)}, f32[2,40,8,128]{3,2,1,0:T(8,128)S(1)}, u32[]{:S(2)}, u32[]{:S(2)}) %collective-permute-start.2) | collective-permute-done | bytes 327712 | tf_op jit(solution)/shard_map/ppermute | solution.py:32
  25.1 1.3 %collective-permute-start.3 = (f32[40,8,128]{2,1,0:T(8,128)S(1)}, f32[40,8,128]{2,1,0:T(8,128)S(1)}, u32[]{:S(2)}, u32[]{:S(2)}) collective-permute-start(f32[40,8,128]{2,1,0:T(8,128)S(1)} %get-tuple-element.37), channel_id=1, source_target_pairs={{0,96},{1,145},{2,98},{3,147},{4,100},{5,149},{6,102},{7,151},{8,1... | collective-permute-start | bytes 491528 | tf_op jit(solution)/shard_map/ppermute | solution.py:32
  26.4 0.8 %collective-permute-done.6.got_a = f32[2,40,8,128]{3,2,1,0:T(8,128)S(1)} collective-permute-done((f32[2,40,8,128]{3,2,1,0:T(8,128)S(1)}, f32[2,40,8,128]{3,2,1,0:T(8,128)S(1)}, u32[]{:S(2)}, u32[]{:S(2)}) %collective-permute-start.6) | collective-permute-done | bytes 327712 | tf_op jit(solution)/shard_map/ppermute | solution.py:32
  27.2 1.3 %collective-permute-done.7.got_b = f32[2,40,8,128]{3,2,1,0:T(8,128)S(1)} collective-permute-done((f32[2,40,8,128]{3,2,1,0:T(8,128)S(1)}, f32[2,40,8,128]{3,2,1,0:T(8,128)S(1)}, u32[]{:S(2)}, u32[]{:S(2)}) %collective-permute-start.7) | collective-permute-done | bytes 327712 | tf_op jit(solution)/shard_map/ppermute | solution.py:32
  28.6 1.3 %collective-permute-start.8 = (f32[40,8,128]{2,1,0:T(8,128)S(1)}, f32[40,8,128]{2,1,0:T(8,128)S(1)}, u32[]{:S(2)}, u32[]{:S(2)}) collective-permute-start(f32[40,8,128]{2,1,0:T(8,128)S(1)} %get-tuple-element.48), channel_id=1, source_target_pairs={{0,96},{1,145},{2,98},{3,147},{4,100},{5,149},{6,102},{7,151},{8,1... | collective-permute-start | bytes 491528 | tf_op jit(solution)/shard_map/ppermute | solution.py:32
  29.9 0.7 collective-permute-done.3.refs_1_
  30.6 3.5 %collective-permute-done.8.refs_5_ = f32[40,8,128]{2,1,0:T(8,128)S(1)} collective-permute-done((f32[40,8,128]{2,1,0:T(8,128)S(1)}, f32[40,8,128]{2,1,0:T(8,128)S(1)}, u32[]{:S(2)}, u32[]{:S(2)}) %collective-permute-start.8) | collective-permute-done | bytes 163872 | tf_op jit(solution)/shard_map/ppermute | solution.py:32
  34.1 0.1 add_ring.1
  34.2 1.4 %collective-permute-start.10 = (f32[40,8,128]{2,1,0:T(8,128)S(1)}, f32[40,8,128]{2,1,0:T(8,128)S(1)}, u32[]{:S(2)}, u32[]{:S(2)}) collective-permute-start(f32[40,8,128]{2,1,0:T(8,128)S(1)} %get-tuple-element.52), channel_id=1, source_target_pairs={{0,16},{1,33},{2,18},{3,35},{4,20},{5,37},{6,22},{7,39},{8,24},{9,... | collective-permute-start | bytes 491528 | tf_op jit(solution)/shard_map/ppermute | solution.py:32
  35.5 2.5 %collective-permute-start.11 = (f32[40,8,128]{2,1,0:T(8,128)S(1)}, f32[40,8,128]{2,1,0:T(8,128)S(1)}, u32[]{:S(2)}, u32[]{:S(2)}) collective-permute-start(f32[40,8,128]{2,1,0:T(8,128)S(1)} %get-tuple-element.53), channel_id=1, source_target_pairs={{0,128},{1,65},{2,130},{3,67},{4,132},{5,69},{6,134},{7,71},{8,136... | collective-permute-start | bytes 491528 | tf_op jit(solution)/shard_map/ppermute | solution.py:32
  38.0 0.1 collective-permute-start.12
  38.1 0.3 collective-permute-done.10
  38.4 4.1 %collective-permute-done.11 = f32[40,8,128]{2,1,0:T(8,128)S(1)} collective-permute-done((f32[40,8,128]{2,1,0:T(8,128)S(1)}, f32[40,8,128]{2,1,0:T(8,128)S(1)}, u32[]{:S(2)}, u32[]{:S(2)}) %collective-permute-start.11) | collective-permute-done | bytes 163872 | tf_op jit(solution)/shard_map/ppermute | solution.py:32
  42.5 1.7 %collective-permute-done.12 = f32[40,8,128]{2,1,0:T(8,128)S(1)} collective-permute-done((f32[40,8,128]{2,1,0:T(8,128)S(1)}, f32[40,8,128]{2,1,0:T(8,128)S(1)}, u32[]{:S(2)}, u32[]{:S(2)}) %collective-permute-start.12) | collective-permute-done | bytes 163872 | tf_op jit(solution)/shard_map/ppermute | solution.py:32
  44.2 16.7 %all_to_all.10 = f32[8,5,8,128]{3,2,1,0:T(8,128)S(1)} all-to-all(f32[8,5,8,128]{3,2,1,0:T(8,128)S(1)} %bitcast.8), channel_id=1, replica_groups=mesh['x_hi'=2,'y'=4,'x_lo'=2,'z'=8,'core'=2] {'z'}, dimensions={0} | all-to-all | bytes 327680 | tf_op jit(solution)/shard_map/all_to_all | solution.py:248
  61.0 10.8 %all_to_all.11 = f32[16,5,8,128]{3,2,1,0:T(8,128)S(1)} all-to-all(f32[16,5,8,128]{3,2,1,0:T(8,128)S(1)} %broadcast_in_dim.2), channel_id=1, replica_groups=mesh['x_hi'=2,'y'=4,'x_lo'=2,'z'=8,'core'=2] {'x_lo','z'}, dimensions={0} | all-to-all | bytes 655360 | tf_op jit(solution)/shard_map/all_to_all | solution.py:250
  71.8 7.7 %collective-permute-start.13 = (f32[80,8,128]{2,1,0:T(8,128)S(1)}, f32[80,8,128]{2,1,0:T(8,128)S(1)}, u32[]{:S(2)}, u32[]{:S(2)}) collective-permute-start(f32[80,8,128]{2,1,0:T(8,128)S(1)} %bitcast.4), channel_id=1, source_target_pairs={{0,1},{1,0},{2,3},{3,2},{4,5},{5,4},{6,7},{7,6},{8,9},{9,8},{10,11... | collective-permute-start | bytes 983048 | tf_op jit(solution)/shard_map/ppermute | solution.py:32
  79.5 1.3 %collective-permute-done.13.other = f32[80,8,128]{2,1,0:T(8,128)S(1)} collective-permute-done((f32[80,8,128]{2,1,0:T(8,128)S(1)}, f32[80,8,128]{2,1,0:T(8,128)S(1)}, u32[]{:S(2)}, u32[]{:S(2)}) %collective-permute-start.13) | collective-permute-done | bytes 327712 | tf_op jit(solution)/shard_map/ppermute | solution.py:32
  80.7 1.0 %lay_out.1 = f32[1,400,400]{2,1,0:T(8,128)} custom-call(f32[80,8,128]{2,1,0:T(8,128)S(1)} %bitcast.5, f32[80,8,128]{2,1,0:T(8,128)S(1)} %collective-permute-done.13.other), custom_call_target="tpu_custom_call" | custom-call | tf_op jit(solution)/shard_map/lay_out/pallas_call | solution.py:217
  (11 shorter events, 0.2 us)
Async XLA Ops:
  0.0 0.7 copy-start
  8.3 9.0 %collective-permute-start = (f32[4,2,40,8,128]{4,3,2,1,0:T(8,128)S(1)}, f32[4,2,40,8,128]{4,3,2,1,0:T(8,128)S(1)}, u32[]{:S(2)}, u32[]{:S(2)}) collective-permute-start(f32[4,2,40,8,128]{4,3,2,1,0:T(8,128)S(1)} %get-tuple-element.31), channel_id=1, source_target_pairs={{0,1},{1,0},{2,3},{3,2},{4,5},{5,4},{6,7},{7,6},{8,9},{9,8},{10,11... | collective-permute-start | bytes 3932168 | tf_op jit(solution)/shard_map/ppermute | solution.py:32
  17.2 3.1 %collective-permute-start.5 = (f32[4,2,40,8,128]{4,3,2,1,0:T(8,128)S(1)}, f32[4,2,40,8,128]{4,3,2,1,0:T(8,128)S(1)}, u32[]{:S(2)}, u32[]{:S(2)}) collective-permute-start(f32[4,2,40,8,128]{4,3,2,1,0:T(8,128)S(1)} %get-tuple-element.42), channel_id=1, source_target_pairs={{0,1},{1,0},{2,3},{3,2},{4,5},{5,4},{6,7},{7,6},{8,9},{9,8},{10,11... | collective-permute-start | bytes 3932168 | tf_op jit(solution)/shard_map/ppermute | solution.py:32
  17.4 6.3 %collective-permute-start.1 = (f32[2,40,8,128]{3,2,1,0:T(8,128)S(1)}, f32[2,40,8,128]{3,2,1,0:T(8,128)S(1)}, u32[]{:S(2)}, u32[]{:S(2)}) collective-permute-start(f32[2,40,8,128]{3,2,1,0:T(8,128)S(1)} %get-tuple-element.33), channel_id=1, source_target_pairs={{0,32},{1,17},{2,34},{3,19},{4,36},{5,21},{6,38},{7,23},{8,40},{9,... | collective-permute-start | bytes 983048 | tf_op jit(solution)/shard_map/ppermute | solution.py:32
  17.5 7.5 %collective-permute-start.2 = (f32[2,40,8,128]{3,2,1,0:T(8,128)S(1)}, f32[2,40,8,128]{3,2,1,0:T(8,128)S(1)}, u32[]{:S(2)}, u32[]{:S(2)}) collective-permute-start(f32[2,40,8,128]{3,2,1,0:T(8,128)S(1)} %get-tuple-element.35), channel_id=1, source_target_pairs={{0,96},{1,145},{2,98},{3,147},{4,100},{5,149},{6,102},{7,151},{8,1... | collective-permute-start | bytes 983048 | tf_op jit(solution)/shard_map/ppermute | solution.py:32
  20.4 6.8 %collective-permute-start.6 = (f32[2,40,8,128]{3,2,1,0:T(8,128)S(1)}, f32[2,40,8,128]{3,2,1,0:T(8,128)S(1)}, u32[]{:S(2)}, u32[]{:S(2)}) collective-permute-start(f32[2,40,8,128]{3,2,1,0:T(8,128)S(1)} %get-tuple-element.44), channel_id=1, source_target_pairs={{0,32},{1,17},{2,34},{3,19},{4,36},{5,21},{6,38},{7,23},{8,40},{9,... | collective-permute-start | bytes 983048 | tf_op jit(solution)/shard_map/ppermute | solution.py:32
  20.5 8.0 %collective-permute-start.7 = (f32[2,40,8,128]{3,2,1,0:T(8,128)S(1)}, f32[2,40,8,128]{3,2,1,0:T(8,128)S(1)}, u32[]{:S(2)}, u32[]{:S(2)}) collective-permute-start(f32[2,40,8,128]{3,2,1,0:T(8,128)S(1)} %get-tuple-element.46), channel_id=1, source_target_pairs={{0,96},{1,145},{2,98},{3,147},{4,100},{5,149},{6,102},{7,151},{8,1... | collective-permute-start | bytes 983048 | tf_op jit(solution)/shard_map/ppermute | solution.py:32
  25.1 5.5 %collective-permute-start.3 = (f32[40,8,128]{2,1,0:T(8,128)S(1)}, f32[40,8,128]{2,1,0:T(8,128)S(1)}, u32[]{:S(2)}, u32[]{:S(2)}) collective-permute-start(f32[40,8,128]{2,1,0:T(8,128)S(1)} %get-tuple-element.37), channel_id=1, source_target_pairs={{0,96},{1,145},{2,98},{3,147},{4,100},{5,149},{6,102},{7,151},{8,1... | collective-permute-start | bytes 491528 | tf_op jit(solution)/shard_map/ppermute | solution.py:32
  26.4 4.2 %collective-permute-start.4 = (f32[40,8,128]{2,1,0:T(8,128)S(1)}, f32[40,8,128]{2,1,0:T(8,128)S(1)}, u32[]{:S(2)}, u32[]{:S(2)}) collective-permute-start(f32[40,8,128]{2,1,0:T(8,128)S(1)} %get-tuple-element.39), channel_id=1, source_target_pairs={{0,32},{1,17},{2,34},{3,19},{4,36},{5,21},{6,38},{7,23},{8,40},{9,... | collective-permute-start | bytes 491528 | tf_op jit(solution)/shard_map/ppermute | solution.py:32
  28.6 5.5 %collective-permute-start.8 = (f32[40,8,128]{2,1,0:T(8,128)S(1)}, f32[40,8,128]{2,1,0:T(8,128)S(1)}, u32[]{:S(2)}, u32[]{:S(2)}) collective-permute-start(f32[40,8,128]{2,1,0:T(8,128)S(1)} %get-tuple-element.48), channel_id=1, source_target_pairs={{0,96},{1,145},{2,98},{3,147},{4,100},{5,149},{6,102},{7,151},{8,1... | collective-permute-start | bytes 491528 | tf_op jit(solution)/shard_map/ppermute | solution.py:32
  29.9 4.2 %collective-permute-start.9 = (f32[40,8,128]{2,1,0:T(8,128)S(1)}, f32[40,8,128]{2,1,0:T(8,128)S(1)}, u32[]{:S(2)}, u32[]{:S(2)}) collective-permute-start(f32[40,8,128]{2,1,0:T(8,128)S(1)} %get-tuple-element.50), channel_id=1, source_target_pairs={{0,32},{1,17},{2,34},{3,19},{4,36},{5,21},{6,38},{7,23},{8,40},{9,... | collective-permute-start | bytes 491528 | tf_op jit(solution)/shard_map/ppermute | solution.py:32
  34.2 4.3 %collective-permute-start.10 = (f32[40,8,128]{2,1,0:T(8,128)S(1)}, f32[40,8,128]{2,1,0:T(8,128)S(1)}, u32[]{:S(2)}, u32[]{:S(2)}) collective-permute-start(f32[40,8,128]{2,1,0:T(8,128)S(1)} %get-tuple-element.52), channel_id=1, source_target_pairs={{0,16},{1,33},{2,18},{3,35},{4,20},{5,37},{6,22},{7,39},{8,24},{9,... | collective-permute-start | bytes 491528 | tf_op jit(solution)/shard_map/ppermute | solution.py:32
  35.5 7.0 %collective-permute-start.11 = (f32[40,8,128]{2,1,0:T(8,128)S(1)}, f32[40,8,128]{2,1,0:T(8,128)S(1)}, u32[]{:S(2)}, u32[]{:S(2)}) collective-permute-start(f32[40,8,128]{2,1,0:T(8,128)S(1)} %get-tuple-element.53), channel_id=1, source_target_pairs={{0,128},{1,65},{2,130},{3,67},{4,132},{5,69},{6,134},{7,71},{8,136... | collective-permute-start | bytes 491528 | tf_op jit(solution)/shard_map/ppermute | solution.py:32
  38.0 6.2 %collective-permute-start.12 = (f32[40,8,128]{2,1,0:T(8,128)S(1)}, f32[40,8,128]{2,1,0:T(8,128)S(1)}, u32[]{:S(2)}, u32[]{:S(2)}) collective-permute-start(f32[40,8,128]{2,1,0:T(8,128)S(1)} %get-tuple-element.54), channel_id=1, source_target_pairs={{0,144},{1,97},{2,146},{3,99},{4,148},{5,101},{6,150},{7,103},{8,1... | collective-permute-start | bytes 491528 | tf_op jit(solution)/shard_map/ppermute | solution.py:32
  71.8 8.9 %collective-permute-start.13 = (f32[80,8,128]{2,1,0:T(8,128)S(1)}, f32[80,8,128]{2,1,0:T(8,128)S(1)}, u32[]{:S(2)}, u32[]{:S(2)}) collective-permute-start(f32[80,8,128]{2,1,0:T(8,128)S(1)} %bitcast.4), channel_id=1, source_target_pairs={{0,1},{1,0},{2,3},{3,2},{4,5},{5,4},{6,7},{7,6},{8,9},{9,8},{10,11... | collective-permute-start | bytes 983048 | tf_op jit(solution)/shard_map/ppermute | solution.py:32

commit v5 on v4

v5 whole, which is shorter than its diff:
```python
import functools
import jax
import jax.numpy as jnp
from jax import lax
from jax.experimental import pallas as pl
from jax.experimental.pallas import tpu as pltpu
from jax.sharding import Mesh, PartitionSpec as P

FINE = ("x_hi", "y", "x_lo", "z", "core")
SIZES = (2, 4, 2, 8, 2)
HALF_GROUPS, WIDE, UNIT = 25, 3, 40
FULL = HALF_GROUPS * WIDE


def position(x, y, z, core):
    x, y, z, core = x % 4, y % 4, z % 8, core % 2
    return (((x // 2 * 4 + y) * 2 + x % 2) * 8 + z) * 2 + core


def pairs(move):
    found = []
    for x in range(4):
        for y in range(4):
            for z in range(8):
                for core in range(2):
                    dx, dy, dz, dc = move(x, y, z, core)
                    found.append((position(x, y, z, core), position(x + dx, y + dy, z + dz, core + dc)))
    return found


def send(value, move):
    return lax.ppermute(value, FINE, pairs(move))


def across(x, y, z, core):
    return 0, 0, 0, 1


def around(step, turn, x, y, z, core):
    return (0, (y ^ step) - y, 0, 0) if core == turn else ((x ^ step) - x, 0, 0, 0)


def add_block(blocks, acc, target, block, half, mix):
    x_low = lax.axis_index("x_lo")
    x, y = lax.axis_index("x_hi") * 2 + x_low, lax.axis_index("y")
    rows = pl.ds(pl.multiple_of(half * (8 * HALF_GROUPS - 8), 16), 8 * HALF_GROUPS + 8)
    size = blocks.shape[2]
    total = None
    for o in range(blocks.shape[1]):
        part = jnp.dot(blocks[block, o, rows, :], mix(o), preferred_element_type=jnp.float32)
        total = part if total is None else total + part
    acc[:, :size] = total

    lane = lax.broadcasted_iota(jnp.int32, (8, 128), 1)

    def read(g, l):
        return acc[pl.ds(pl.multiple_of(half * 8 + 8 * g, 8), 8), 128 * l : 128 * l + 128]

    def tile_of(m):
        if m == UNIT * 2 - 1:
            return jnp.zeros((8, 128), jnp.float32)
        if m < FULL:
            return read(*divmod(m, WIDE))
        first = 8 * (m - FULL)
        tile = read(first, WIDE)
        for k in range(1, min(8, HALF_GROUPS - first)):
            tile = jnp.where(lane < 16 * k, tile, pltpu.roll(read(first + k, WIDE), 16 * k, 1))
        return tile

    high, dy = block // 4, (block % 4) ^ y
    for low in range(2):
        dx = (high * 2 + low) ^ x
        k = jnp.where(half == 0, dy, dx)
        j = jnp.where(half == 0, dx, dy)
        for n in range(UNIT):
            target[k, j, n] = tile_of(low * UNIT + n)


def give_kernel(table_in, amps, blocks, mixes, give, acc, table, table_sem, sems):
    pltpu.make_async_copy(amps.at[0], blocks.at[0], sems.at[0]).start()
    copy = pltpu.make_async_copy(table_in, table, table_sem)
    copy.start()
    copy.wait()
    count, orbitals = blocks.shape[:2]
    half = 1 - lax.axis_index("core")

    def arrivals(block, act, own=True):
        partner = table[block]

        @pl.when((partner >= block) & own)
        def _():
            act(pltpu.make_async_copy(amps.at[block], blocks.at[block], sems.at[block]))

        @pl.when(partner > block)
        def _():
            act(pltpu.make_async_copy(amps.at[partner], blocks.at[partner], sems.at[partner]))

    for block in range(count):
        arrivals(block, lambda copy: copy.start(), block > 0)

    def step(pair, carry):
        first = pair * 2
        for block in (first, first + 1):
            arrivals(block, lambda copy: copy.wait())
        for block, own_acc in ((first, acc.at[0]), (first + 1, acc.at[1])):
            partner = table[block]

            def mix(o, block=block, partner=partner):
                turned = blocks[block, o].T
                value = turned + turned - blocks[partner, o]
                mixes[block, o] = value
                return value

            add_block(blocks, own_acc, give, block, half, mix)
        return carry

    lax.fori_loop(0, count // 2, step, 0)


def keep_kernel(blocks, mixes, keep, acc):
    half = lax.axis_index("core")

    def step(group, carry):
        for n in range(4):
            block = group * 4 + n
            add_block(blocks, acc.at[n % 2], keep, block, half, lambda o, block=block: mixes[block, o])
        return carry

    lax.fori_loop(0, blocks.shape[0] // 4, step, 0)


def kernel_params(name):
    return dict(
        compiler_params=pltpu.CompilerParams(vmem_limit_bytes=10 << 20),
        cost_estimate=pl.CostEstimate(flops=4 << 30, bytes_accessed=13 << 20, transcendentals=0),
        name=name,
    )


def give_half(table, amps):
    in_vmem = pl.BlockSpec(memory_space=pltpu.VMEM)
    whole = pltpu.VMEM(amps.shape, amps.dtype)
    return pl.pallas_call(
        give_kernel,
        out_shape=(whole, whole, pltpu.VMEM((4, 4, UNIT, 8, 128), jnp.float32)),
        in_specs=[pl.BlockSpec(memory_space=pltpu.HBM)] * 2,
        out_specs=(in_vmem,) * 3,
        scratch_shapes=[pltpu.VMEM((2, 8 * HALF_GROUPS + 8, 512), jnp.float32), pltpu.SMEM(table.shape, jnp.int32), pltpu.SemaphoreType.DMA, pltpu.SemaphoreType.DMA(amps.shape[:1])],
        **kernel_params("give_half"),
    )(*(pltpu.with_memory_space_constraint(array, pltpu.HBM) for array in (table, amps)))


def keep_half(blocks, mixes):
    in_vmem = pl.BlockSpec(memory_space=pltpu.VMEM)
    return pl.pallas_call(
        keep_kernel,
        out_shape=pltpu.VMEM((4, 4, UNIT, 8, 128), jnp.float32),
        in_specs=[in_vmem] * 2,
        out_specs=in_vmem,
        scratch_shapes=[pltpu.VMEM((2, 8 * HALF_GROUPS + 8, 512), jnp.float32)],
        **kernel_params("keep_half"),
    )(*(pltpu.with_memory_space_constraint(array, pltpu.VMEM) for array in (blocks, mixes)))


def combine(body, outs, *arrays):
    in_vmem = pl.BlockSpec(memory_space=pltpu.VMEM)
    return pl.pallas_call(
        body,
        out_shape=tuple(pltpu.VMEM(shape, jnp.float32) for shape in outs),
        in_specs=[in_vmem] * len(arrays),
        out_specs=(in_vmem,) * len(outs),
        compiler_params=pltpu.CompilerParams(vmem_limit_bytes=4 << 20),
        name=body.__name__,
    )(*(pltpu.with_memory_space_constraint(array, pltpu.VMEM) for array in arrays))


def add_halves(keep, got, send_a, keep_a, send_b, keep_b):
    for first, out, distances in ((0, send_a, (1, 2)), (0, keep_a, (0, 3)), (2, send_b, (3, 2)), (2, keep_b, (0, 1))):
        for n, k in enumerate(distances):
            for j in range(2):
                out[n, j] = keep[k, first + j] + got[k, first + j]


def add_first(keep_a, got_a, keep_b, got_b, own_a, send_a, own_b, send_b):
    own_a[...] = keep_a[0] + got_a[0]
    send_a[...] = keep_a[1] + got_a[1]
    own_b[...] = keep_b[0] + got_b[0]
    send_b[...] = keep_b[1] + got_b[1]


def add_second(own_a, got_a, own_b, got_b, *sums):
    for j in range(2):
        sums[j][...] = own_a[j] + got_a[j]
        sums[2 + j][...] = own_b[j] + got_b[j]


def layout_kernel(scale, mine, other, out, whole):
    core = lax.axis_index("core")
    whole[pl.ds(core * 2 * UNIT, 2 * UNIT)] = mine[...] * scale
    whole[pl.ds((1 - core) * 2 * UNIT, 2 * UNIT)] = other[...] * scale
    for half in range(2):
        for m in range(FULL):
            g, l = divmod(m, WIDE)
            row = 8 * (half * HALF_GROUPS + g)
            out[0, row : row + 8, 128 * l : 128 * l + 128] = whole[half * 2 * UNIT + m]
        for g in range(HALF_GROUPS):
            n, k = divmod(g, 8)
            tile = whole[half * 2 * UNIT + FULL + n]
            if k:
                tile = pltpu.roll(tile, 128 - 16 * k, 1)
            row = 8 * (half * HALF_GROUPS + g)
            out[0, row : row + 8, 128 * WIDE : 128 * WIDE + 16] = tile[:, :16]


def lay_out(scale, size, *units):
    return pl.pallas_call(
        functools.partial(layout_kernel, scale),
        out_shape=jax.ShapeDtypeStruct((1, size, size), jnp.float32),
        in_specs=[pl.BlockSpec(memory_space=pltpu.VMEM)] * 2,
        out_specs=pl.BlockSpec(memory_space=pltpu.VMEM),
        scratch_shapes=[pltpu.VMEM((4 * UNIT, 8, 128), jnp.float32)],
        compiler_params=pltpu.CompilerParams(vmem_limit_bytes=8 << 20),
        name="lay_out",
    )(*(pltpu.with_memory_space_constraint(unit, pltpu.VMEM) for unit in units))


def on_device(amps, conserve):
    scale = 1.0 / (8 * 32 * amps.shape[3] * amps.shape[4])
    table, own = conserve[0, 0], amps[0, 0]
    blocks, mixes, give = give_half(table, own)
    got = send(give, across)
    keep = keep_half(blocks, mixes)

    unit = (UNIT, 8, 128)
    send_a, keep_a, send_b, keep_b = combine(add_halves, [(2, 2, *unit)] * 4, keep, got)
    halves = keep_a, send(send_a, functools.partial(around, 1, 0)), keep_b, send(send_b, functools.partial(around, 3, 0))
    own_a, send_a, own_b, send_b = combine(add_first, [(2, *unit)] * 4, *halves)
    halves = own_a, send(send_a, functools.partial(around, 3, 0)), own_b, send(send_b, functools.partial(around, 1, 0))
    second = combine(add_second, [unit] * 4, *halves)
    came = [send(second[j], functools.partial(around, j, 1)) for j in (1, 2, 3)]
    third = (second[0] + came[0]) + (came[1] + came[2])
    parts = lax.all_to_all(third.reshape(8, UNIT // 8, 8, 128), "z", 0, 0, tiled=True)
    eighth = jnp.sum(parts, axis=0, keepdims=True)
    mine = lax.all_to_all(jnp.broadcast_to(eighth, (16, *parts.shape[1:])), ("x_lo", "z"), 0, 0, tiled=True)
    mine = mine.reshape(2 * UNIT, 8, 128)
    return lay_out(scale, amps.shape[4], mine, send(mine, across))


def solution(mesh):
    fine = Mesh(mesh.devices.reshape(SIZES), FINE)
    ki, kj = ("x_hi", "y"), ("x_lo", "z", "core")
    return jax.shard_map(
        on_device,
        mesh=fine,
        in_specs=(P(ki, kj, None, None, None, None), P(ki, kj, None)),
        out_specs=P(ki, None, None),
        check_vma=False,
    )
```

time: 81.5 us -> 83.6 us (1.026)
  waiting for transfers between devices: 18.4 us -> 23.3 us
  starting transfers between devices: 20.3 us -> 16.7 us
  Pallas kernels: 14.7 us -> 15.9 us
    ppermute x14 -> x9, waiting for transfers between devices: 18.4 us -> 23.3 us  [send(): return lax.ppermute(value, FINE, pairs(move))]
    ppermute x14 -> x9, starting transfers between devices: 20.3 us -> 16.7 us  [send(): return lax.ppermute(value, FINE, pairs(move))]
    pallas_call x2, Pallas kernels: 13.2 us -> 14.4 us  [the longest x1 9.76 us: give_half(): pl.pallas_call(give_kernel, out_shape=(whole, whole, pltpu.VMEM((4, 4, UN...]
  transfers between devices with their start and end apart: 14 -> 9, of which waited for: 11 -> 8; matrix products, arithmetic and copies ran while one was open for 0% -> 0% of each run, Pallas kernels for 7% -> 6%
where the time goes in v5:
time: 83.6 us; the launch traced here: 83.3 us
  blocking collectives  27.4 us (33%)
  waiting for transfers between devices  23.3 us (28%)
  starting transfers between devices  16.7 us (20%)
  Pallas kernels  15.9 us (19%)
    ppermute x9, waiting for transfers between devices, send(): return lax.ppermute(value, FINE, pairs(move))  23.3 us
    ppermute x9, starting transfers between devices, send(): return lax.ppermute(value, FINE, pairs(move))  16.7 us
    all_to_all x1, blocking collectives, on_device(): lax.all_to_all(third.reshape(8, UNIT // 8, 8, 128), 'z', 0, 0, tiled=True)  16.6 us
    all_to_all x1, blocking collectives, on_device(): lax.all_to_all(jnp.broadcast_to(eighth, (16, *parts.shape[1:])), ('x_lo',...  10.8 us
    pallas_call x1, Pallas kernels, give_half(): pl.pallas_call(give_kernel, out_shape=(whole, whole, pltpu.VMEM((4, 4, UN...  9.76 us
    pallas_call x1, Pallas kernels, keep_half(): pl.pallas_call(keep_kernel, out_shape=pltpu.VMEM((4, 4, UNIT, 8, 128), jn...  4.63 us
  transfers between devices with their start and end apart: 9, of which 8 were waited for; matrix products, arithmetic and copies ran while one was open for 0% of the time, Pallas kernels for 6%

profile of v5, /device:TPU:1, one launch (start us, length us, event | category | flops | bytes accessed | tf_op | source)
XLA Modules:
  0.0 83.3 jit_solution(9972519871916390363)
XLA Ops:
  0.0 9.8 %give_half.1 = (bf16[8,4,400,400]{3,2,1,0:T(8,128)(2,1)S(1)}, bf16[8,4,400,400]{3,2,1,0:T(8,128)(2,1)S(1)}, f32[4,4,40,8,128]{4,3,2,1,0:T(8,128)S(1)}) custom-call(s32[8]{0:T(128)} %bitcast.8, bf16[8,4,400,400]{3,2,1,0:T(8,128)(2,1)} %bitcast.7), custom_call_target="tpu_custom_call" | custom-call | flops 4294967296 | bytes 13631488 | tf_op jit(solution)/shard_map/give_half/pallas_call | solution.py:143
  9.8 2.9 %collective-permute-start = (f32[4,4,40,8,128]{4,3,2,1,0:T(8,128)S(1)}, f32[4,4,40,8,128]{4,3,2,1,0:T(8,128)S(1)}, u32[]{:S(2)}, u32[]{:S(2)}) collective-permute-start(f32[4,4,40,8,128]{4,3,2,1,0:T(8,128)S(1)} %get-tuple-element.22), channel_id=1, source_target_pairs={{0,1},{1,0},{2,3},{3,2},{4,5},{5,4},{6,7},{7,6},{8,9},{9,8},{10,11... | collective-permute-start | bytes 7864328 | tf_op jit(solution)/shard_map/ppermute | solution.py:32
  12.6 4.6 %keep_half.1.keep = f32[4,4,40,8,128]{4,3,2,1,0:T(8,128)S(1)} custom-call(bf16[8,4,400,400]{3,2,1,0:T(8,128)(2,1)S(1)} %get-tuple-element.20.blocks, bf16[8,4,400,400]{3,2,1,0:T(8,128)(2,1)S(1)} %get-tuple-element.21.mixes), custom_call_target="tpu_custom_call" | custom-call | flops 4294967296 | bytes 13631488 | tf_op jit(solution)/shard_map/keep_half/pallas_call | solution.py:155
  17.3 0.0 collective-permute-done.got
  17.3 0.3 add_halves.1
  17.5 0.1 collective-permute-start.1
  17.6 1.4 %collective-permute-start.2 = (f32[2,2,40,8,128]{4,3,2,1,0:T(8,128)S(1)}, f32[2,2,40,8,128]{4,3,2,1,0:T(8,128)S(1)}, u32[]{:S(2)}, u32[]{:S(2)}) collective-permute-start(f32[2,2,40,8,128]{4,3,2,1,0:T(8,128)S(1)} %get-tuple-element.26), channel_id=1, source_target_pairs={{0,96},{1,145},{2,98},{3,147},{4,100},{5,149},{6,102},{7,151},{8,1... | collective-permute-start | bytes 1966088 | tf_op jit(solution)/shard_map/ppermute | solution.py:32
  19.0 8.3 %collective-permute-done.1.got_a = f32[2,2,40,8,128]{4,3,2,1,0:T(8,128)S(1)} collective-permute-done((f32[2,2,40,8,128]{4,3,2,1,0:T(8,128)S(1)}, f32[2,2,40,8,128]{4,3,2,1,0:T(8,128)S(1)}, u32[]{:S(2)}, u32[]{:S(2)}) %collective-permute-start.1) | collective-permute-done | bytes 655392 | tf_op jit(solution)/shard_map/ppermute | solution.py:32
  27.4 1.3 %collective-permute-done.2.got_b = f32[2,2,40,8,128]{4,3,2,1,0:T(8,128)S(1)} collective-permute-done((f32[2,2,40,8,128]{4,3,2,1,0:T(8,128)S(1)}, f32[2,2,40,8,128]{4,3,2,1,0:T(8,128)S(1)}, u32[]{:S(2)}, u32[]{:S(2)}) %collective-permute-start.2) | collective-permute-done | bytes 655392 | tf_op jit(solution)/shard_map/ppermute | solution.py:32
  28.7 0.1 add_first.1
  28.8 1.4 %collective-permute-start.3 = (f32[2,40,8,128]{3,2,1,0:T(8,128)S(1)}, f32[2,40,8,128]{3,2,1,0:T(8,128)S(1)}, u32[]{:S(2)}, u32[]{:S(2)}) collective-permute-start(f32[2,40,8,128]{3,2,1,0:T(8,128)S(1)} %get-tuple-element.28), channel_id=1, source_target_pairs={{0,96},{1,145},{2,98},{3,147},{4,100},{5,149},{6,102},{7,151},{8,1... | collective-permute-start | bytes 983048 | tf_op jit(solution)/shard_map/ppermute | solution.py:32
  30.2 0.0 collective-permute-start.4
  30.2 6.1 %collective-permute-done.3.got_a = f32[2,40,8,128]{3,2,1,0:T(8,128)S(1)} collective-permute-done((f32[2,40,8,128]{3,2,1,0:T(8,128)S(1)}, f32[2,40,8,128]{3,2,1,0:T(8,128)S(1)}, u32[]{:S(2)}, u32[]{:S(2)}) %collective-permute-start.3) | collective-permute-done | bytes 327712 | tf_op jit(solution)/shard_map/ppermute | solution.py:32
  36.3 0.1 collective-permute-done.4.got_b
  36.4 0.1 add_second.1
  36.5 1.0 %collective-permute-start.5 = (f32[40,8,128]{2,1,0:T(8,128)S(1)}, f32[40,8,128]{2,1,0:T(8,128)S(1)}, u32[]{:S(2)}, u32[]{:S(2)}) collective-permute-start(f32[40,8,128]{2,1,0:T(8,128)S(1)} %get-tuple-element.32), channel_id=1, source_target_pairs={{0,16},{1,33},{2,18},{3,35},{4,20},{5,37},{6,22},{7,39},{8,24},{9,... | collective-permute-start | bytes 491528 | tf_op jit(solution)/shard_map/ppermute | solution.py:32
  37.5 2.9 %collective-permute-start.6 = (f32[40,8,128]{2,1,0:T(8,128)S(1)}, f32[40,8,128]{2,1,0:T(8,128)S(1)}, u32[]{:S(2)}, u32[]{:S(2)}) collective-permute-start(f32[40,8,128]{2,1,0:T(8,128)S(1)} %get-tuple-element.33), channel_id=1, source_target_pairs={{0,128},{1,65},{2,130},{3,67},{4,132},{5,69},{6,134},{7,71},{8,136... | collective-permute-start | bytes 491528 | tf_op jit(solution)/shard_map/ppermute | solution.py:32
  40.4 0.0 collective-permute-start.7
  40.4 0.3 collective-permute-done.5
  40.7 4.2 %collective-permute-done.6 = f32[40,8,128]{2,1,0:T(8,128)S(1)} collective-permute-done((f32[40,8,128]{2,1,0:T(8,128)S(1)}, f32[40,8,128]{2,1,0:T(8,128)S(1)}, u32[]{:S(2)}, u32[]{:S(2)}) %collective-permute-start.6) | collective-permute-done | bytes 163872 | tf_op jit(solution)/shard_map/ppermute | solution.py:32
  44.9 1.7 %collective-permute-done.7 = f32[40,8,128]{2,1,0:T(8,128)S(1)} collective-permute-done((f32[40,8,128]{2,1,0:T(8,128)S(1)}, f32[40,8,128]{2,1,0:T(8,128)S(1)}, u32[]{:S(2)}, u32[]{:S(2)}) %collective-permute-start.7) | collective-permute-done | bytes 163872 | tf_op jit(solution)/shard_map/ppermute | solution.py:32
  46.6 16.6 %all_to_all.10 = f32[8,5,8,128]{3,2,1,0:T(8,128)S(1)} all-to-all(f32[8,5,8,128]{3,2,1,0:T(8,128)S(1)} %bitcast.6), channel_id=1, replica_groups=mesh['x_hi'=2,'y'=4,'x_lo'=2,'z'=8,'core'=2] {'z'}, dimensions={0} | all-to-all | bytes 327680 | tf_op jit(solution)/shard_map/all_to_all | solution.py:242
  63.3 10.8 %all_to_all.11 = f32[16,5,8,128]{3,2,1,0:T(8,128)S(1)} all-to-all(f32[16,5,8,128]{3,2,1,0:T(8,128)S(1)} %broadcast_in_dim.2), channel_id=1, replica_groups=mesh['x_hi'=2,'y'=4,'x_lo'=2,'z'=8,'core'=2] {'x_lo','z'}, dimensions={0} | all-to-all | bytes 655360 | tf_op jit(solution)/shard_map/all_to_all | solution.py:244
  74.0 7.0 %collective-permute-start.8 = (f32[80,8,128]{2,1,0:T(8,128)S(1)}, f32[80,8,128]{2,1,0:T(8,128)S(1)}, u32[]{:S(2)}, u32[]{:S(2)}) collective-permute-start(f32[80,8,128]{2,1,0:T(8,128)S(1)} %bitcast.4), channel_id=1, source_target_pairs={{0,1},{1,0},{2,3},{3,2},{4,5},{5,4},{6,7},{7,6},{8,9},{9,8},{10,11... | collective-permute-start | bytes 983048 | tf_op jit(solution)/shard_map/ppermute | solution.py:32
  81.1 1.3 %collective-permute-done.8.other = f32[80,8,128]{2,1,0:T(8,128)S(1)} collective-permute-done((f32[80,8,128]{2,1,0:T(8,128)S(1)}, f32[80,8,128]{2,1,0:T(8,128)S(1)}, u32[]{:S(2)}, u32[]{:S(2)}) %collective-permute-start.8) | collective-permute-done | bytes 327712 | tf_op jit(solution)/shard_map/ppermute | solution.py:32
  82.3 1.0 %lay_out.1 = f32[1,400,400]{2,1,0:T(8,128)} custom-call(f32[80,8,128]{2,1,0:T(8,128)S(1)} %bitcast.5, f32[80,8,128]{2,1,0:T(8,128)S(1)} %collective-permute-done.8.other), custom_call_target="tpu_custom_call" | custom-call | tf_op jit(solution)/shard_map/lay_out/pallas_call | solution.py:216
  (3 shorter events, 0.1 us)
Async XLA Ops:
  9.8 7.5 %collective-permute-start = (f32[4,4,40,8,128]{4,3,2,1,0:T(8,128)S(1)}, f32[4,4,40,8,128]{4,3,2,1,0:T(8,128)S(1)}, u32[]{:S(2)}, u32[]{:S(2)}) collective-permute-start(f32[4,4,40,8,128]{4,3,2,1,0:T(8,128)S(1)} %get-tuple-element.22), channel_id=1, source_target_pairs={{0,1},{1,0},{2,3},{3,2},{4,5},{5,4},{6,7},{7,6},{8,9},{9,8},{10,11... | collective-permute-start | bytes 7864328 | tf_op jit(solution)/shard_map/ppermute | solution.py:32
  17.5 9.8 %collective-permute-start.1 = (f32[2,2,40,8,128]{4,3,2,1,0:T(8,128)S(1)}, f32[2,2,40,8,128]{4,3,2,1,0:T(8,128)S(1)}, u32[]{:S(2)}, u32[]{:S(2)}) collective-permute-start(f32[2,2,40,8,128]{4,3,2,1,0:T(8,128)S(1)} %get-tuple-element.24), channel_id=1, source_target_pairs={{0,32},{1,17},{2,34},{3,19},{4,36},{5,21},{6,38},{7,23},{8,40},{9,... | collective-permute-start | bytes 1966088 | tf_op jit(solution)/shard_map/ppermute | solution.py:32
  17.6 11.0 %collective-permute-start.2 = (f32[2,2,40,8,128]{4,3,2,1,0:T(8,128)S(1)}, f32[2,2,40,8,128]{4,3,2,1,0:T(8,128)S(1)}, u32[]{:S(2)}, u32[]{:S(2)}) collective-permute-start(f32[2,2,40,8,128]{4,3,2,1,0:T(8,128)S(1)} %get-tuple-element.26), channel_id=1, source_target_pairs={{0,96},{1,145},{2,98},{3,147},{4,100},{5,149},{6,102},{7,151},{8,1... | collective-permute-start | bytes 1966088 | tf_op jit(solution)/shard_map/ppermute | solution.py:32
  28.8 7.5 %collective-permute-start.3 = (f32[2,40,8,128]{3,2,1,0:T(8,128)S(1)}, f32[2,40,8,128]{3,2,1,0:T(8,128)S(1)}, u32[]{:S(2)}, u32[]{:S(2)}) collective-permute-start(f32[2,40,8,128]{3,2,1,0:T(8,128)S(1)} %get-tuple-element.28), channel_id=1, source_target_pairs={{0,96},{1,145},{2,98},{3,147},{4,100},{5,149},{6,102},{7,151},{8,1... | collective-permute-start | bytes 983048 | tf_op jit(solution)/shard_map/ppermute | solution.py:32
  30.2 6.2 %collective-permute-start.4 = (f32[2,40,8,128]{3,2,1,0:T(8,128)S(1)}, f32[2,40,8,128]{3,2,1,0:T(8,128)S(1)}, u32[]{:S(2)}, u32[]{:S(2)}) collective-permute-start(f32[2,40,8,128]{3,2,1,0:T(8,128)S(1)} %get-tuple-element.30), channel_id=1, source_target_pairs={{0,32},{1,17},{2,34},{3,19},{4,36},{5,21},{6,38},{7,23},{8,40},{9,... | collective-permute-start | bytes 983048 | tf_op jit(solution)/shard_map/ppermute | solution.py:32
  36.5 4.3 %collective-permute-start.5 = (f32[40,8,128]{2,1,0:T(8,128)S(1)}, f32[40,8,128]{2,1,0:T(8,128)S(1)}, u32[]{:S(2)}, u32[]{:S(2)}) collective-permute-start(f32[40,8,128]{2,1,0:T(8,128)S(1)} %get-tuple-element.32), channel_id=1, source_target_pairs={{0,16},{1,33},{2,18},{3,35},{4,20},{5,37},{6,22},{7,39},{8,24},{9,... | collective-permute-start | bytes 491528 | tf_op jit(solution)/shard_map/ppermute | solution.py:32
  37.5 7.5 %collective-permute-start.6 = (f32[40,8,128]{2,1,0:T(8,128)S(1)}, f32[40,8,128]{2,1,0:T(8,128)S(1)}, u32[]{:S(2)}, u32[]{:S(2)}) collective-permute-start(f32[40,8,128]{2,1,0:T(8,128)S(1)} %get-tuple-element.33), channel_id=1, source_target_pairs={{0,128},{1,65},{2,130},{3,67},{4,132},{5,69},{6,134},{7,71},{8,136... | collective-permute-start | bytes 491528 | tf_op jit(solution)/shard_map/ppermute | solution.py:32
  40.4 6.2 %collective-permute-start.7 = (f32[40,8,128]{2,1,0:T(8,128)S(1)}, f32[40,8,128]{2,1,0:T(8,128)S(1)}, u32[]{:S(2)}, u32[]{:S(2)}) collective-permute-start(f32[40,8,128]{2,1,0:T(8,128)S(1)} %get-tuple-element.34), channel_id=1, source_target_pairs={{0,144},{1,97},{2,146},{3,99},{4,148},{5,101},{6,150},{7,103},{8,1... | collective-permute-start | bytes 491528 | tf_op jit(solution)/shard_map/ppermute | solution.py:32
  74.0 8.3 %collective-permute-start.8 = (f32[80,8,128]{2,1,0:T(8,128)S(1)}, f32[80,8,128]{2,1,0:T(8,128)S(1)}, u32[]{:S(2)}, u32[]{:S(2)}) collective-permute-start(f32[80,8,128]{2,1,0:T(8,128)S(1)} %bitcast.4), channel_id=1, source_target_pairs={{0,1},{1,0},{2,3},{3,2},{4,5},{5,4},{6,7},{7,6},{8,9},{9,8},{10,11... | collective-permute-start | bytes 983048 | tf_op jit(solution)/shard_map/ppermute | solution.py:32

commit v6 on v4

--- a/solution.py
+++ b/solution.py
@@ -50,33 +50,25 @@
     return (block // 4 ^ y // 2) * 4 + y
 
 
-def density_kernel(run, table, amps, blocks, keep, give, acc, in_sems):
-    count, orbitals, size = blocks.shape[0], blocks.shape[1], blocks.shape[2]
+def add_block(blocks, acc, keep, give, block, partner, arrive=None):
+    size = blocks.shape[2]
     x_low = lax.axis_index("x_lo")
-    x = lax.axis_index("x_hi") * 2 + x_low
-    y = lax.axis_index("y")
+    x, y = lax.axis_index("x_hi") * 2 + x_low, lax.axis_index("y")
     core = lax.axis_index("core")
-
-    def arrivals(place, o, act):
-        block = block_of(place)
-        partner = table[block]
-        other_place = place_of(partner)
-
-        @pl.when(other_place >= place)
-        def _():
-            act(pltpu.make_async_copy(amps.at[block], blocks.at[block], in_sems.at[block]))
-
-        @pl.when(other_place > place)
-        def _():
-            act(pltpu.make_async_copy(amps.at[partner], blocks.at[partner], in_sems.at[partner]))
-
-    if run == 0:
-        for place in range(count):
-            arrivals(place, slice(None), lambda copy: copy.start())
+    total = None
+    for o in range(blocks.shape[1]):
+        if arrive is not None:
+            arrive(o)
+        own = blocks[block, o]
+        turned = own.T
+        mix = turned + turned - blocks[partner, o]
+        part = jnp.dot(own, mix, preferred_element_type=jnp.float32)
+        total = part if total is None else total + part
+    acc[:, :size] = total
 
     lane = lax.broadcasted_iota(jnp.int32, (8, 128), 1)
 
-    def tile_of(acc, half, m):
+    def tile_of(half, m):
         if m == UNIT * 2 - 1:
             return jnp.zeros((8, 128), jnp.float32)
 
@@ -92,69 +84,99 @@
             tile = jnp.where(lane < 16 * k, tile, pltpu.roll(read(first + k, WIDE), 16 * k, 1))
         return tile
 
-    def step(i, carry):
-        place = run * 4 + i
+    high, dy = block // 4, (block % 4) ^ y
+    for target, half in ((keep, core), (give, 1 - core)):
+        for low in range(2):
+            dx = (high * 2 + low) ^ x
+            k = jnp.where(half == 0, dy, dx)
+            j = jnp.where(half == 0, low ^ x_low, dy & 1)
+            for n in range(UNIT):
+                target[k, j, n] = tile_of(half, low * UNIT + n)
+
+
+def first_kernel(table_in, amps, blocks, keep, give, acc, table, table_sem, sems, early):
+    count, orbitals = blocks.shape[:2]
+
+    def fetch(block, o=None):
+        if o is None:
+            return pltpu.make_async_copy(amps.at[block], blocks.at[block], sems.at[block])
+        return pltpu.make_async_copy(amps.at[block, o], blocks.at[block, o], early.at[block, o])
+
+    def arrivals(place, act, o=None):
         block = block_of(place)
         partner = table[block]
-        total = None
-        for o in range(orbitals):
-            if run == 0 and o == 0:
-                arrivals(place, slice(None), lambda copy: copy.wait())
-            own = blocks[block, o]
-            turned = own.T
-            mix = turned + turned - blocks[partner, o]
-            part = jnp.dot(own, mix, preferred_element_type=jnp.float32)
-            total = part if total is None else total + part
-        acc[:, :size] = total
-
-        high, dy = block // 4, i ^ y
-        for target, half in ((keep, core), (give, 1 - core)):
-            for low in range(2):
-                dx = (high * 2 + low) ^ x
-                k = jnp.where(half == 0, dy, dx)
-                j = jnp.where(half == 0, low ^ x_low, dy & 1)
-                for n in range(UNIT):
-                    target[k, j, n] = tile_of(acc, half, low * UNIT + n)
-
+        other_place = place_of(partner)
+
+        @pl.when(other_place >= place)
+        def _():
+            act(fetch(block, o))
+
+        @pl.when(other_place > place)
+        def _():
+            act(fetch(partner, o))
+
+    fetch(0, 0).start()
+    copy = pltpu.make_async_copy(table_in, table, table_sem)
+    copy.start()
+    copy.wait()
+    partner = table[0]
+    for o in range(orbitals):
+        if o:
+            fetch(0, o).start()
+
+        @pl.when(partner > 0)
+        def _():
+            fetch(partner, o).start()
+
+    for place in range(1, count):
+        arrivals(place, lambda copy: copy.start())
+
+    add_block(blocks, acc.at[0], keep, give, 0, partner, lambda o: arrivals(0, lambda copy: copy.wait(), o))
+
+    def step(place, carry):
+        arrivals(place, lambda copy: copy.wait())
+        block = block_of(place)
+        add_block(blocks, acc.at[1], keep, give, block, table[block])
         return carry
 
-    lax.fori_loop(0, 4, step, 0)
-    if run == 0:
-        for place in range(4, count):
-            arrivals(place, slice(None), lambda copy: copy.wait())
-
-
-def densities(run, table, amps, blocks=None):
-    shape = amps.shape
+    lax.fori_loop(1, 4, step, 0)
+    for place in range(4, count):
+        arrivals(place, lambda copy: copy.wait())
+
+
+def second_kernel(table, blocks, keep, give, acc):
+    for i in range(4):
+        block = block_of(4 + i)
+        add_block(blocks, acc.at[i % 2], keep, give, block, table[block])
+
+
+def densities(run, table, amps):
     half = pltpu.VMEM((4, 2, UNIT, 8, 128), jnp.float32)
     in_vmem = pl.BlockSpec(memory_space=pltpu.VMEM)
+    acc = pltpu.VMEM((2, amps.shape[2], 512), jnp.float32)
     params = dict(
         compiler_params=pltpu.CompilerParams(vmem_limit_bytes=12 << 20),
         cost_estimate=pl.CostEstimate(flops=4 << 30, bytes_accessed=13 << 20, transcendentals=0),
         name="densities",
     )
-    acc = pltpu.VMEM((shape[2], 512), jnp.float32)
     if run == 0:
+        dma = pltpu.SemaphoreType.DMA
         return pl.pallas_call(
-            functools.partial(density_kernel, 0),
-            out_shape=(pltpu.VMEM(shape, jnp.bfloat16), half, half),
-            in_specs=[pl.BlockSpec(memory_space=pltpu.SMEM), pl.BlockSpec(memory_space=pltpu.HBM)],
+            first_kernel,
+            out_shape=(pltpu.VMEM(amps.shape, amps.dtype), half, half),
+            in_specs=[pl.BlockSpec(memory_space=pltpu.HBM)] * 2,
             out_specs=(in_vmem,) * 3,
-            scratch_shapes=[acc, pltpu.SemaphoreType.DMA(shape[:1])],
+            scratch_shapes=[acc, pltpu.SMEM(table.shape, table.dtype), dma, dma(amps.shape[:1]), dma(amps.shape[:2])],
             **params,
-        )(table, pltpu.with_memory_space_constraint(amps, pltpu.HBM))
-
-    def later(table, blocks, keep, give, acc):
-        density_kernel(run, table, None, blocks, keep, give, acc, None)
-
+        )(*(pltpu.with_memory_space_constraint(array, pltpu.HBM) for array in (table, amps)))
     return pl.pallas_call(
-        later,
+        second_kernel,
         out_shape=(half, half),
         in_specs=[pl.BlockSpec(memory_space=pltpu.SMEM), in_vmem],
         out_specs=(in_vmem,) * 2,
         scratch_shapes=[acc],
         **params,
-    )(table, pltpu.with_memory_space_constraint(blocks, pltpu.VMEM))
+    )(table, pltpu.with_memory_space_constraint(amps, pltpu.VMEM))
 
 
 def combine(body, outs, *arrays):
@@ -230,7 +252,7 @@
     table, own = conserve[0, 0], amps[0, 0]
     blocks, keep, give = densities(0, table, own)
     runs = [(keep, send(give, across)), None]
-    keep, give = densities(1, table, own, blocks)
+    keep, give = densities(1, table, blocks)
     runs[1] = (keep, send(give, across))
 
     unit = (UNIT, 8, 128)
@@ -243,7 +265,7 @@
         own_a, send_a, own_b, send_b = combine(add_first, [unit] * 4, *halves)
         arrived += [own_a, send(send_a, functools.partial(around, 3, 0)), own_b, send(send_b, functools.partial(around, 1, 0))]
     second = combine(add_ring, [unit] * 4, *arrived)
-    came = [send(second[j], functools.partial(around, j, 1)) for j in (1, 2, 3)]
+    came = [send(second[j], functools.partial(around, j, 1)) for j in (2, 1, 3)]
     third = (second[0] + came[0]) + (came[1] + came[2])
     parts = lax.all_to_all(third.reshape(8, UNIT // 8, 8, 128), "z", 0, 0, tiled=True)
     eighth = jnp.sum(parts, axis=0, keepdims=True)

time: 81.5 us -> 78.3 us (0.961)
  Pallas kernels: 14.7 us -> 13.7 us
  starting transfers between devices: 20.3 us -> 19.4 us
    pallas_call x2, Pallas kernels: 13.2 us -> 12.1 us  [the longest x1 7.52 us: densities(): pl.pallas_call(first_kernel, out_shape=(pltpu.VMEM(amps.shape, amps.dtype...]
    ppermute x14, starting transfers between devices: 20.3 us -> 19.4 us  [send(): return lax.ppermute(value, FINE, pairs(move))]
  transfers between devices with their start and end apart: 14 -> 14, of which waited for: 11 -> 11; matrix products, arithmetic and copies ran while one was open for 0% -> 0% of each run, Pallas kernels for 7% -> 6%
where the time goes in v6:
time: 78.3 us; the launch traced here: 78.1 us
  blocking collectives  27.2 us (35%)
  starting transfers between devices  19.4 us (25%)
  waiting for transfers between devices  17.7 us (23%)
  Pallas kernels  13.7 us (17%)
    ppermute x14, starting transfers between devices, send(): return lax.ppermute(value, FINE, pairs(move))  19.4 us
    ppermute x14, waiting for transfers between devices, send(): return lax.ppermute(value, FINE, pairs(move))  17.7 us
    all_to_all x1, blocking collectives, on_device(): lax.all_to_all(third.reshape(8, UNIT // 8, 8, 128), 'z', 0, 0, tiled=True)  16.4 us
    all_to_all x1, blocking collectives, on_device(): lax.all_to_all(jnp.broadcast_to(eighth, (16, *parts.shape[1:])), ('x_lo',...  10.8 us
    pallas_call x1, Pallas kernels, densities(): pl.pallas_call(first_kernel, out_shape=(pltpu.VMEM(amps.shape, amps.dtype...  7.52 us
    pallas_call x1, Pallas kernels, densities(): pl.pallas_call(second_kernel, out_shape=(half, half), in_specs=[pl.BlockS...  4.63 us
  transfers between devices with their start and end apart: 14, of which 11 were waited for; matrix products, arithmetic and copies ran while one was open for 0% of the time, Pallas kernels for 6%

profile of v6, /device:TPU:1, one launch (start us, length us, event | category | flops | bytes accessed | tf_op | source)
XLA Modules:
  0.0 78.1 jit_solution(14083362043765518944)
XLA Ops:
  0.0 7.5 %densities.2 = (bf16[8,4,400,400]{3,2,1,0:T(8,128)(2,1)S(1)}, f32[4,2,40,8,128]{4,3,2,1,0:T(8,128)S(1)}, f32[4,2,40,8,128]{4,3,2,1,0:T(8,128)S(1)}) custom-call(s32[8]{0:T(128)} %bitcast.6, bf16[8,4,400,400]{3,2,1,0:T(8,128)(2,1)} %bitcast.9), custom_call_target="tpu_custom_call" | custom-call | flops 4294967296 | bytes 13631488 | tf_op jit(solution)/shard_map/densities/pallas_call | solution.py:164
  7.5 3.6 %collective-permute-start = (f32[4,2,40,8,128]{4,3,2,1,0:T(8,128)S(1)}, f32[4,2,40,8,128]{4,3,2,1,0:T(8,128)S(1)}, u32[]{:S(2)}, u32[]{:S(2)}) collective-permute-start(f32[4,2,40,8,128]{4,3,2,1,0:T(8,128)S(1)} %get-tuple-element.31), channel_id=1, source_target_pairs={{0,1},{1,0},{2,3},{3,2},{4,5},{5,4},{6,7},{7,6},{8,9},{9,8},{10,11... | collective-permute-start | bytes 3932168 | tf_op jit(solution)/shard_map/ppermute | solution.py:32
  11.1 4.6 %densities.3 = (f32[4,2,40,8,128]{4,3,2,1,0:T(8,128)S(1)}, f32[4,2,40,8,128]{4,3,2,1,0:T(8,128)S(1)}) custom-call(s32[8]{0:T(128)S(1)} %bitcast.7, bf16[8,4,400,400]{3,2,1,0:T(8,128)(2,1)S(1)} %get-tuple-element.40.blocks), custom_call_target="tpu_custom_call" | custom-call | flops 4294967296 | bytes 13631488 | tf_op jit(solution)/shard_map/densities/pallas_call | solution.py:172
  15.7 0.1 collective-permute-start.5
  15.8 0.1 add_halves.2
  16.0 0.1 collective-permute-start.1
  16.1 1.3 %collective-permute-start.2 = (f32[2,40,8,128]{3,2,1,0:T(8,128)S(1)}, f32[2,40,8,128]{3,2,1,0:T(8,128)S(1)}, u32[]{:S(2)}, u32[]{:S(2)}) collective-permute-start(f32[2,40,8,128]{3,2,1,0:T(8,128)S(1)} %get-tuple-element.35), channel_id=1, source_target_pairs={{0,96},{1,145},{2,98},{3,147},{4,100},{5,149},{6,102},{7,151},{8,1... | collective-permute-start | bytes 983048 | tf_op jit(solution)/shard_map/ppermute | solution.py:32
  17.4 1.5 %collective-permute-done.5.got = f32[4,2,40,8,128]{4,3,2,1,0:T(8,128)S(1)} collective-permute-done((f32[4,2,40,8,128]{4,3,2,1,0:T(8,128)S(1)}, f32[4,2,40,8,128]{4,3,2,1,0:T(8,128)S(1)}, u32[]{:S(2)}, u32[]{:S(2)}) %collective-permute-start.5) | collective-permute-done | bytes 1310752 | tf_op jit(solution)/shard_map/ppermute | solution.py:32
  18.8 0.1 add_halves.3
  19.0 0.1 collective-permute-start.6
  19.1 1.3 %collective-permute-start.7 = (f32[2,40,8,128]{3,2,1,0:T(8,128)S(1)}, f32[2,40,8,128]{3,2,1,0:T(8,128)S(1)}, u32[]{:S(2)}, u32[]{:S(2)}) collective-permute-start(f32[2,40,8,128]{3,2,1,0:T(8,128)S(1)} %get-tuple-element.46), channel_id=1, source_target_pairs={{0,96},{1,145},{2,98},{3,147},{4,100},{5,149},{6,102},{7,151},{8,1... | collective-permute-start | bytes 983048 | tf_op jit(solution)/shard_map/ppermute | solution.py:32
  20.4 1.9 %collective-permute-done.1.got_a = f32[2,40,8,128]{3,2,1,0:T(8,128)S(1)} collective-permute-done((f32[2,40,8,128]{3,2,1,0:T(8,128)S(1)}, f32[2,40,8,128]{3,2,1,0:T(8,128)S(1)}, u32[]{:S(2)}, u32[]{:S(2)}) %collective-permute-start.1) | collective-permute-done | bytes 327712 | tf_op jit(solution)/shard_map/ppermute | solution.py:32
  22.3 1.3 %collective-permute-done.2.got_b = f32[2,40,8,128]{3,2,1,0:T(8,128)S(1)} collective-permute-done((f32[2,40,8,128]{3,2,1,0:T(8,128)S(1)}, f32[2,40,8,128]{3,2,1,0:T(8,128)S(1)}, u32[]{:S(2)}, u32[]{:S(2)}) %collective-permute-start.2) | collective-permute-done | bytes 327712 | tf_op jit(solution)/shard_map/ppermute | solution.py:32
  23.7 1.3 %collective-permute-start.3 = (f32[40,8,128]{2,1,0:T(8,128)S(1)}, f32[40,8,128]{2,1,0:T(8,128)S(1)}, u32[]{:S(2)}, u32[]{:S(2)}) collective-permute-start(f32[40,8,128]{2,1,0:T(8,128)S(1)} %get-tuple-element.37), channel_id=1, source_target_pairs={{0,96},{1,145},{2,98},{3,147},{4,100},{5,149},{6,102},{7,151},{8,1... | collective-permute-start | bytes 491528 | tf_op jit(solution)/shard_map/ppermute | solution.py:32
  24.9 0.8 %collective-permute-done.6.got_a = f32[2,40,8,128]{3,2,1,0:T(8,128)S(1)} collective-permute-done((f32[2,40,8,128]{3,2,1,0:T(8,128)S(1)}, f32[2,40,8,128]{3,2,1,0:T(8,128)S(1)}, u32[]{:S(2)}, u32[]{:S(2)}) %collective-permute-start.6) | collective-permute-done | bytes 327712 | tf_op jit(solution)/shard_map/ppermute | solution.py:32
  25.8 1.3 %collective-permute-done.7.got_b = f32[2,40,8,128]{3,2,1,0:T(8,128)S(1)} collective-permute-done((f32[2,40,8,128]{3,2,1,0:T(8,128)S(1)}, f32[2,40,8,128]{3,2,1,0:T(8,128)S(1)}, u32[]{:S(2)}, u32[]{:S(2)}) %collective-permute-start.7) | collective-permute-done | bytes 327712 | tf_op jit(solution)/shard_map/ppermute | solution.py:32
  27.1 0.1 add_first.3
  27.2 1.3 %collective-permute-start.8 = (f32[40,8,128]{2,1,0:T(8,128)S(1)}, f32[40,8,128]{2,1,0:T(8,128)S(1)}, u32[]{:S(2)}, u32[]{:S(2)}) collective-permute-start(f32[40,8,128]{2,1,0:T(8,128)S(1)} %get-tuple-element.48), channel_id=1, source_target_pairs={{0,96},{1,145},{2,98},{3,147},{4,100},{5,149},{6,102},{7,151},{8,1... | collective-permute-start | bytes 491528 | tf_op jit(solution)/shard_map/ppermute | solution.py:32
  28.5 0.7 collective-permute-done.3.refs_1_
  29.1 3.5 %collective-permute-done.8.refs_5_ = f32[40,8,128]{2,1,0:T(8,128)S(1)} collective-permute-done((f32[40,8,128]{2,1,0:T(8,128)S(1)}, f32[40,8,128]{2,1,0:T(8,128)S(1)}, u32[]{:S(2)}, u32[]{:S(2)}) %collective-permute-start.8) | collective-permute-done | bytes 163872 | tf_op jit(solution)/shard_map/ppermute | solution.py:32
  32.7 0.1 add_ring.1
  32.7 3.0 %collective-permute-start.10 = (f32[40,8,128]{2,1,0:T(8,128)S(1)}, f32[40,8,128]{2,1,0:T(8,128)S(1)}, u32[]{:S(2)}, u32[]{:S(2)}) collective-permute-start(f32[40,8,128]{2,1,0:T(8,128)S(1)} %get-tuple-element.52), channel_id=1, source_target_pairs={{0,128},{1,65},{2,130},{3,67},{4,132},{5,69},{6,134},{7,71},{8,136... | collective-permute-start | bytes 491528 | tf_op jit(solution)/shard_map/ppermute | solution.py:32
  35.7 0.5 collective-permute-start.11
  36.2 0.3 collective-permute-start.12
  36.5 2.0 %collective-permute-done.10 = f32[40,8,128]{2,1,0:T(8,128)S(1)} collective-permute-done((f32[40,8,128]{2,1,0:T(8,128)S(1)}, f32[40,8,128]{2,1,0:T(8,128)S(1)}, u32[]{:S(2)}, u32[]{:S(2)}) %collective-permute-start.10) | collective-permute-done | bytes 163872 | tf_op jit(solution)/shard_map/ppermute | solution.py:32
  38.5 2.5 %collective-permute-done.11 = f32[40,8,128]{2,1,0:T(8,128)S(1)} collective-permute-done((f32[40,8,128]{2,1,0:T(8,128)S(1)}, f32[40,8,128]{2,1,0:T(8,128)S(1)}, u32[]{:S(2)}, u32[]{:S(2)}) %collective-permute-start.11) | collective-permute-done | bytes 163872 | tf_op jit(solution)/shard_map/ppermute | solution.py:32
  41.0 0.9 %collective-permute-done.12 = f32[40,8,128]{2,1,0:T(8,128)S(1)} collective-permute-done((f32[40,8,128]{2,1,0:T(8,128)S(1)}, f32[40,8,128]{2,1,0:T(8,128)S(1)}, u32[]{:S(2)}, u32[]{:S(2)}) %collective-permute-start.12) | collective-permute-done | bytes 163872 | tf_op jit(solution)/shard_map/ppermute | solution.py:32
  41.9 16.4 %all_to_all.10 = f32[8,5,8,128]{3,2,1,0:T(8,128)S(1)} all-to-all(f32[8,5,8,128]{3,2,1,0:T(8,128)S(1)} %bitcast.8), channel_id=1, replica_groups=mesh['x_hi'=2,'y'=4,'x_lo'=2,'z'=8,'core'=2] {'z'}, dimensions={0} | all-to-all | bytes 327680 | tf_op jit(solution)/shard_map/all_to_all | solution.py:270
  58.4 10.8 %all_to_all.11 = f32[16,5,8,128]{3,2,1,0:T(8,128)S(1)} all-to-all(f32[16,5,8,128]{3,2,1,0:T(8,128)S(1)} %broadcast_in_dim.2), channel_id=1, replica_groups=mesh['x_hi'=2,'y'=4,'x_lo'=2,'z'=8,'core'=2] {'x_lo','z'}, dimensions={0} | all-to-all | bytes 655360 | tf_op jit(solution)/shard_map/all_to_all | solution.py:272
  69.2 6.7 %collective-permute-start.13 = (f32[80,8,128]{2,1,0:T(8,128)S(1)}, f32[80,8,128]{2,1,0:T(8,128)S(1)}, u32[]{:S(2)}, u32[]{:S(2)}) collective-permute-start(f32[80,8,128]{2,1,0:T(8,128)S(1)} %bitcast.4), channel_id=1, source_target_pairs={{0,1},{1,0},{2,3},{3,2},{4,5},{5,4},{6,7},{7,6},{8,9},{9,8},{10,11... | collective-permute-start | bytes 983048 | tf_op jit(solution)/shard_map/ppermute | solution.py:32
  75.9 1.3 %collective-permute-done.13.other = f32[80,8,128]{2,1,0:T(8,128)S(1)} collective-permute-done((f32[80,8,128]{2,1,0:T(8,128)S(1)}, f32[80,8,128]{2,1,0:T(8,128)S(1)}, u32[]{:S(2)}, u32[]{:S(2)}) %collective-permute-start.13) | collective-permute-done | bytes 327712 | tf_op jit(solution)/shard_map/ppermute | solution.py:32
  77.1 1.0 %lay_out.1 = f32[1,400,400]{2,1,0:T(8,128)} custom-call(f32[80,8,128]{2,1,0:T(8,128)S(1)} %bitcast.5, f32[80,8,128]{2,1,0:T(8,128)S(1)} %collective-permute-done.13.other), custom_call_target="tpu_custom_call" | custom-call | tf_op jit(solution)/shard_map/lay_out/pallas_call | solution.py:239
  (11 shorter events, 0.2 us)
Async XLA Ops:
  0.0 11.1 %copy-start = (s32[1,1,8]{2,1,0:T(1,128)S(1)}, s32[1,1,8]{2,1,0:T(1,128)}, u32[]{:S(2)}) copy-start(s32[1,1,8]{2,1,0:T(1,128)} %param.3) | copy-start | bytes 100
  7.5 8.3 %collective-permute-start = (f32[4,2,40,8,128]{4,3,2,1,0:T(8,128)S(1)}, f32[4,2,40,8,128]{4,3,2,1,0:T(8,128)S(1)}, u32[]{:S(2)}, u32[]{:S(2)}) collective-permute-start(f32[4,2,40,8,128]{4,3,2,1,0:T(8,128)S(1)} %get-tuple-element.31), channel_id=1, source_target_pairs={{0,1},{1,0},{2,3},{3,2},{4,5},{5,4},{6,7},{7,6},{8,9},{9,8},{10,11... | collective-permute-start | bytes 3932168 | tf_op jit(solution)/shard_map/ppermute | solution.py:32
  15.7 3.1 %collective-permute-start.5 = (f32[4,2,40,8,128]{4,3,2,1,0:T(8,128)S(1)}, f32[4,2,40,8,128]{4,3,2,1,0:T(8,128)S(1)}, u32[]{:S(2)}, u32[]{:S(2)}) collective-permute-start(f32[4,2,40,8,128]{4,3,2,1,0:T(8,128)S(1)} %get-tuple-element.42), channel_id=1, source_target_pairs={{0,1},{1,0},{2,3},{3,2},{4,5},{5,4},{6,7},{7,6},{8,9},{9,8},{10,11... | collective-permute-start | bytes 3932168 | tf_op jit(solution)/shard_map/ppermute | solution.py:32
  16.0 6.3 %collective-permute-start.1 = (f32[2,40,8,128]{3,2,1,0:T(8,128)S(1)}, f32[2,40,8,128]{3,2,1,0:T(8,128)S(1)}, u32[]{:S(2)}, u32[]{:S(2)}) collective-permute-start(f32[2,40,8,128]{3,2,1,0:T(8,128)S(1)} %get-tuple-element.33), channel_id=1, source_target_pairs={{0,32},{1,17},{2,34},{3,19},{4,36},{5,21},{6,38},{7,23},{8,40},{9,... | collective-permute-start | bytes 983048 | tf_op jit(solution)/shard_map/ppermute | solution.py:32
  16.1 7.5 %collective-permute-start.2 = (f32[2,40,8,128]{3,2,1,0:T(8,128)S(1)}, f32[2,40,8,128]{3,2,1,0:T(8,128)S(1)}, u32[]{:S(2)}, u32[]{:S(2)}) collective-permute-start(f32[2,40,8,128]{3,2,1,0:T(8,128)S(1)} %get-tuple-element.35), channel_id=1, source_target_pairs={{0,96},{1,145},{2,98},{3,147},{4,100},{5,149},{6,102},{7,151},{8,1... | collective-permute-start | bytes 983048 | tf_op jit(solution)/shard_map/ppermute | solution.py:32
  19.0 6.8 %collective-permute-start.6 = (f32[2,40,8,128]{3,2,1,0:T(8,128)S(1)}, f32[2,40,8,128]{3,2,1,0:T(8,128)S(1)}, u32[]{:S(2)}, u32[]{:S(2)}) collective-permute-start(f32[2,40,8,128]{3,2,1,0:T(8,128)S(1)} %get-tuple-element.44), channel_id=1, source_target_pairs={{0,32},{1,17},{2,34},{3,19},{4,36},{5,21},{6,38},{7,23},{8,40},{9,... | collective-permute-start | bytes 983048 | tf_op jit(solution)/shard_map/ppermute | solution.py:32
  19.1 8.0 %collective-permute-start.7 = (f32[2,40,8,128]{3,2,1,0:T(8,128)S(1)}, f32[2,40,8,128]{3,2,1,0:T(8,128)S(1)}, u32[]{:S(2)}, u32[]{:S(2)}) collective-permute-start(f32[2,40,8,128]{3,2,1,0:T(8,128)S(1)} %get-tuple-element.46), channel_id=1, source_target_pairs={{0,96},{1,145},{2,98},{3,147},{4,100},{5,149},{6,102},{7,151},{8,1... | collective-permute-start | bytes 983048 | tf_op jit(solution)/shard_map/ppermute | solution.py:32
  23.7 5.5 %collective-permute-start.3 = (f32[40,8,128]{2,1,0:T(8,128)S(1)}, f32[40,8,128]{2,1,0:T(8,128)S(1)}, u32[]{:S(2)}, u32[]{:S(2)}) collective-permute-start(f32[40,8,128]{2,1,0:T(8,128)S(1)} %get-tuple-element.37), channel_id=1, source_target_pairs={{0,96},{1,145},{2,98},{3,147},{4,100},{5,149},{6,102},{7,151},{8,1... | collective-permute-start | bytes 491528 | tf_op jit(solution)/shard_map/ppermute | solution.py:32
  24.9 4.2 %collective-permute-start.4 = (f32[40,8,128]{2,1,0:T(8,128)S(1)}, f32[40,8,128]{2,1,0:T(8,128)S(1)}, u32[]{:S(2)}, u32[]{:S(2)}) collective-permute-start(f32[40,8,128]{2,1,0:T(8,128)S(1)} %get-tuple-element.39), channel_id=1, source_target_pairs={{0,32},{1,17},{2,34},{3,19},{4,36},{5,21},{6,38},{7,23},{8,40},{9,... | collective-permute-start | bytes 491528 | tf_op jit(solution)/shard_map/ppermute | solution.py:32
  27.2 5.5 %collective-permute-start.8 = (f32[40,8,128]{2,1,0:T(8,128)S(1)}, f32[40,8,128]{2,1,0:T(8,128)S(1)}, u32[]{:S(2)}, u32[]{:S(2)}) collective-permute-start(f32[40,8,128]{2,1,0:T(8,128)S(1)} %get-tuple-element.48), channel_id=1, source_target_pairs={{0,96},{1,145},{2,98},{3,147},{4,100},{5,149},{6,102},{7,151},{8,1... | collective-permute-start | bytes 491528 | tf_op jit(solution)/shard_map/ppermute | solution.py:32
  28.5 4.2 %collective-permute-start.9 = (f32[40,8,128]{2,1,0:T(8,128)S(1)}, f32[40,8,128]{2,1,0:T(8,128)S(1)}, u32[]{:S(2)}, u32[]{:S(2)}) collective-permute-start(f32[40,8,128]{2,1,0:T(8,128)S(1)} %get-tuple-element.50), channel_id=1, source_target_pairs={{0,32},{1,17},{2,34},{3,19},{4,36},{5,21},{6,38},{7,23},{8,40},{9,... | collective-permute-start | bytes 491528 | tf_op jit(solution)/shard_map/ppermute | solution.py:32
  32.7 5.8 %collective-permute-start.10 = (f32[40,8,128]{2,1,0:T(8,128)S(1)}, f32[40,8,128]{2,1,0:T(8,128)S(1)}, u32[]{:S(2)}, u32[]{:S(2)}) collective-permute-start(f32[40,8,128]{2,1,0:T(8,128)S(1)} %get-tuple-element.52), channel_id=1, source_target_pairs={{0,128},{1,65},{2,130},{3,67},{4,132},{5,69},{6,134},{7,71},{8,136... | collective-permute-start | bytes 491528 | tf_op jit(solution)/shard_map/ppermute | solution.py:32
  35.7 5.3 %collective-permute-start.11 = (f32[40,8,128]{2,1,0:T(8,128)S(1)}, f32[40,8,128]{2,1,0:T(8,128)S(1)}, u32[]{:S(2)}, u32[]{:S(2)}) collective-permute-start(f32[40,8,128]{2,1,0:T(8,128)S(1)} %get-tuple-element.53), channel_id=1, source_target_pairs={{0,16},{1,33},{2,18},{3,35},{4,20},{5,37},{6,22},{7,39},{8,24},{9,... | collective-permute-start | bytes 491528 | tf_op jit(solution)/shard_map/ppermute | solution.py:32
  36.2 5.7 %collective-permute-start.12 = (f32[40,8,128]{2,1,0:T(8,128)S(1)}, f32[40,8,128]{2,1,0:T(8,128)S(1)}, u32[]{:S(2)}, u32[]{:S(2)}) collective-permute-start(f32[40,8,128]{2,1,0:T(8,128)S(1)} %get-tuple-element.54), channel_id=1, source_target_pairs={{0,144},{1,97},{2,146},{3,99},{4,148},{5,101},{6,150},{7,103},{8,1... | collective-permute-start | bytes 491528 | tf_op jit(solution)/shard_map/ppermute | solution.py:32
  69.2 7.9 %collective-permute-start.13 = (f32[80,8,128]{2,1,0:T(8,128)S(1)}, f32[80,8,128]{2,1,0:T(8,128)S(1)}, u32[]{:S(2)}, u32[]{:S(2)}) collective-permute-start(f32[80,8,128]{2,1,0:T(8,128)S(1)} %bitcast.4), channel_id=1, source_target_pairs={{0,1},{1,0},{2,3},{3,2},{4,5},{5,4},{6,7},{7,6},{8,9},{9,8},{10,11... | collective-permute-start | bytes 983048 | tf_op jit(solution)/shard_map/ppermute | solution.py:32

commit v7 on v6

--- a/solution.py
+++ b/solution.py
@@ -94,54 +94,35 @@
                 target[k, j, n] = tile_of(half, low * UNIT + n)
 
 
-def first_kernel(table_in, amps, blocks, keep, give, acc, table, table_sem, sems, early):
-    count, orbitals = blocks.shape[:2]
-
-    def fetch(block, o=None):
-        if o is None:
-            return pltpu.make_async_copy(amps.at[block], blocks.at[block], sems.at[block])
-        return pltpu.make_async_copy(amps.at[block, o], blocks.at[block, o], early.at[block, o])
-
-    def arrivals(place, act, o=None):
+def first_kernel(table_in, amps, blocks, keep, give, acc, table, order, table_sem, sems):
+    count = blocks.shape[0]
+
+    def fetch(n):
+        block = order[n]
+        return pltpu.make_async_copy(amps.at[block], blocks.at[block], sems.at[n])
+
+    order[0] = 0
+    fetch(0).start()
+    copy = pltpu.make_async_copy(table_in, table, table_sem)
+    copy.start()
+    copy.wait()
+    n = 0
+    for place in range(count):
         block = block_of(place)
         partner = table[block]
         other_place = place_of(partner)
-
-        @pl.when(other_place >= place)
-        def _():
-            act(fetch(block, o))
-
-        @pl.when(other_place > place)
-        def _():
-            act(fetch(partner, o))
-
-    fetch(0, 0).start()
-    copy = pltpu.make_async_copy(table_in, table, table_sem)
-    copy.start()
-    copy.wait()
-    partner = table[0]
-    for o in range(orbitals):
-        if o:
-            fetch(0, o).start()
-
-        @pl.when(partner > 0)
-        def _():
-            fetch(partner, o).start()
-
-    for place in range(1, count):
-        arrivals(place, lambda copy: copy.start())
-
-    add_block(blocks, acc.at[0], keep, give, 0, partner, lambda o: arrivals(0, lambda copy: copy.wait(), o))
-
-    def step(place, carry):
-        arrivals(place, lambda copy: copy.wait())
+        order[n] = block
+        n = n + (other_place >= place).astype(jnp.int32)
+        order[n] = partner
+        n = n + (other_place > place).astype(jnp.int32)
+    for n in range(1, count):
+        fetch(n).start()
+
+    for place in range(4):
+        fetch(2 * place).wait()
+        fetch(2 * place + 1).wait()
         block = block_of(place)
-        add_block(blocks, acc.at[1], keep, give, block, table[block])
-        return carry
-
-    lax.fori_loop(1, 4, step, 0)
-    for place in range(4, count):
-        arrivals(place, lambda copy: copy.wait())
+        add_block(blocks, acc.at[place % 2], keep, give, block, table[block])
 
 
 def second_kernel(table, blocks, keep, give, acc):
@@ -166,7 +147,7 @@
             out_shape=(pltpu.VMEM(amps.shape, amps.dtype), half, half),
             in_specs=[pl.BlockSpec(memory_space=pltpu.HBM)] * 2,
             out_specs=(in_vmem,) * 3,
-            scratch_shapes=[acc, pltpu.SMEM(table.shape, table.dtype), dma, dma(amps.shape[:1]), dma(amps.shape[:2])],
+            scratch_shapes=[acc, *[pltpu.SMEM((n,), table.dtype) for n in (8, 10)], dma, dma((8,))],
             **params,
         )(*(pltpu.with_memory_space_constraint(array, pltpu.HBM) for array in (table, amps)))
     return pl.pallas_call(
@@ -217,34 +198,41 @@
                     sums[2 * (run ^ turn) + low][...] = own[...] + got[...]
 
 
-def layout_kernel(scale, mine, other, out, whole):
+def layout_kernel(scale, own, tiles, *refs):
+    out, rows, sem = refs[-3:]
     core = lax.axis_index("core")
-    whole[pl.ds(core * 2 * UNIT, 2 * UNIT)] = mine[...] * scale
-    whole[pl.ds((1 - core) * 2 * UNIT, 2 * UNIT)] = other[...] * scale
-    for half in range(2):
-        for m in range(FULL):
-            g, l = divmod(m, WIDE)
-            row = 8 * (half * HALF_GROUPS + g)
-            out[0, row : row + 8, 128 * l : 128 * l + 128] = whole[half * 2 * UNIT + m]
-        for g in range(HALF_GROUPS):
-            n, k = divmod(g, 8)
-            tile = whole[half * 2 * UNIT + FULL + n]
-            if k:
-                tile = pltpu.roll(tile, 128 - 16 * k, 1)
-            row = 8 * (half * HALF_GROUPS + g)
-            out[0, row : row + 8, 128 * WIDE : 128 * WIDE + 16] = tile[:, :16]
-
-
-def lay_out(scale, size, *units):
+    half = core if own else 1 - core
+    for m in range(FULL):
+        g, l = divmod(m, WIDE)
+        rows[8 * g : 8 * g + 8, 128 * l : 128 * l + 128] = tiles[m] * scale
+    for g in range(HALF_GROUPS):
+        n, k = divmod(g, 8)
+        tile = tiles[FULL + n] * scale
+        if k:
+            tile = pltpu.roll(tile, 128 - 16 * k, 1)
+        rows[8 * g : 8 * g + 8, 128 * WIDE : 128 * WIDE + 16] = tile[:, :16]
+    count = 8 * HALF_GROUPS
+    copy = pltpu.make_async_copy(rows, out.at[0, pl.ds(pl.multiple_of(half * count, 8), count)], sem)
+    copy.start()
+    copy.wait()
+
+
+def lay_out(scale, size, tiles, begun=None):
+    in_hbm = pl.BlockSpec(memory_space=pltpu.HBM)
+    arrays = [pltpu.with_memory_space_constraint(tiles, pltpu.VMEM)]
+    if begun is not None:
+        arrays.append(pltpu.with_memory_space_constraint(begun, pltpu.HBM))
     return pl.pallas_call(
-        functools.partial(layout_kernel, scale),
-        out_shape=jax.ShapeDtypeStruct((1, size, size), jnp.float32),
-        in_specs=[pl.BlockSpec(memory_space=pltpu.VMEM)] * 2,
-        out_specs=pl.BlockSpec(memory_space=pltpu.VMEM),
-        scratch_shapes=[pltpu.VMEM((4 * UNIT, 8, 128), jnp.float32)],
+        functools.partial(layout_kernel, scale, begun is None),
+        out_shape=pltpu.HBM((1, size, size), jnp.float32),
+        in_specs=[pl.BlockSpec(memory_space=pltpu.VMEM), in_hbm][: len(arrays)],
+        out_specs=in_hbm,
+        scratch_shapes=[pltpu.VMEM((8 * HALF_GROUPS, size), jnp.float32), pltpu.SemaphoreType.DMA],
+        input_output_aliases={} if begun is None else {1: 0},
         compiler_params=pltpu.CompilerParams(vmem_limit_bytes=8 << 20),
+        cost_estimate=pl.CostEstimate(flops=80000, bytes_accessed=700000, transcendentals=0),
         name="lay_out",
-    )(*(pltpu.with_memory_space_constraint(unit, pltpu.VMEM) for unit in units))
+    )(*arrays)
 
 
 def on_device(amps, conserve):
@@ -271,7 +259,8 @@
     eighth = jnp.sum(parts, axis=0, keepdims=True)
     mine = lax.all_to_all(jnp.broadcast_to(eighth, (16, *parts.shape[1:])), ("x_lo", "z"), 0, 0, tiled=True)
     mine = mine.reshape(2 * UNIT, 8, 128)
-    return lay_out(scale, amps.shape[4], mine, send(mine, across))
+    other = send(mine, across)
+    return lay_out(scale, amps.shape[4], other, lay_out(scale, amps.shape[4], mine))
 
 
 def solution(mesh):

time: 78.3 us -> 78 us (level)
    pallas_call x1 -> x2, Pallas kernels: 1.03 us -> 1.7 us  [lay_out(): pl.pallas_call(functools.partial(layout_kernel, scale, begun is None), ou...]
  transfers between devices with their start and end apart: 14 -> 14, of which waited for: 11 -> 11; matrix products, arithmetic and copies ran while one was open for 0% -> 0% of each run, Pallas kernels for 6% -> 8%
where the time goes in v7:
time: 78 us; the launch traced here: 77.9 us
  blocking collectives  27 us (35%)
  starting transfers between devices  19.1 us (24%)
  waiting for transfers between devices  17.1 us (22%)
  Pallas kernels  14.3 us (18%)
    ppermute x14, starting transfers between devices, send(): return lax.ppermute(value, FINE, pairs(move))  19.1 us
    ppermute x14, waiting for transfers between devices, send(): return lax.ppermute(value, FINE, pairs(move))  17.1 us
    all_to_all x1, blocking collectives, on_device(): lax.all_to_all(third.reshape(8, UNIT // 8, 8, 128), 'z', 0, 0, tiled=True)  16.3 us
    all_to_all x1, blocking collectives, on_device(): lax.all_to_all(jnp.broadcast_to(eighth, (16, *parts.shape[1:])), ('x_lo',...  10.8 us
    pallas_call x1, Pallas kernels, densities(): pl.pallas_call(first_kernel, out_shape=(pltpu.VMEM(amps.shape, amps.dtype...  7.52 us
    pallas_call x1, Pallas kernels, densities(): pl.pallas_call(second_kernel, out_shape=(half, half), in_specs=[pl.BlockS...  4.63 us
    pallas_call x2, Pallas kernels, lay_out(): pl.pallas_call(functools.partial(layout_kernel, scale, begun is None), ou...  1.7 us
  transfers between devices with their start and end apart: 14, of which 11 were waited for; matrix products, arithmetic and copies ran while one was open for 0% of the time, Pallas kernels for 8%

profile of v7, /device:TPU:1, one launch (start us, length us, event | category | flops | bytes accessed | tf_op | source)
XLA Modules:
  0.0 77.9 jit_solution(14445680250012620767)
XLA Ops:
  0.0 7.5 %densities.2 = (bf16[8,4,400,400]{3,2,1,0:T(8,128)(2,1)S(1)}, f32[4,2,40,8,128]{4,3,2,1,0:T(8,128)S(1)}, f32[4,2,40,8,128]{4,3,2,1,0:T(8,128)S(1)}) custom-call(s32[8]{0:T(128)} %bitcast.6, bf16[8,4,400,400]{3,2,1,0:T(8,128)(2,1)} %bitcast.9), custom_call_target="tpu_custom_call" | custom-call | flops 4294967296 | bytes 13631488 | tf_op jit(solution)/shard_map/densities/pallas_call | solution.py:145
  7.5 3.3 %collective-permute-start = (f32[4,2,40,8,128]{4,3,2,1,0:T(8,128)S(1)}, f32[4,2,40,8,128]{4,3,2,1,0:T(8,128)S(1)}, u32[]{:S(2)}, u32[]{:S(2)}) collective-permute-start(f32[4,2,40,8,128]{4,3,2,1,0:T(8,128)S(1)} %get-tuple-element.31), channel_id=1, source_target_pairs={{0,1},{1,0},{2,3},{3,2},{4,5},{5,4},{6,7},{7,6},{8,9},{9,8},{10,11... | collective-permute-start | bytes 3932168 | tf_op jit(solution)/shard_map/ppermute | solution.py:32
  10.9 4.6 %densities.3 = (f32[4,2,40,8,128]{4,3,2,1,0:T(8,128)S(1)}, f32[4,2,40,8,128]{4,3,2,1,0:T(8,128)S(1)}) custom-call(s32[8]{0:T(128)S(1)} %bitcast.7, bf16[8,4,400,400]{3,2,1,0:T(8,128)(2,1)S(1)} %get-tuple-element.40.blocks), custom_call_target="tpu_custom_call" | custom-call | flops 4294967296 | bytes 13631488 | tf_op jit(solution)/shard_map/densities/pallas_call | solution.py:153
  15.5 0.1 collective-permute-start.5
  15.6 0.1 add_halves.2
  15.7 0.1 collective-permute-start.1
  15.8 1.3 %collective-permute-start.2 = (f32[2,40,8,128]{3,2,1,0:T(8,128)S(1)}, f32[2,40,8,128]{3,2,1,0:T(8,128)S(1)}, u32[]{:S(2)}, u32[]{:S(2)}) collective-permute-start(f32[2,40,8,128]{3,2,1,0:T(8,128)S(1)} %get-tuple-element.35), channel_id=1, source_target_pairs={{0,96},{1,145},{2,98},{3,147},{4,100},{5,149},{6,102},{7,151},{8,1... | collective-permute-start | bytes 983048 | tf_op jit(solution)/shard_map/ppermute | solution.py:32
  17.1 1.5 %collective-permute-done.5.got = f32[4,2,40,8,128]{4,3,2,1,0:T(8,128)S(1)} collective-permute-done((f32[4,2,40,8,128]{4,3,2,1,0:T(8,128)S(1)}, f32[4,2,40,8,128]{4,3,2,1,0:T(8,128)S(1)}, u32[]{:S(2)}, u32[]{:S(2)}) %collective-permute-start.5) | collective-permute-done | bytes 1310752 | tf_op jit(solution)/shard_map/ppermute | solution.py:32
  18.6 0.1 add_halves.3
  18.7 0.1 collective-permute-start.6
  18.8 1.3 %collective-permute-start.7 = (f32[2,40,8,128]{3,2,1,0:T(8,128)S(1)}, f32[2,40,8,128]{3,2,1,0:T(8,128)S(1)}, u32[]{:S(2)}, u32[]{:S(2)}) collective-permute-start(f32[2,40,8,128]{3,2,1,0:T(8,128)S(1)} %get-tuple-element.46), channel_id=1, source_target_pairs={{0,96},{1,145},{2,98},{3,147},{4,100},{5,149},{6,102},{7,151},{8,1... | collective-permute-start | bytes 983048 | tf_op jit(solution)/shard_map/ppermute | solution.py:32
  20.1 1.9 %collective-permute-done.1.got_a = f32[2,40,8,128]{3,2,1,0:T(8,128)S(1)} collective-permute-done((f32[2,40,8,128]{3,2,1,0:T(8,128)S(1)}, f32[2,40,8,128]{3,2,1,0:T(8,128)S(1)}, u32[]{:S(2)}, u32[]{:S(2)}) %collective-permute-start.1) | collective-permute-done | bytes 327712 | tf_op jit(solution)/shard_map/ppermute | solution.py:32
  22.0 1.3 %collective-permute-done.2.got_b = f32[2,40,8,128]{3,2,1,0:T(8,128)S(1)} collective-permute-done((f32[2,40,8,128]{3,2,1,0:T(8,128)S(1)}, f32[2,40,8,128]{3,2,1,0:T(8,128)S(1)}, u32[]{:S(2)}, u32[]{:S(2)}) %collective-permute-start.2) | collective-permute-done | bytes 327712 | tf_op jit(solution)/shard_map/ppermute | solution.py:32
  23.4 1.3 %collective-permute-start.3 = (f32[40,8,128]{2,1,0:T(8,128)S(1)}, f32[40,8,128]{2,1,0:T(8,128)S(1)}, u32[]{:S(2)}, u32[]{:S(2)}) collective-permute-start(f32[40,8,128]{2,1,0:T(8,128)S(1)} %get-tuple-element.37), channel_id=1, source_target_pairs={{0,96},{1,145},{2,98},{3,147},{4,100},{5,149},{6,102},{7,151},{8,1... | collective-permute-start | bytes 491528 | tf_op jit(solution)/shard_map/ppermute | solution.py:32
  24.7 0.9 %collective-permute-done.6.got_a = f32[2,40,8,128]{3,2,1,0:T(8,128)S(1)} collective-permute-done((f32[2,40,8,128]{3,2,1,0:T(8,128)S(1)}, f32[2,40,8,128]{3,2,1,0:T(8,128)S(1)}, u32[]{:S(2)}, u32[]{:S(2)}) %collective-permute-start.6) | collective-permute-done | bytes 327712 | tf_op jit(solution)/shard_map/ppermute | solution.py:32
  25.5 1.3 %collective-permute-done.7.got_b = f32[2,40,8,128]{3,2,1,0:T(8,128)S(1)} collective-permute-done((f32[2,40,8,128]{3,2,1,0:T(8,128)S(1)}, f32[2,40,8,128]{3,2,1,0:T(8,128)S(1)}, u32[]{:S(2)}, u32[]{:S(2)}) %collective-permute-start.7) | collective-permute-done | bytes 327712 | tf_op jit(solution)/shard_map/ppermute | solution.py:32
  26.9 1.3 %collective-permute-start.8 = (f32[40,8,128]{2,1,0:T(8,128)S(1)}, f32[40,8,128]{2,1,0:T(8,128)S(1)}, u32[]{:S(2)}, u32[]{:S(2)}) collective-permute-start(f32[40,8,128]{2,1,0:T(8,128)S(1)} %get-tuple-element.48), channel_id=1, source_target_pairs={{0,96},{1,145},{2,98},{3,147},{4,100},{5,149},{6,102},{7,151},{8,1... | collective-permute-start | bytes 491528 | tf_op jit(solution)/shard_map/ppermute | solution.py:32
  28.2 0.7 collective-permute-done.3.refs_1_
  28.9 3.5 %collective-permute-done.8.refs_5_ = f32[40,8,128]{2,1,0:T(8,128)S(1)} collective-permute-done((f32[40,8,128]{2,1,0:T(8,128)S(1)}, f32[40,8,128]{2,1,0:T(8,128)S(1)}, u32[]{:S(2)}, u32[]{:S(2)}) %collective-permute-start.8) | collective-permute-done | bytes 163872 | tf_op jit(solution)/shard_map/ppermute | solution.py:32
  32.4 0.1 add_ring.1
  32.5 3.0 %collective-permute-start.10 = (f32[40,8,128]{2,1,0:T(8,128)S(1)}, f32[40,8,128]{2,1,0:T(8,128)S(1)}, u32[]{:S(2)}, u32[]{:S(2)}) collective-permute-start(f32[40,8,128]{2,1,0:T(8,128)S(1)} %get-tuple-element.52), channel_id=1, source_target_pairs={{0,128},{1,65},{2,130},{3,67},{4,132},{5,69},{6,134},{7,71},{8,136... | collective-permute-start | bytes 491528 | tf_op jit(solution)/shard_map/ppermute | solution.py:32
  35.4 0.7 collective-permute-start.11
  36.1 0.1 collective-permute-start.12
  36.2 2.0 %collective-permute-done.10 = f32[40,8,128]{2,1,0:T(8,128)S(1)} collective-permute-done((f32[40,8,128]{2,1,0:T(8,128)S(1)}, f32[40,8,128]{2,1,0:T(8,128)S(1)}, u32[]{:S(2)}, u32[]{:S(2)}) %collective-permute-start.10) | collective-permute-done | bytes 163872 | tf_op jit(solution)/shard_map/ppermute | solution.py:32
  38.2 2.7 %collective-permute-done.11 = f32[40,8,128]{2,1,0:T(8,128)S(1)} collective-permute-done((f32[40,8,128]{2,1,0:T(8,128)S(1)}, f32[40,8,128]{2,1,0:T(8,128)S(1)}, u32[]{:S(2)}, u32[]{:S(2)}) %collective-permute-start.11) | collective-permute-done | bytes 163872 | tf_op jit(solution)/shard_map/ppermute | solution.py:32
  40.9 0.9 %collective-permute-done.12 = f32[40,8,128]{2,1,0:T(8,128)S(1)} collective-permute-done((f32[40,8,128]{2,1,0:T(8,128)S(1)}, f32[40,8,128]{2,1,0:T(8,128)S(1)}, u32[]{:S(2)}, u32[]{:S(2)}) %collective-permute-start.12) | collective-permute-done | bytes 163872 | tf_op jit(solution)/shard_map/ppermute | solution.py:32
  41.9 16.3 %all_to_all.10 = f32[8,5,8,128]{3,2,1,0:T(8,128)S(1)} all-to-all(f32[8,5,8,128]{3,2,1,0:T(8,128)S(1)} %bitcast.8), channel_id=1, replica_groups=mesh['x_hi'=2,'y'=4,'x_lo'=2,'z'=8,'core'=2] {'z'}, dimensions={0} | all-to-all | bytes 327680 | tf_op jit(solution)/shard_map/all_to_all | solution.py:258
  58.2 10.8 %all_to_all.11 = f32[16,5,8,128]{3,2,1,0:T(8,128)S(1)} all-to-all(f32[16,5,8,128]{3,2,1,0:T(8,128)S(1)} %broadcast_in_dim.2), channel_id=1, replica_groups=mesh['x_hi'=2,'y'=4,'x_lo'=2,'z'=8,'core'=2] {'x_lo','z'}, dimensions={0} | all-to-all | bytes 655360 | tf_op jit(solution)/shard_map/all_to_all | solution.py:260
  68.9 6.7 %collective-permute-start.13 = (f32[80,8,128]{2,1,0:T(8,128)S(1)}, f32[80,8,128]{2,1,0:T(8,128)S(1)}, u32[]{:S(2)}, u32[]{:S(2)}) collective-permute-start(f32[80,8,128]{2,1,0:T(8,128)S(1)} %bitcast.4), channel_id=1, source_target_pairs={{0,1},{1,0},{2,3},{3,2},{4,5},{5,4},{6,7},{7,6},{8,9},{9,8},{10,11... | collective-permute-start | bytes 983048 | tf_op jit(solution)/shard_map/ppermute | solution.py:32
  75.6 0.8 %lay_out.2.refs_0_ = f32[1,400,400]{2,1,0:T(8,128)} custom-call(f32[80,8,128]{2,1,0:T(8,128)S(1)} %bitcast.5), custom_call_target="tpu_custom_call" | custom-call | flops 80000 | bytes 700000 | tf_op jit(solution)/shard_map/lay_out/pallas_call | solution.py:225
  76.5 0.4 collective-permute-done.13.tiles
  76.9 0.8 %lay_out.3 = f32[1,400,400]{2,1,0:T(8,128)} custom-call(f32[80,8,128]{2,1,0:T(8,128)S(1)} %collective-permute-done.13.tiles, f32[1,400,400]{2,1,0:T(8,128)} %lay_out.2.refs_0_), custom_call_target="tpu_custom_call", output_to_operand_aliasing={{}: (1, {})} | custom-call | flops 80000 | bytes 700000 | tf_op jit(solution)/shard_map/lay_out/pallas_call | solution.py:225
  (12 shorter events, 0.2 us)
Async XLA Ops:
  0.0 10.9 %copy-start = (s32[1,1,8]{2,1,0:T(1,128)S(1)}, s32[1,1,8]{2,1,0:T(1,128)}, u32[]{:S(2)}) copy-start(s32[1,1,8]{2,1,0:T(1,128)} %param.3) | copy-start | bytes 100
  7.5 8.0 %collective-permute-start = (f32[4,2,40,8,128]{4,3,2,1,0:T(8,128)S(1)}, f32[4,2,40,8,128]{4,3,2,1,0:T(8,128)S(1)}, u32[]{:S(2)}, u32[]{:S(2)}) collective-permute-start(f32[4,2,40,8,128]{4,3,2,1,0:T(8,128)S(1)} %get-tuple-element.31), channel_id=1, source_target_pairs={{0,1},{1,0},{2,3},{3,2},{4,5},{5,4},{6,7},{7,6},{8,9},{9,8},{10,11... | collective-permute-start | bytes 3932168 | tf_op jit(solution)/shard_map/ppermute | solution.py:32
  15.5 3.1 %collective-permute-start.5 = (f32[4,2,40,8,128]{4,3,2,1,0:T(8,128)S(1)}, f32[4,2,40,8,128]{4,3,2,1,0:T(8,128)S(1)}, u32[]{:S(2)}, u32[]{:S(2)}) collective-permute-start(f32[4,2,40,8,128]{4,3,2,1,0:T(8,128)S(1)} %get-tuple-element.42), channel_id=1, source_target_pairs={{0,1},{1,0},{2,3},{3,2},{4,5},{5,4},{6,7},{7,6},{8,9},{9,8},{10,11... | collective-permute-start | bytes 3932168 | tf_op jit(solution)/shard_map/ppermute | solution.py:32
  15.7 6.3 %collective-permute-start.1 = (f32[2,40,8,128]{3,2,1,0:T(8,128)S(1)}, f32[2,40,8,128]{3,2,1,0:T(8,128)S(1)}, u32[]{:S(2)}, u32[]{:S(2)}) collective-permute-start(f32[2,40,8,128]{3,2,1,0:T(8,128)S(1)} %get-tuple-element.33), channel_id=1, source_target_pairs={{0,32},{1,17},{2,34},{3,19},{4,36},{5,21},{6,38},{7,23},{8,40},{9,... | collective-permute-start | bytes 983048 | tf_op jit(solution)/shard_map/ppermute | solution.py:32
  15.8 7.5 %collective-permute-start.2 = (f32[2,40,8,128]{3,2,1,0:T(8,128)S(1)}, f32[2,40,8,128]{3,2,1,0:T(8,128)S(1)}, u32[]{:S(2)}, u32[]{:S(2)}) collective-permute-start(f32[2,40,8,128]{3,2,1,0:T(8,128)S(1)} %get-tuple-element.35), channel_id=1, source_target_pairs={{0,96},{1,145},{2,98},{3,147},{4,100},{5,149},{6,102},{7,151},{8,1... | collective-permute-start | bytes 983048 | tf_op jit(solution)/shard_map/ppermute | solution.py:32
  18.7 6.8 %collective-permute-start.6 = (f32[2,40,8,128]{3,2,1,0:T(8,128)S(1)}, f32[2,40,8,128]{3,2,1,0:T(8,128)S(1)}, u32[]{:S(2)}, u32[]{:S(2)}) collective-permute-start(f32[2,40,8,128]{3,2,1,0:T(8,128)S(1)} %get-tuple-element.44), channel_id=1, source_target_pairs={{0,32},{1,17},{2,34},{3,19},{4,36},{5,21},{6,38},{7,23},{8,40},{9,... | collective-permute-start | bytes 983048 | tf_op jit(solution)/shard_map/ppermute | solution.py:32
  18.8 8.0 %collective-permute-start.7 = (f32[2,40,8,128]{3,2,1,0:T(8,128)S(1)}, f32[2,40,8,128]{3,2,1,0:T(8,128)S(1)}, u32[]{:S(2)}, u32[]{:S(2)}) collective-permute-start(f32[2,40,8,128]{3,2,1,0:T(8,128)S(1)} %get-tuple-element.46), channel_id=1, source_target_pairs={{0,96},{1,145},{2,98},{3,147},{4,100},{5,149},{6,102},{7,151},{8,1... | collective-permute-start | bytes 983048 | tf_op jit(solution)/shard_map/ppermute | solution.py:32
  23.4 5.5 %collective-permute-start.3 = (f32[40,8,128]{2,1,0:T(8,128)S(1)}, f32[40,8,128]{2,1,0:T(8,128)S(1)}, u32[]{:S(2)}, u32[]{:S(2)}) collective-permute-start(f32[40,8,128]{2,1,0:T(8,128)S(1)} %get-tuple-element.37), channel_id=1, source_target_pairs={{0,96},{1,145},{2,98},{3,147},{4,100},{5,149},{6,102},{7,151},{8,1... | collective-permute-start | bytes 491528 | tf_op jit(solution)/shard_map/ppermute | solution.py:32
  24.7 4.2 %collective-permute-start.4 = (f32[40,8,128]{2,1,0:T(8,128)S(1)}, f32[40,8,128]{2,1,0:T(8,128)S(1)}, u32[]{:S(2)}, u32[]{:S(2)}) collective-permute-start(f32[40,8,128]{2,1,0:T(8,128)S(1)} %get-tuple-element.39), channel_id=1, source_target_pairs={{0,32},{1,17},{2,34},{3,19},{4,36},{5,21},{6,38},{7,23},{8,40},{9,... | collective-permute-start | bytes 491528 | tf_op jit(solution)/shard_map/ppermute | solution.py:32
  26.9 5.5 %collective-permute-start.8 = (f32[40,8,128]{2,1,0:T(8,128)S(1)}, f32[40,8,128]{2,1,0:T(8,128)S(1)}, u32[]{:S(2)}, u32[]{:S(2)}) collective-permute-start(f32[40,8,128]{2,1,0:T(8,128)S(1)} %get-tuple-element.48), channel_id=1, source_target_pairs={{0,96},{1,145},{2,98},{3,147},{4,100},{5,149},{6,102},{7,151},{8,1... | collective-permute-start | bytes 491528 | tf_op jit(solution)/shard_map/ppermute | solution.py:32
  28.2 4.2 %collective-permute-start.9 = (f32[40,8,128]{2,1,0:T(8,128)S(1)}, f32[40,8,128]{2,1,0:T(8,128)S(1)}, u32[]{:S(2)}, u32[]{:S(2)}) collective-permute-start(f32[40,8,128]{2,1,0:T(8,128)S(1)} %get-tuple-element.50), channel_id=1, source_target_pairs={{0,32},{1,17},{2,34},{3,19},{4,36},{5,21},{6,38},{7,23},{8,40},{9,... | collective-permute-start | bytes 491528 | tf_op jit(solution)/shard_map/ppermute | solution.py:32
  32.5 5.8 %collective-permute-start.10 = (f32[40,8,128]{2,1,0:T(8,128)S(1)}, f32[40,8,128]{2,1,0:T(8,128)S(1)}, u32[]{:S(2)}, u32[]{:S(2)}) collective-permute-start(f32[40,8,128]{2,1,0:T(8,128)S(1)} %get-tuple-element.52), channel_id=1, source_target_pairs={{0,128},{1,65},{2,130},{3,67},{4,132},{5,69},{6,134},{7,71},{8,136... | collective-permute-start | bytes 491528 | tf_op jit(solution)/shard_map/ppermute | solution.py:32
  35.4 5.4 %collective-permute-start.11 = (f32[40,8,128]{2,1,0:T(8,128)S(1)}, f32[40,8,128]{2,1,0:T(8,128)S(1)}, u32[]{:S(2)}, u32[]{:S(2)}) collective-permute-start(f32[40,8,128]{2,1,0:T(8,128)S(1)} %get-tuple-element.53), channel_id=1, source_target_pairs={{0,16},{1,33},{2,18},{3,35},{4,20},{5,37},{6,22},{7,39},{8,24},{9,... | collective-permute-start | bytes 491528 | tf_op jit(solution)/shard_map/ppermute | solution.py:32
  36.1 5.7 %collective-permute-start.12 = (f32[40,8,128]{2,1,0:T(8,128)S(1)}, f32[40,8,128]{2,1,0:T(8,128)S(1)}, u32[]{:S(2)}, u32[]{:S(2)}) collective-permute-start(f32[40,8,128]{2,1,0:T(8,128)S(1)} %get-tuple-element.54), channel_id=1, source_target_pairs={{0,144},{1,97},{2,146},{3,99},{4,148},{5,101},{6,150},{7,103},{8,1... | collective-permute-start | bytes 491528 | tf_op jit(solution)/shard_map/ppermute | solution.py:32
  68.9 7.9 %collective-permute-start.13 = (f32[80,8,128]{2,1,0:T(8,128)S(1)}, f32[80,8,128]{2,1,0:T(8,128)S(1)}, u32[]{:S(2)}, u32[]{:S(2)}) collective-permute-start(f32[80,8,128]{2,1,0:T(8,128)S(1)} %bitcast.4), channel_id=1, source_target_pairs={{0,1},{1,0},{2,3},{3,2},{4,5},{5,4},{6,7},{7,6},{8,9},{9,8},{10,11... | collective-permute-start | bytes 983048 | tf_op jit(solution)/shard_map/ppermute | solution.py:32

commit v8 on v7

--- a/solution.py
+++ b/solution.py
@@ -202,12 +202,18 @@
     out, rows, sem = refs[-3:]
     core = lax.axis_index("core")
     half = core if own else 1 - core
+
+    def lies(m):
+        unit, n = divmod(m, UNIT)
+        z, n = divmod(n, UNIT // 8)
+        return (z * 2 + unit) * (UNIT // 8) + n
+
     for m in range(FULL):
         g, l = divmod(m, WIDE)
-        rows[8 * g : 8 * g + 8, 128 * l : 128 * l + 128] = tiles[m] * scale
+        rows[8 * g : 8 * g + 8, 128 * l : 128 * l + 128] = tiles[lies(m)] * scale
     for g in range(HALF_GROUPS):
         n, k = divmod(g, 8)
-        tile = tiles[FULL + n] * scale
+        tile = tiles[lies(FULL + n)] * scale
         if k:
             tile = pltpu.roll(tile, 128 - 16 * k, 1)
         rows[8 * g : 8 * g + 8, 128 * WIDE : 128 * WIDE + 16] = tile[:, :16]
@@ -257,7 +263,7 @@
     third = (second[0] + came[0]) + (came[1] + came[2])
     parts = lax.all_to_all(third.reshape(8, UNIT // 8, 8, 128), "z", 0, 0, tiled=True)
     eighth = jnp.sum(parts, axis=0, keepdims=True)
-    mine = lax.all_to_all(jnp.broadcast_to(eighth, (16, *parts.shape[1:])), ("x_lo", "z"), 0, 0, tiled=True)
+    mine = lax.all_to_all(jnp.broadcast_to(eighth, (16, *parts.shape[1:])), ("z", "x_lo"), 0, 0, tiled=True)
     mine = mine.reshape(2 * UNIT, 8, 128)
     other = send(mine, across)
     return lay_out(scale, amps.shape[4], other, lay_out(scale, amps.shape[4], mine))

time: 78 us -> 80 us (1.026)
  blocking collectives: 27 us -> 29 us
    all_to_all x1, blocking collectives: 10.8 us -> 12.8 us  [on_device(): lax.all_to_all(jnp.broadcast_to(eighth, (16, *parts.shape[1:])), ('z', 'x...]
  transfers between devices with their start and end apart: 14 -> 14, of which waited for: 11 -> 11; matrix products, arithmetic and copies ran while one was open for 0% -> 0% of each run, Pallas kernels for 8% -> 7%
where the time goes in v8:
time: 80 us; the launch traced here: 79.8 us
  blocking collectives  29 us (36%)
  starting transfers between devices  19.1 us (24%)
  waiting for transfers between devices  17.1 us (21%)
  Pallas kernels  14.3 us (18%)
    ppermute x14, starting transfers between devices, send(): return lax.ppermute(value, FINE, pairs(move))  19.1 us
    ppermute x14, waiting for transfers between devices, send(): return lax.ppermute(value, FINE, pairs(move))  17.1 us
    all_to_all x1, blocking collectives, on_device(): lax.all_to_all(third.reshape(8, UNIT // 8, 8, 128), 'z', 0, 0, tiled=True)  16.3 us
    all_to_all x1, blocking collectives, on_device(): lax.all_to_all(jnp.broadcast_to(eighth, (16, *parts.shape[1:])), ('z', 'x...  12.8 us
    pallas_call x1, Pallas kernels, densities(): pl.pallas_call(first_kernel, out_shape=(pltpu.VMEM(amps.shape, amps.dtype...  7.52 us
    pallas_call x1, Pallas kernels, densities(): pl.pallas_call(second_kernel, out_shape=(half, half), in_specs=[pl.BlockS...  4.63 us
    pallas_call x2, Pallas kernels, lay_out(): pl.pallas_call(functools.partial(layout_kernel, scale, begun is None), ou...  1.7 us
  transfers between devices with their start and end apart: 14, of which 11 were waited for; matrix products, arithmetic and copies ran while one was open for 0% of the time, Pallas kernels for 7%

profile of v8, /device:TPU:1, one launch (start us, length us, event | category | flops | bytes accessed | tf_op | source)
XLA Modules:
  0.0 79.8 jit_solution(10989355998562260491)
XLA Ops:
  0.0 7.5 %densities.2 = (bf16[8,4,400,400]{3,2,1,0:T(8,128)(2,1)S(1)}, f32[4,2,40,8,128]{4,3,2,1,0:T(8,128)S(1)}, f32[4,2,40,8,128]{4,3,2,1,0:T(8,128)S(1)}) custom-call(s32[8]{0:T(128)} %bitcast.6, bf16[8,4,400,400]{3,2,1,0:T(8,128)(2,1)} %bitcast.9), custom_call_target="tpu_custom_call" | custom-call | flops 4294967296 | bytes 13631488 | tf_op jit(solution)/shard_map/densities/pallas_call | solution.py:145
  7.5 3.3 %collective-permute-start = (f32[4,2,40,8,128]{4,3,2,1,0:T(8,128)S(1)}, f32[4,2,40,8,128]{4,3,2,1,0:T(8,128)S(1)}, u32[]{:S(2)}, u32[]{:S(2)}) collective-permute-start(f32[4,2,40,8,128]{4,3,2,1,0:T(8,128)S(1)} %get-tuple-element.31), channel_id=1, source_target_pairs={{0,1},{1,0},{2,3},{3,2},{4,5},{5,4},{6,7},{7,6},{8,9},{9,8},{10,11... | collective-permute-start | bytes 3932168 | tf_op jit(solution)/shard_map/ppermute | solution.py:32
  10.9 4.6 %densities.3 = (f32[4,2,40,8,128]{4,3,2,1,0:T(8,128)S(1)}, f32[4,2,40,8,128]{4,3,2,1,0:T(8,128)S(1)}) custom-call(s32[8]{0:T(128)S(1)} %bitcast.7, bf16[8,4,400,400]{3,2,1,0:T(8,128)(2,1)S(1)} %get-tuple-element.40.blocks), custom_call_target="tpu_custom_call" | custom-call | flops 4294967296 | bytes 13631488 | tf_op jit(solution)/shard_map/densities/pallas_call | solution.py:153
  15.5 0.1 collective-permute-start.5
  15.6 0.1 add_halves.2
  15.7 0.1 collective-permute-start.1
  15.8 1.3 %collective-permute-start.2 = (f32[2,40,8,128]{3,2,1,0:T(8,128)S(1)}, f32[2,40,8,128]{3,2,1,0:T(8,128)S(1)}, u32[]{:S(2)}, u32[]{:S(2)}) collective-permute-start(f32[2,40,8,128]{3,2,1,0:T(8,128)S(1)} %get-tuple-element.35), channel_id=1, source_target_pairs={{0,96},{1,145},{2,98},{3,147},{4,100},{5,149},{6,102},{7,151},{8,1... | collective-permute-start | bytes 983048 | tf_op jit(solution)/shard_map/ppermute | solution.py:32
  17.1 1.5 %collective-permute-done.5.got = f32[4,2,40,8,128]{4,3,2,1,0:T(8,128)S(1)} collective-permute-done((f32[4,2,40,8,128]{4,3,2,1,0:T(8,128)S(1)}, f32[4,2,40,8,128]{4,3,2,1,0:T(8,128)S(1)}, u32[]{:S(2)}, u32[]{:S(2)}) %collective-permute-start.5) | collective-permute-done | bytes 1310752 | tf_op jit(solution)/shard_map/ppermute | solution.py:32
  18.6 0.1 add_halves.3
  18.7 0.1 collective-permute-start.6
  18.8 1.3 %collective-permute-start.7 = (f32[2,40,8,128]{3,2,1,0:T(8,128)S(1)}, f32[2,40,8,128]{3,2,1,0:T(8,128)S(1)}, u32[]{:S(2)}, u32[]{:S(2)}) collective-permute-start(f32[2,40,8,128]{3,2,1,0:T(8,128)S(1)} %get-tuple-element.46), channel_id=1, source_target_pairs={{0,96},{1,145},{2,98},{3,147},{4,100},{5,149},{6,102},{7,151},{8,1... | collective-permute-start | bytes 983048 | tf_op jit(solution)/shard_map/ppermute | solution.py:32
  20.1 1.9 %collective-permute-done.1.got_a = f32[2,40,8,128]{3,2,1,0:T(8,128)S(1)} collective-permute-done((f32[2,40,8,128]{3,2,1,0:T(8,128)S(1)}, f32[2,40,8,128]{3,2,1,0:T(8,128)S(1)}, u32[]{:S(2)}, u32[]{:S(2)}) %collective-permute-start.1) | collective-permute-done | bytes 327712 | tf_op jit(solution)/shard_map/ppermute | solution.py:32
  22.0 1.3 %collective-permute-done.2.got_b = f32[2,40,8,128]{3,2,1,0:T(8,128)S(1)} collective-permute-done((f32[2,40,8,128]{3,2,1,0:T(8,128)S(1)}, f32[2,40,8,128]{3,2,1,0:T(8,128)S(1)}, u32[]{:S(2)}, u32[]{:S(2)}) %collective-permute-start.2) | collective-permute-done | bytes 327712 | tf_op jit(solution)/shard_map/ppermute | solution.py:32
  23.4 1.3 %collective-permute-start.3 = (f32[40,8,128]{2,1,0:T(8,128)S(1)}, f32[40,8,128]{2,1,0:T(8,128)S(1)}, u32[]{:S(2)}, u32[]{:S(2)}) collective-permute-start(f32[40,8,128]{2,1,0:T(8,128)S(1)} %get-tuple-element.37), channel_id=1, source_target_pairs={{0,96},{1,145},{2,98},{3,147},{4,100},{5,149},{6,102},{7,151},{8,1... | collective-permute-start | bytes 491528 | tf_op jit(solution)/shard_map/ppermute | solution.py:32
  24.7 0.9 %collective-permute-done.6.got_a = f32[2,40,8,128]{3,2,1,0:T(8,128)S(1)} collective-permute-done((f32[2,40,8,128]{3,2,1,0:T(8,128)S(1)}, f32[2,40,8,128]{3,2,1,0:T(8,128)S(1)}, u32[]{:S(2)}, u32[]{:S(2)}) %collective-permute-start.6) | collective-permute-done | bytes 327712 | tf_op jit(solution)/shard_map/ppermute | solution.py:32
  25.5 1.3 %collective-permute-done.7.got_b = f32[2,40,8,128]{3,2,1,0:T(8,128)S(1)} collective-permute-done((f32[2,40,8,128]{3,2,1,0:T(8,128)S(1)}, f32[2,40,8,128]{3,2,1,0:T(8,128)S(1)}, u32[]{:S(2)}, u32[]{:S(2)}) %collective-permute-start.7) | collective-permute-done | bytes 327712 | tf_op jit(solution)/shard_map/ppermute | solution.py:32
  26.9 1.3 %collective-permute-start.8 = (f32[40,8,128]{2,1,0:T(8,128)S(1)}, f32[40,8,128]{2,1,0:T(8,128)S(1)}, u32[]{:S(2)}, u32[]{:S(2)}) collective-permute-start(f32[40,8,128]{2,1,0:T(8,128)S(1)} %get-tuple-element.48), channel_id=1, source_target_pairs={{0,96},{1,145},{2,98},{3,147},{4,100},{5,149},{6,102},{7,151},{8,1... | collective-permute-start | bytes 491528 | tf_op jit(solution)/shard_map/ppermute | solution.py:32
  28.2 0.7 collective-permute-done.3.refs_1_
  28.9 3.5 %collective-permute-done.8.refs_5_ = f32[40,8,128]{2,1,0:T(8,128)S(1)} collective-permute-done((f32[40,8,128]{2,1,0:T(8,128)S(1)}, f32[40,8,128]{2,1,0:T(8,128)S(1)}, u32[]{:S(2)}, u32[]{:S(2)}) %collective-permute-start.8) | collective-permute-done | bytes 163872 | tf_op jit(solution)/shard_map/ppermute | solution.py:32
  32.4 0.1 add_ring.1
  32.5 3.0 %collective-permute-start.10 = (f32[40,8,128]{2,1,0:T(8,128)S(1)}, f32[40,8,128]{2,1,0:T(8,128)S(1)}, u32[]{:S(2)}, u32[]{:S(2)}) collective-permute-start(f32[40,8,128]{2,1,0:T(8,128)S(1)} %get-tuple-element.52), channel_id=1, source_target_pairs={{0,128},{1,65},{2,130},{3,67},{4,132},{5,69},{6,134},{7,71},{8,136... | collective-permute-start | bytes 491528 | tf_op jit(solution)/shard_map/ppermute | solution.py:32
  35.4 0.7 collective-permute-start.11
  36.1 0.1 collective-permute-start.12
  36.2 2.0 %collective-permute-done.10 = f32[40,8,128]{2,1,0:T(8,128)S(1)} collective-permute-done((f32[40,8,128]{2,1,0:T(8,128)S(1)}, f32[40,8,128]{2,1,0:T(8,128)S(1)}, u32[]{:S(2)}, u32[]{:S(2)}) %collective-permute-start.10) | collective-permute-done | bytes 163872 | tf_op jit(solution)/shard_map/ppermute | solution.py:32
  38.2 2.7 %collective-permute-done.11 = f32[40,8,128]{2,1,0:T(8,128)S(1)} collective-permute-done((f32[40,8,128]{2,1,0:T(8,128)S(1)}, f32[40,8,128]{2,1,0:T(8,128)S(1)}, u32[]{:S(2)}, u32[]{:S(2)}) %collective-permute-start.11) | collective-permute-done | bytes 163872 | tf_op jit(solution)/shard_map/ppermute | solution.py:32
  40.9 0.9 %collective-permute-done.12 = f32[40,8,128]{2,1,0:T(8,128)S(1)} collective-permute-done((f32[40,8,128]{2,1,0:T(8,128)S(1)}, f32[40,8,128]{2,1,0:T(8,128)S(1)}, u32[]{:S(2)}, u32[]{:S(2)}) %collective-permute-start.12) | collective-permute-done | bytes 163872 | tf_op jit(solution)/shard_map/ppermute | solution.py:32
  41.9 16.3 %all_to_all.10 = f32[8,5,8,128]{3,2,1,0:T(8,128)S(1)} all-to-all(f32[8,5,8,128]{3,2,1,0:T(8,128)S(1)} %bitcast.8), channel_id=1, replica_groups=mesh['x_hi'=2,'y'=4,'x_lo'=2,'z'=8,'core'=2] {'z'}, dimensions={0} | all-to-all | bytes 327680 | tf_op jit(solution)/shard_map/all_to_all | solution.py:264
  58.2 12.8 %all_to_all.11 = f32[16,5,8,128]{3,2,1,0:T(8,128)S(1)} all-to-all(f32[16,5,8,128]{3,2,1,0:T(8,128)S(1)} %broadcast_in_dim.2), channel_id=1, replica_groups=mesh['x_hi'=2,'y'=4,'x_lo'=2,'z'=8,'core'=2] {'z','x_lo'}, dimensions={0} | all-to-all | bytes 655360 | tf_op jit(solution)/shard_map/all_to_all | solution.py:266
  70.9 6.7 %collective-permute-start.13 = (f32[80,8,128]{2,1,0:T(8,128)S(1)}, f32[80,8,128]{2,1,0:T(8,128)S(1)}, u32[]{:S(2)}, u32[]{:S(2)}) collective-permute-start(f32[80,8,128]{2,1,0:T(8,128)S(1)} %bitcast.4), channel_id=1, source_target_pairs={{0,1},{1,0},{2,3},{3,2},{4,5},{5,4},{6,7},{7,6},{8,9},{9,8},{10,11... | collective-permute-start | bytes 983048 | tf_op jit(solution)/shard_map/ppermute | solution.py:32
  77.6 0.8 %lay_out.2.refs_0_ = f32[1,400,400]{2,1,0:T(8,128)} custom-call(f32[80,8,128]{2,1,0:T(8,128)S(1)} %bitcast.5), custom_call_target="tpu_custom_call" | custom-call | flops 80000 | bytes 700000 | tf_op jit(solution)/shard_map/lay_out/pallas_call | solution.py:231
  78.4 0.4 collective-permute-done.13.tiles
  78.8 0.8 %lay_out.3 = f32[1,400,400]{2,1,0:T(8,128)} custom-call(f32[80,8,128]{2,1,0:T(8,128)S(1)} %collective-permute-done.13.tiles, f32[1,400,400]{2,1,0:T(8,128)} %lay_out.2.refs_0_), custom_call_target="tpu_custom_call", output_to_operand_aliasing={{}: (1, {})} | custom-call | flops 80000 | bytes 700000 | tf_op jit(solution)/shard_map/lay_out/pallas_call | solution.py:231
  (12 shorter events, 0.2 us)
Async XLA Ops:
  0.0 10.9 %copy-start = (s32[1,1,8]{2,1,0:T(1,128)S(1)}, s32[1,1,8]{2,1,0:T(1,128)}, u32[]{:S(2)}) copy-start(s32[1,1,8]{2,1,0:T(1,128)} %param.3) | copy-start | bytes 100
  7.5 8.0 %collective-permute-start = (f32[4,2,40,8,128]{4,3,2,1,0:T(8,128)S(1)}, f32[4,2,40,8,128]{4,3,2,1,0:T(8,128)S(1)}, u32[]{:S(2)}, u32[]{:S(2)}) collective-permute-start(f32[4,2,40,8,128]{4,3,2,1,0:T(8,128)S(1)} %get-tuple-element.31), channel_id=1, source_target_pairs={{0,1},{1,0},{2,3},{3,2},{4,5},{5,4},{6,7},{7,6},{8,9},{9,8},{10,11... | collective-permute-start | bytes 3932168 | tf_op jit(solution)/shard_map/ppermute | solution.py:32
  15.5 3.1 %collective-permute-start.5 = (f32[4,2,40,8,128]{4,3,2,1,0:T(8,128)S(1)}, f32[4,2,40,8,128]{4,3,2,1,0:T(8,128)S(1)}, u32[]{:S(2)}, u32[]{:S(2)}) collective-permute-start(f32[4,2,40,8,128]{4,3,2,1,0:T(8,128)S(1)} %get-tuple-element.42), channel_id=1, source_target_pairs={{0,1},{1,0},{2,3},{3,2},{4,5},{5,4},{6,7},{7,6},{8,9},{9,8},{10,11... | collective-permute-start | bytes 3932168 | tf_op jit(solution)/shard_map/ppermute | solution.py:32
  15.7 6.3 %collective-permute-start.1 = (f32[2,40,8,128]{3,2,1,0:T(8,128)S(1)}, f32[2,40,8,128]{3,2,1,0:T(8,128)S(1)}, u32[]{:S(2)}, u32[]{:S(2)}) collective-permute-start(f32[2,40,8,128]{3,2,1,0:T(8,128)S(1)} %get-tuple-element.33), channel_id=1, source_target_pairs={{0,32},{1,17},{2,34},{3,19},{4,36},{5,21},{6,38},{7,23},{8,40},{9,... | collective-permute-start | bytes 983048 | tf_op jit(solution)/shard_map/ppermute | solution.py:32
  15.8 7.5 %collective-permute-start.2 = (f32[2,40,8,128]{3,2,1,0:T(8,128)S(1)}, f32[2,40,8,128]{3,2,1,0:T(8,128)S(1)}, u32[]{:S(2)}, u32[]{:S(2)}) collective-permute-start(f32[2,40,8,128]{3,2,1,0:T(8,128)S(1)} %get-tuple-element.35), channel_id=1, source_target_pairs={{0,96},{1,145},{2,98},{3,147},{4,100},{5,149},{6,102},{7,151},{8,1... | collective-permute-start | bytes 983048 | tf_op jit(solution)/shard_map/ppermute | solution.py:32
  18.7 6.8 %collective-permute-start.6 = (f32[2,40,8,128]{3,2,1,0:T(8,128)S(1)}, f32[2,40,8,128]{3,2,1,0:T(8,128)S(1)}, u32[]{:S(2)}, u32[]{:S(2)}) collective-permute-start(f32[2,40,8,128]{3,2,1,0:T(8,128)S(1)} %get-tuple-element.44), channel_id=1, source_target_pairs={{0,32},{1,17},{2,34},{3,19},{4,36},{5,21},{6,38},{7,23},{8,40},{9,... | collective-permute-start | bytes 983048 | tf_op jit(solution)/shard_map/ppermute | solution.py:32
  18.8 8.0 %collective-permute-start.7 = (f32[2,40,8,128]{3,2,1,0:T(8,128)S(1)}, f32[2,40,8,128]{3,2,1,0:T(8,128)S(1)}, u32[]{:S(2)}, u32[]{:S(2)}) collective-permute-start(f32[2,40,8,128]{3,2,1,0:T(8,128)S(1)} %get-tuple-element.46), channel_id=1, source_target_pairs={{0,96},{1,145},{2,98},{3,147},{4,100},{5,149},{6,102},{7,151},{8,1... | collective-permute-start | bytes 983048 | tf_op jit(solution)/shard_map/ppermute | solution.py:32
  23.4 5.5 %collective-permute-start.3 = (f32[40,8,128]{2,1,0:T(8,128)S(1)}, f32[40,8,128]{2,1,0:T(8,128)S(1)}, u32[]{:S(2)}, u32[]{:S(2)}) collective-permute-start(f32[40,8,128]{2,1,0:T(8,128)S(1)} %get-tuple-element.37), channel_id=1, source_target_pairs={{0,96},{1,145},{2,98},{3,147},{4,100},{5,149},{6,102},{7,151},{8,1... | collective-permute-start | bytes 491528 | tf_op jit(solution)/shard_map/ppermute | solution.py:32
  24.7 4.2 %collective-permute-start.4 = (f32[40,8,128]{2,1,0:T(8,128)S(1)}, f32[40,8,128]{2,1,0:T(8,128)S(1)}, u32[]{:S(2)}, u32[]{:S(2)}) collective-permute-start(f32[40,8,128]{2,1,0:T(8,128)S(1)} %get-tuple-element.39), channel_id=1, source_target_pairs={{0,32},{1,17},{2,34},{3,19},{4,36},{5,21},{6,38},{7,23},{8,40},{9,... | collective-permute-start | bytes 491528 | tf_op jit(solution)/shard_map/ppermute | solution.py:32
  26.9 5.5 %collective-permute-start.8 = (f32[40,8,128]{2,1,0:T(8,128)S(1)}, f32[40,8,128]{2,1,0:T(8,128)S(1)}, u32[]{:S(2)}, u32[]{:S(2)}) collective-permute-start(f32[40,8,128]{2,1,0:T(8,128)S(1)} %get-tuple-element.48), channel_id=1, source_target_pairs={{0,96},{1,145},{2,98},{3,147},{4,100},{5,149},{6,102},{7,151},{8,1... | collective-permute-start | bytes 491528 | tf_op jit(solution)/shard_map/ppermute | solution.py:32
  28.2 4.2 %collective-permute-start.9 = (f32[40,8,128]{2,1,0:T(8,128)S(1)}, f32[40,8,128]{2,1,0:T(8,128)S(1)}, u32[]{:S(2)}, u32[]{:S(2)}) collective-permute-start(f32[40,8,128]{2,1,0:T(8,128)S(1)} %get-tuple-element.50), channel_id=1, source_target_pairs={{0,32},{1,17},{2,34},{3,19},{4,36},{5,21},{6,38},{7,23},{8,40},{9,... | collective-permute-start | bytes 491528 | tf_op jit(solution)/shard_map/ppermute | solution.py:32
  32.5 5.8 %collective-permute-start.10 = (f32[40,8,128]{2,1,0:T(8,128)S(1)}, f32[40,8,128]{2,1,0:T(8,128)S(1)}, u32[]{:S(2)}, u32[]{:S(2)}) collective-permute-start(f32[40,8,128]{2,1,0:T(8,128)S(1)} %get-tuple-element.52), channel_id=1, source_target_pairs={{0,128},{1,65},{2,130},{3,67},{4,132},{5,69},{6,134},{7,71},{8,136... | collective-permute-start | bytes 491528 | tf_op jit(solution)/shard_map/ppermute | solution.py:32
  35.4 5.4 %collective-permute-start.11 = (f32[40,8,128]{2,1,0:T(8,128)S(1)}, f32[40,8,128]{2,1,0:T(8,128)S(1)}, u32[]{:S(2)}, u32[]{:S(2)}) collective-permute-start(f32[40,8,128]{2,1,0:T(8,128)S(1)} %get-tuple-element.53), channel_id=1, source_target_pairs={{0,16},{1,33},{2,18},{3,35},{4,20},{5,37},{6,22},{7,39},{8,24},{9,... | collective-permute-start | bytes 491528 | tf_op jit(solution)/shard_map/ppermute | solution.py:32
  36.1 5.7 %collective-permute-start.12 = (f32[40,8,128]{2,1,0:T(8,128)S(1)}, f32[40,8,128]{2,1,0:T(8,128)S(1)}, u32[]{:S(2)}, u32[]{:S(2)}) collective-permute-start(f32[40,8,128]{2,1,0:T(8,128)S(1)} %get-tuple-element.54), channel_id=1, source_target_pairs={{0,144},{1,97},{2,146},{3,99},{4,148},{5,101},{6,150},{7,103},{8,1... | collective-permute-start | bytes 491528 | tf_op jit(solution)/shard_map/ppermute | solution.py:32
  70.9 7.9 %collective-permute-start.13 = (f32[80,8,128]{2,1,0:T(8,128)S(1)}, f32[80,8,128]{2,1,0:T(8,128)S(1)}, u32[]{:S(2)}, u32[]{:S(2)}) collective-permute-start(f32[80,8,128]{2,1,0:T(8,128)S(1)} %bitcast.4), channel_id=1, source_target_pairs={{0,1},{1,0},{2,3},{3,2},{4,5},{5,4},{6,7},{7,6},{8,9},{9,8},{10,11... | collective-permute-start | bytes 983048 | tf_op jit(solution)/shard_map/ppermute | solution.py:32

commit v9 on v7

--- a/solution.py
+++ b/solution.py
@@ -199,22 +199,25 @@
 
 
 def layout_kernel(scale, own, tiles, *refs):
-    out, rows, sem = refs[-3:]
+    out, rows, sems = refs[-3:]
     core = lax.axis_index("core")
     half = core if own else 1 - core
-    for m in range(FULL):
-        g, l = divmod(m, WIDE)
-        rows[8 * g : 8 * g + 8, 128 * l : 128 * l + 128] = tiles[m] * scale
-    for g in range(HALF_GROUPS):
-        n, k = divmod(g, 8)
-        tile = tiles[FULL + n] * scale
-        if k:
-            tile = pltpu.roll(tile, 128 - 16 * k, 1)
-        rows[8 * g : 8 * g + 8, 128 * WIDE : 128 * WIDE + 16] = tile[:, :16]
-    count = 8 * HALF_GROUPS
-    copy = pltpu.make_async_copy(rows, out.at[0, pl.ds(pl.multiple_of(half * count, 8), count)], sem)
-    copy.start()
-    copy.wait()
+    copies = []
+    for part, groups in enumerate((range(16), range(16, HALF_GROUPS))):
+        for g in groups:
+            for l in range(WIDE):
+                rows[8 * g : 8 * g + 8, 128 * l : 128 * l + 128] = tiles[g * WIDE + l] * scale
+            n, k = divmod(g, 8)
+            tile = tiles[FULL + n] * scale
+            if k:
+                tile = pltpu.roll(tile, 128 - 16 * k, 1)
+            rows[8 * g : 8 * g + 8, 128 * WIDE : 128 * WIDE + 16] = tile[:, :16]
+        first, count = 8 * groups[0], 8 * len(groups)
+        there = pl.ds(pl.multiple_of(half * (8 * HALF_GROUPS) + first, 8), count)
+        copies.append(pltpu.make_async_copy(rows.at[first : first + count], out.at[0, there], sems.at[part]))
+        copies[-1].start()
+    for copy in copies:
+        copy.wait()
 
 
 def lay_out(scale, size, tiles, begun=None):
@@ -227,7 +230,7 @@
         out_shape=pltpu.HBM((1, size, size), jnp.float32),
         in_specs=[pl.BlockSpec(memory_space=pltpu.VMEM), in_hbm][: len(arrays)],
         out_specs=in_hbm,
-        scratch_shapes=[pltpu.VMEM((8 * HALF_GROUPS, size), jnp.float32), pltpu.SemaphoreType.DMA],
+        scratch_shapes=[pltpu.VMEM((8 * HALF_GROUPS, size), jnp.float32), pltpu.SemaphoreType.DMA((2,))],
         input_output_aliases={} if begun is None else {1: 0},
         compiler_params=pltpu.CompilerParams(vmem_limit_bytes=8 << 20),
         cost_estimate=pl.CostEstimate(flops=80000, bytes_accessed=700000, transcendentals=0),

time: 78 us -> 78 us (level)
  no operation moved by 1% of the time
where the time goes in v9:
time: 78 us; the launch traced here: 77.9 us
  blocking collectives  27 us (35%)
  starting transfers between devices  19.1 us (24%)
  waiting for transfers between devices  17.1 us (22%)
  Pallas kernels  14.3 us (18%)
    ppermute x14, starting transfers between devices, send(): return lax.ppermute(value, FINE, pairs(move))  19.1 us
    ppermute x14, waiting for transfers between devices, send(): return lax.ppermute(value, FINE, pairs(move))  17.1 us
    all_to_all x1, blocking collectives, on_device(): lax.all_to_all(third.reshape(8, UNIT // 8, 8, 128), 'z', 0, 0, tiled=True)  16.3 us
    all_to_all x1, blocking collectives, on_device(): lax.all_to_all(jnp.broadcast_to(eighth, (16, *parts.shape[1:])), ('x_lo',...  10.8 us
    pallas_call x1, Pallas kernels, densities(): pl.pallas_call(first_kernel, out_shape=(pltpu.VMEM(amps.shape, amps.dtype...  7.52 us
    pallas_call x1, Pallas kernels, densities(): pl.pallas_call(second_kernel, out_shape=(half, half), in_specs=[pl.BlockS...  4.63 us
    pallas_call x2, Pallas kernels, lay_out(): pl.pallas_call(functools.partial(layout_kernel, scale, begun is None), ou...  1.69 us
  transfers between devices with their start and end apart: 14, of which 11 were waited for; matrix products, arithmetic and copies ran while one was open for 0% of the time, Pallas kernels for 8%

profile of v9, /device:TPU:1, one launch (start us, length us, event | category | flops | bytes accessed | tf_op | source)
XLA Modules:
  0.0 77.9 jit_solution(4908188685129529140)
XLA Ops:
  0.0 7.5 %densities.2 = (bf16[8,4,400,400]{3,2,1,0:T(8,128)(2,1)S(1)}, f32[4,2,40,8,128]{4,3,2,1,0:T(8,128)S(1)}, f32[4,2,40,8,128]{4,3,2,1,0:T(8,128)S(1)}) custom-call(s32[8]{0:T(128)} %bitcast.6, bf16[8,4,400,400]{3,2,1,0:T(8,128)(2,1)} %bitcast.9), custom_call_target="tpu_custom_call" | custom-call | flops 4294967296 | bytes 13631488 | tf_op jit(solution)/shard_map/densities/pallas_call | solution.py:145
  7.5 3.3 %collective-permute-start = (f32[4,2,40,8,128]{4,3,2,1,0:T(8,128)S(1)}, f32[4,2,40,8,128]{4,3,2,1,0:T(8,128)S(1)}, u32[]{:S(2)}, u32[]{:S(2)}) collective-permute-start(f32[4,2,40,8,128]{4,3,2,1,0:T(8,128)S(1)} %get-tuple-element.31), channel_id=1, source_target_pairs={{0,1},{1,0},{2,3},{3,2},{4,5},{5,4},{6,7},{7,6},{8,9},{9,8},{10,11... | collective-permute-start | bytes 3932168 | tf_op jit(solution)/shard_map/ppermute | solution.py:32
  10.9 4.6 %densities.3 = (f32[4,2,40,8,128]{4,3,2,1,0:T(8,128)S(1)}, f32[4,2,40,8,128]{4,3,2,1,0:T(8,128)S(1)}) custom-call(s32[8]{0:T(128)S(1)} %bitcast.7, bf16[8,4,400,400]{3,2,1,0:T(8,128)(2,1)S(1)} %get-tuple-element.40.blocks), custom_call_target="tpu_custom_call" | custom-call | flops 4294967296 | bytes 13631488 | tf_op jit(solution)/shard_map/densities/pallas_call | solution.py:153
  15.5 0.1 collective-permute-start.5
  15.6 0.1 add_halves.2
  15.7 0.1 collective-permute-start.1
  15.8 1.3 %collective-permute-start.2 = (f32[2,40,8,128]{3,2,1,0:T(8,128)S(1)}, f32[2,40,8,128]{3,2,1,0:T(8,128)S(1)}, u32[]{:S(2)}, u32[]{:S(2)}) collective-permute-start(f32[2,40,8,128]{3,2,1,0:T(8,128)S(1)} %get-tuple-element.35), channel_id=1, source_target_pairs={{0,96},{1,145},{2,98},{3,147},{4,100},{5,149},{6,102},{7,151},{8,1... | collective-permute-start | bytes 983048 | tf_op jit(solution)/shard_map/ppermute | solution.py:32
  17.1 1.5 %collective-permute-done.5.got = f32[4,2,40,8,128]{4,3,2,1,0:T(8,128)S(1)} collective-permute-done((f32[4,2,40,8,128]{4,3,2,1,0:T(8,128)S(1)}, f32[4,2,40,8,128]{4,3,2,1,0:T(8,128)S(1)}, u32[]{:S(2)}, u32[]{:S(2)}) %collective-permute-start.5) | collective-permute-done | bytes 1310752 | tf_op jit(solution)/shard_map/ppermute | solution.py:32
  18.6 0.1 add_halves.3
  18.7 0.1 collective-permute-start.6
  18.8 1.3 %collective-permute-start.7 = (f32[2,40,8,128]{3,2,1,0:T(8,128)S(1)}, f32[2,40,8,128]{3,2,1,0:T(8,128)S(1)}, u32[]{:S(2)}, u32[]{:S(2)}) collective-permute-start(f32[2,40,8,128]{3,2,1,0:T(8,128)S(1)} %get-tuple-element.46), channel_id=1, source_target_pairs={{0,96},{1,145},{2,98},{3,147},{4,100},{5,149},{6,102},{7,151},{8,1... | collective-permute-start | bytes 983048 | tf_op jit(solution)/shard_map/ppermute | solution.py:32
  20.1 1.9 %collective-permute-done.1.got_a = f32[2,40,8,128]{3,2,1,0:T(8,128)S(1)} collective-permute-done((f32[2,40,8,128]{3,2,1,0:T(8,128)S(1)}, f32[2,40,8,128]{3,2,1,0:T(8,128)S(1)}, u32[]{:S(2)}, u32[]{:S(2)}) %collective-permute-start.1) | collective-permute-done | bytes 327712 | tf_op jit(solution)/shard_map/ppermute | solution.py:32
  22.0 1.3 %collective-permute-done.2.got_b = f32[2,40,8,128]{3,2,1,0:T(8,128)S(1)} collective-permute-done((f32[2,40,8,128]{3,2,1,0:T(8,128)S(1)}, f32[2,40,8,128]{3,2,1,0:T(8,128)S(1)}, u32[]{:S(2)}, u32[]{:S(2)}) %collective-permute-start.2) | collective-permute-done | bytes 327712 | tf_op jit(solution)/shard_map/ppermute | solution.py:32
  23.4 1.3 %collective-permute-start.3 = (f32[40,8,128]{2,1,0:T(8,128)S(1)}, f32[40,8,128]{2,1,0:T(8,128)S(1)}, u32[]{:S(2)}, u32[]{:S(2)}) collective-permute-start(f32[40,8,128]{2,1,0:T(8,128)S(1)} %get-tuple-element.37), channel_id=1, source_target_pairs={{0,96},{1,145},{2,98},{3,147},{4,100},{5,149},{6,102},{7,151},{8,1... | collective-permute-start | bytes 491528 | tf_op jit(solution)/shard_map/ppermute | solution.py:32
  24.7 0.9 %collective-permute-done.6.got_a = f32[2,40,8,128]{3,2,1,0:T(8,128)S(1)} collective-permute-done((f32[2,40,8,128]{3,2,1,0:T(8,128)S(1)}, f32[2,40,8,128]{3,2,1,0:T(8,128)S(1)}, u32[]{:S(2)}, u32[]{:S(2)}) %collective-permute-start.6) | collective-permute-done | bytes 327712 | tf_op jit(solution)/shard_map/ppermute | solution.py:32
  25.5 1.3 %collective-permute-done.7.got_b = f32[2,40,8,128]{3,2,1,0:T(8,128)S(1)} collective-permute-done((f32[2,40,8,128]{3,2,1,0:T(8,128)S(1)}, f32[2,40,8,128]{3,2,1,0:T(8,128)S(1)}, u32[]{:S(2)}, u32[]{:S(2)}) %collective-permute-start.7) | collective-permute-done | bytes 327712 | tf_op jit(solution)/shard_map/ppermute | solution.py:32
  26.9 1.3 %collective-permute-start.8 = (f32[40,8,128]{2,1,0:T(8,128)S(1)}, f32[40,8,128]{2,1,0:T(8,128)S(1)}, u32[]{:S(2)}, u32[]{:S(2)}) collective-permute-start(f32[40,8,128]{2,1,0:T(8,128)S(1)} %get-tuple-element.48), channel_id=1, source_target_pairs={{0,96},{1,145},{2,98},{3,147},{4,100},{5,149},{6,102},{7,151},{8,1... | collective-permute-start | bytes 491528 | tf_op jit(solution)/shard_map/ppermute | solution.py:32
  28.2 0.7 collective-permute-done.3.refs_1_
  28.9 3.5 %collective-permute-done.8.refs_5_ = f32[40,8,128]{2,1,0:T(8,128)S(1)} collective-permute-done((f32[40,8,128]{2,1,0:T(8,128)S(1)}, f32[40,8,128]{2,1,0:T(8,128)S(1)}, u32[]{:S(2)}, u32[]{:S(2)}) %collective-permute-start.8) | collective-permute-done | bytes 163872 | tf_op jit(solution)/shard_map/ppermute | solution.py:32
  32.4 0.1 add_ring.1
  32.5 3.0 %collective-permute-start.10 = (f32[40,8,128]{2,1,0:T(8,128)S(1)}, f32[40,8,128]{2,1,0:T(8,128)S(1)}, u32[]{:S(2)}, u32[]{:S(2)}) collective-permute-start(f32[40,8,128]{2,1,0:T(8,128)S(1)} %get-tuple-element.52), channel_id=1, source_target_pairs={{0,128},{1,65},{2,130},{3,67},{4,132},{5,69},{6,134},{7,71},{8,136... | collective-permute-start | bytes 491528 | tf_op jit(solution)/shard_map/ppermute | solution.py:32
  35.4 0.7 collective-permute-start.11
  36.1 0.1 collective-permute-start.12
  36.2 2.0 %collective-permute-done.10 = f32[40,8,128]{2,1,0:T(8,128)S(1)} collective-permute-done((f32[40,8,128]{2,1,0:T(8,128)S(1)}, f32[40,8,128]{2,1,0:T(8,128)S(1)}, u32[]{:S(2)}, u32[]{:S(2)}) %collective-permute-start.10) | collective-permute-done | bytes 163872 | tf_op jit(solution)/shard_map/ppermute | solution.py:32
  38.2 2.7 %collective-permute-done.11 = f32[40,8,128]{2,1,0:T(8,128)S(1)} collective-permute-done((f32[40,8,128]{2,1,0:T(8,128)S(1)}, f32[40,8,128]{2,1,0:T(8,128)S(1)}, u32[]{:S(2)}, u32[]{:S(2)}) %collective-permute-start.11) | collective-permute-done | bytes 163872 | tf_op jit(solution)/shard_map/ppermute | solution.py:32
  40.9 0.9 %collective-permute-done.12 = f32[40,8,128]{2,1,0:T(8,128)S(1)} collective-permute-done((f32[40,8,128]{2,1,0:T(8,128)S(1)}, f32[40,8,128]{2,1,0:T(8,128)S(1)}, u32[]{:S(2)}, u32[]{:S(2)}) %collective-permute-start.12) | collective-permute-done | bytes 163872 | tf_op jit(solution)/shard_map/ppermute | solution.py:32
  41.9 16.3 %all_to_all.10 = f32[8,5,8,128]{3,2,1,0:T(8,128)S(1)} all-to-all(f32[8,5,8,128]{3,2,1,0:T(8,128)S(1)} %bitcast.8), channel_id=1, replica_groups=mesh['x_hi'=2,'y'=4,'x_lo'=2,'z'=8,'core'=2] {'z'}, dimensions={0} | all-to-all | bytes 327680 | tf_op jit(solution)/shard_map/all_to_all | solution.py:261
  58.2 10.8 %all_to_all.11 = f32[16,5,8,128]{3,2,1,0:T(8,128)S(1)} all-to-all(f32[16,5,8,128]{3,2,1,0:T(8,128)S(1)} %broadcast_in_dim.2), channel_id=1, replica_groups=mesh['x_hi'=2,'y'=4,'x_lo'=2,'z'=8,'core'=2] {'x_lo','z'}, dimensions={0} | all-to-all | bytes 655360 | tf_op jit(solution)/shard_map/all_to_all | solution.py:263
  68.9 6.7 %collective-permute-start.13 = (f32[80,8,128]{2,1,0:T(8,128)S(1)}, f32[80,8,128]{2,1,0:T(8,128)S(1)}, u32[]{:S(2)}, u32[]{:S(2)}) collective-permute-start(f32[80,8,128]{2,1,0:T(8,128)S(1)} %bitcast.4), channel_id=1, source_target_pairs={{0,1},{1,0},{2,3},{3,2},{4,5},{5,4},{6,7},{7,6},{8,9},{9,8},{10,11... | collective-permute-start | bytes 983048 | tf_op jit(solution)/shard_map/ppermute | solution.py:32
  75.6 0.8 %lay_out.2.refs_0_ = f32[1,400,400]{2,1,0:T(8,128)} custom-call(f32[80,8,128]{2,1,0:T(8,128)S(1)} %bitcast.5), custom_call_target="tpu_custom_call" | custom-call | flops 80000 | bytes 700000 | tf_op jit(solution)/shard_map/lay_out/pallas_call | solution.py:228
  76.5 0.4 collective-permute-done.13.tiles
  76.9 0.8 %lay_out.3 = f32[1,400,400]{2,1,0:T(8,128)} custom-call(f32[80,8,128]{2,1,0:T(8,128)S(1)} %collective-permute-done.13.tiles, f32[1,400,400]{2,1,0:T(8,128)} %lay_out.2.refs_0_), custom_call_target="tpu_custom_call", output_to_operand_aliasing={{}: (1, {})} | custom-call | flops 80000 | bytes 700000 | tf_op jit(solution)/shard_map/lay_out/pallas_call | solution.py:228
  (12 shorter events, 0.2 us)
Async XLA Ops:
  0.0 10.9 %copy-start = (s32[1,1,8]{2,1,0:T(1,128)S(1)}, s32[1,1,8]{2,1,0:T(1,128)}, u32[]{:S(2)}) copy-start(s32[1,1,8]{2,1,0:T(1,128)} %param.3) | copy-start | bytes 100
  7.5 8.0 %collective-permute-start = (f32[4,2,40,8,128]{4,3,2,1,0:T(8,128)S(1)}, f32[4,2,40,8,128]{4,3,2,1,0:T(8,128)S(1)}, u32[]{:S(2)}, u32[]{:S(2)}) collective-permute-start(f32[4,2,40,8,128]{4,3,2,1,0:T(8,128)S(1)} %get-tuple-element.31), channel_id=1, source_target_pairs={{0,1},{1,0},{2,3},{3,2},{4,5},{5,4},{6,7},{7,6},{8,9},{9,8},{10,11... | collective-permute-start | bytes 3932168 | tf_op jit(solution)/shard_map/ppermute | solution.py:32
  15.5 3.1 %collective-permute-start.5 = (f32[4,2,40,8,128]{4,3,2,1,0:T(8,128)S(1)}, f32[4,2,40,8,128]{4,3,2,1,0:T(8,128)S(1)}, u32[]{:S(2)}, u32[]{:S(2)}) collective-permute-start(f32[4,2,40,8,128]{4,3,2,1,0:T(8,128)S(1)} %get-tuple-element.42), channel_id=1, source_target_pairs={{0,1},{1,0},{2,3},{3,2},{4,5},{5,4},{6,7},{7,6},{8,9},{9,8},{10,11... | collective-permute-start | bytes 3932168 | tf_op jit(solution)/shard_map/ppermute | solution.py:32
  15.7 6.3 %collective-permute-start.1 = (f32[2,40,8,128]{3,2,1,0:T(8,128)S(1)}, f32[2,40,8,128]{3,2,1,0:T(8,128)S(1)}, u32[]{:S(2)}, u32[]{:S(2)}) collective-permute-start(f32[2,40,8,128]{3,2,1,0:T(8,128)S(1)} %get-tuple-element.33), channel_id=1, source_target_pairs={{0,32},{1,17},{2,34},{3,19},{4,36},{5,21},{6,38},{7,23},{8,40},{9,... | collective-permute-start | bytes 983048 | tf_op jit(solution)/shard_map/ppermute | solution.py:32
  15.8 7.5 %collective-permute-start.2 = (f32[2,40,8,128]{3,2,1,0:T(8,128)S(1)}, f32[2,40,8,128]{3,2,1,0:T(8,128)S(1)}, u32[]{:S(2)}, u32[]{:S(2)}) collective-permute-start(f32[2,40,8,128]{3,2,1,0:T(8,128)S(1)} %get-tuple-element.35), channel_id=1, source_target_pairs={{0,96},{1,145},{2,98},{3,147},{4,100},{5,149},{6,102},{7,151},{8,1... | collective-permute-start | bytes 983048 | tf_op jit(solution)/shard_map/ppermute | solution.py:32
  18.7 6.8 %collective-permute-start.6 = (f32[2,40,8,128]{3,2,1,0:T(8,128)S(1)}, f32[2,40,8,128]{3,2,1,0:T(8,128)S(1)}, u32[]{:S(2)}, u32[]{:S(2)}) collective-permute-start(f32[2,40,8,128]{3,2,1,0:T(8,128)S(1)} %get-tuple-element.44), channel_id=1, source_target_pairs={{0,32},{1,17},{2,34},{3,19},{4,36},{5,21},{6,38},{7,23},{8,40},{9,... | collective-permute-start | bytes 983048 | tf_op jit(solution)/shard_map/ppermute | solution.py:32
  18.8 8.0 %collective-permute-start.7 = (f32[2,40,8,128]{3,2,1,0:T(8,128)S(1)}, f32[2,40,8,128]{3,2,1,0:T(8,128)S(1)}, u32[]{:S(2)}, u32[]{:S(2)}) collective-permute-start(f32[2,40,8,128]{3,2,1,0:T(8,128)S(1)} %get-tuple-element.46), channel_id=1, source_target_pairs={{0,96},{1,145},{2,98},{3,147},{4,100},{5,149},{6,102},{7,151},{8,1... | collective-permute-start | bytes 983048 | tf_op jit(solution)/shard_map/ppermute | solution.py:32
  23.4 5.5 %collective-permute-start.3 = (f32[40,8,128]{2,1,0:T(8,128)S(1)}, f32[40,8,128]{2,1,0:T(8,128)S(1)}, u32[]{:S(2)}, u32[]{:S(2)}) collective-permute-start(f32[40,8,128]{2,1,0:T(8,128)S(1)} %get-tuple-element.37), channel_id=1, source_target_pairs={{0,96},{1,145},{2,98},{3,147},{4,100},{5,149},{6,102},{7,151},{8,1... | collective-permute-start | bytes 491528 | tf_op jit(solution)/shard_map/ppermute | solution.py:32
  24.7 4.2 %collective-permute-start.4 = (f32[40,8,128]{2,1,0:T(8,128)S(1)}, f32[40,8,128]{2,1,0:T(8,128)S(1)}, u32[]{:S(2)}, u32[]{:S(2)}) collective-permute-start(f32[40,8,128]{2,1,0:T(8,128)S(1)} %get-tuple-element.39), channel_id=1, source_target_pairs={{0,32},{1,17},{2,34},{3,19},{4,36},{5,21},{6,38},{7,23},{8,40},{9,... | collective-permute-start | bytes 491528 | tf_op jit(solution)/shard_map/ppermute | solution.py:32
  26.9 5.5 %collective-permute-start.8 = (f32[40,8,128]{2,1,0:T(8,128)S(1)}, f32[40,8,128]{2,1,0:T(8,128)S(1)}, u32[]{:S(2)}, u32[]{:S(2)}) collective-permute-start(f32[40,8,128]{2,1,0:T(8,128)S(1)} %get-tuple-element.48), channel_id=1, source_target_pairs={{0,96},{1,145},{2,98},{3,147},{4,100},{5,149},{6,102},{7,151},{8,1... | collective-permute-start | bytes 491528 | tf_op jit(solution)/shard_map/ppermute | solution.py:32
  28.2 4.2 %collective-permute-start.9 = (f32[40,8,128]{2,1,0:T(8,128)S(1)}, f32[40,8,128]{2,1,0:T(8,128)S(1)}, u32[]{:S(2)}, u32[]{:S(2)}) collective-permute-start(f32[40,8,128]{2,1,0:T(8,128)S(1)} %get-tuple-element.50), channel_id=1, source_target_pairs={{0,32},{1,17},{2,34},{3,19},{4,36},{5,21},{6,38},{7,23},{8,40},{9,... | collective-permute-start | bytes 491528 | tf_op jit(solution)/shard_map/ppermute | solution.py:32
  32.5 5.8 %collective-permute-start.10 = (f32[40,8,128]{2,1,0:T(8,128)S(1)}, f32[40,8,128]{2,1,0:T(8,128)S(1)}, u32[]{:S(2)}, u32[]{:S(2)}) collective-permute-start(f32[40,8,128]{2,1,0:T(8,128)S(1)} %get-tuple-element.52), channel_id=1, source_target_pairs={{0,128},{1,65},{2,130},{3,67},{4,132},{5,69},{6,134},{7,71},{8,136... | collective-permute-start | bytes 491528 | tf_op jit(solution)/shard_map/ppermute | solution.py:32
  35.4 5.4 %collective-permute-start.11 = (f32[40,8,128]{2,1,0:T(8,128)S(1)}, f32[40,8,128]{2,1,0:T(8,128)S(1)}, u32[]{:S(2)}, u32[]{:S(2)}) collective-permute-start(f32[40,8,128]{2,1,0:T(8,128)S(1)} %get-tuple-element.53), channel_id=1, source_target_pairs={{0,16},{1,33},{2,18},{3,35},{4,20},{5,37},{6,22},{7,39},{8,24},{9,... | collective-permute-start | bytes 491528 | tf_op jit(solution)/shard_map/ppermute | solution.py:32
  36.1 5.7 %collective-permute-start.12 = (f32[40,8,128]{2,1,0:T(8,128)S(1)}, f32[40,8,128]{2,1,0:T(8,128)S(1)}, u32[]{:S(2)}, u32[]{:S(2)}) collective-permute-start(f32[40,8,128]{2,1,0:T(8,128)S(1)} %get-tuple-element.54), channel_id=1, source_target_pairs={{0,144},{1,97},{2,146},{3,99},{4,148},{5,101},{6,150},{7,103},{8,1... | collective-permute-start | bytes 491528 | tf_op jit(solution)/shard_map/ppermute | solution.py:32
  68.9 7.9 %collective-permute-start.13 = (f32[80,8,128]{2,1,0:T(8,128)S(1)}, f32[80,8,128]{2,1,0:T(8,128)S(1)}, u32[]{:S(2)}, u32[]{:S(2)}) collective-permute-start(f32[80,8,128]{2,1,0:T(8,128)S(1)} %bitcast.4), channel_id=1, source_target_pairs={{0,1},{1,0},{2,3},{3,2},{4,5},{5,4},{6,7},{7,6},{8,9},{9,8},{10,11... | collective-permute-start | bytes 983048 | tf_op jit(solution)/shard_map/ppermute | solution.py:32
